TPU v7x, 256 devices: a whole 4x4x8 slice. The times are simulated.
256 devices in a mesh: row: 32 (over y, z_lo, core), col: 8 (over z_hi, x).
Axes of the slice: x: 4, y: 4, z: 8 (z_hi: 2, z_lo: 4; z = z_hi * 4 + z_lo), core: 2. Of those that a mesh axis runs over, the one named last changes fastest.
Arguments:
- views: bfloat16 [81, 2048, 2048], P(None, 'row', 'col'), may hold values from -6 to 6
Outputs:
- increment: float32 [2048, 2048], P('row', 'col')
- residual: float32 [2048, 2048], P('row', 'col')
All inputs are finite; a program needn't handle non-finite values.
Results may differ from a plain program's by a relative error of at most 0.0005.
Values may be sent and summed in bfloat16 or wider, within the bound.
No kernel may reach another device: no remote copies, remote signals or barrier semaphores. Data moves between devices by JAX's collectives and lax.ppermute only.
A program may use at most 64 MiB of HBM per device.

v0:
```python
import jax
import jax.numpy as jnp
from jax import lax
from jax.sharding import Mesh
from jax.sharding import PartitionSpec as P

ANG = 9
VIEWS = 81
D0 = 3
HALO = 13
ITERS = 2
ROW_COL = ("row_0", "row_1", "row_2", "col_0", "col_1")
ROW = ("row_0", "row_1", "row_2")
COL = ("col_0", "col_1")


smooth_weight = 2.0
damping = 0.1


def with_halo(array, sides, width):
    for axis, dim in sides:
        count, length = (lax.axis_size(axis), array.shape[dim])
        up = [(i, (i + 1) % count) for i in range(count - 1)]
        down = [(j, i) for i, j in up]
        last = lax.slice_in_dim(array, length - width, length, axis=dim)
        leading = lax.slice_in_dim(array, 0, width, axis=dim)
        before = lax.ppermute(last, axis, up)
        after = lax.ppermute(leading, axis, down)
        array = jnp.concatenate([before, array, after], axis=dim)
    return array


def by_axis(array, axes):
    for axis in axes:
        array = lax.psum(array, axis)
    return array


def operate(field, coeff, horiz, verti):
    padded = with_halo(field, ((ROW, 0), (COL, 1)), 1)
    edges = horiz[:, 1:] * (field - padded[1:-1, 2:]) + horiz[:, :-1] * (field - padded[1:-1, :-2])
    edges = (
        edges + verti[1:] * (field - padded[2:, 1:-1]) + verti[:-1] * (field - padded[:-2, 1:-1])
    )
    return coeff * field + smooth_weight * edges


def row_band(col_ext, srow_index, rows_dev):
    srow = srow_index - ANG // 2
    reach = D0 * abs(srow) + 1
    block = col_ext[srow_index * ANG : (srow_index + 1) * ANG]
    grown = with_halo(block, ((ROW, 1),), reach)
    start = reach + D0 * srow - 1
    return grown[:, start : start + rows_dev + 2, :]


def shards(views):
    rows_dev = views.shape[1]
    cols_dev = views.shape[2]
    total_rows = rows_dev * lax.axis_size(ROW)
    total_cols = cols_dev * lax.axis_size(COL)
    bands = []
    col_ext = with_halo(views, ((COL, 2),), HALO)
    for srow_index in range(ANG):
        bands.append(row_band(col_ext, srow_index, rows_dev))
    center_ext = bands[ANG // 2][ANG // 2, :, HALO - 1 : HALO + cols_dev + 1].astype(jnp.float32)
    center = center_ext[1:-1, 1:-1]
    data_sum = jnp.zeros((rows_dev, cols_dev), jnp.float32)
    source_sum = jnp.zeros((rows_dev, cols_dev), jnp.float32)
    for srow_index in range(ANG):
        srow = float(srow_index - ANG // 2)
        band = bands[srow_index]
        for tindex in range(ANG):
            tcol = tindex - ANG // 2
            left = HALO + D0 * tcol
            image = band[tindex].astype(jnp.float32)
            warped = image[1:-1, left : left + cols_dev]
            down_diff = 0.5 * (
                image[2:, left : left + cols_dev] - image[:-2, left : left + cols_dev]
            )
            side_diff = 0.5 * (
                image[1:-1, left + 1 : left + 1 + cols_dev]
                - image[1:-1, left - 1 : left - 1 + cols_dev]
            )
            slope = srow * down_diff + tcol * side_diff
            error = warped - center
            robust = 1.0 / jnp.sqrt(1.0 + error * error)
            data_sum = data_sum + robust * slope * slope
            source_sum = source_sum - robust * slope * error
    coeff = damping + data_sum / VIEWS
    source = source_sum / VIEWS
    across = center_ext[1:-1, 1:] - center_ext[1:-1, :-1]
    vertical = center_ext[1:, 1:-1] - center_ext[:-1, 1:-1]
    columns = lax.axis_index(COL) * cols_dev + jnp.arange(cols_dev + 1)
    row_index = lax.axis_index(ROW) * rows_dev + jnp.arange(rows_dev + 1)
    horiz = jnp.where(
        ((columns >= 1) & (columns <= total_cols - 1))[None, :], jnp.exp(-across * across), 0.0
    )
    verti = jnp.where(
        ((row_index >= 1) & (row_index <= total_rows - 1))[:, None],
        jnp.exp(-vertical * vertical),
        0.0,
    )
    precond = coeff + smooth_weight * (horiz[:, 1:] + horiz[:, :-1] + verti[1:] + verti[:-1])
    solution = jnp.zeros_like(source)
    residual = source
    scaled_res = residual / precond
    image_res = operate(scaled_res, coeff, horiz, verti)
    inner_old = None
    step_old = None
    for step in range(ITERS):
        inner_rz, inner_wu = (
            by_axis(jnp.sum(residual * scaled_res), ROW_COL),
            by_axis(jnp.sum(image_res * scaled_res), ROW_COL),
        )
        scaled_img = image_res / precond
        last_step = step + 1 == ITERS
        if not last_step:
            next_image = operate(scaled_img, coeff, horiz, verti)
        if step == 0:
            step_size = inner_rz / inner_wu
            direction = scaled_res
            dir_image = image_res
            dir_scaled = scaled_img
            dir_second = next_image
        else:
            momentum = inner_rz / inner_old
            step_size = inner_rz / (inner_wu - momentum * inner_rz / step_old)
            direction = scaled_res + momentum * direction
            dir_image = image_res + momentum * dir_image
        solution = solution + step_size * direction
        residual = residual - step_size * dir_image
        if not last_step:
            scaled_res = scaled_res - step_size * dir_scaled
            image_res = image_res - step_size * dir_second
        inner_old = inner_rz
        step_old = step_size
    return (solution, residual)


def solution(mesh):
    finer = Mesh(mesh.devices.reshape(4, 4, 2, 2, 4), ("row_0", "row_1", "row_2", "col_0", "col_1"))
    in_specs = (P(None, ROW, COL),)
    out_specs = (P(ROW, COL), P(ROW, COL))
    return jax.shard_map(
        shards, mesh=finer, in_specs=in_specs, out_specs=out_specs, check_vma=False
    )
```

profile of v0, /device:TPU:1, one launch (start us, length us, event | category | flops | bytes accessed | tf_op | source)
XLA Modules:
  0.0 253.4 jit_solution(15290785969575630049)
XLA Ops:
  0.6 3.4 %fusion.427 = (bf16[81,64,13]{2,1,0:T(8,128)(2,1)}, bf16[81,64,13]{2,1,0:T(8,128)(2,1)S(1)}) fusion(bf16[81,64,256]{2,1,0:T(8,128)(2,1)} %param.1), kind=kLoop, calls=%fused_computation.861 | loop fusion | bytes 539136 | tf_op jit(solution)/shard_map/slice | solution.py:26
  4.0 1.7 copy.8
  5.8 1.6 collective-permute-start.1
  7.4 2.9 %copy.7 = bf16[81,64,13]{0,1,2:T(8,128)(2,1)S(1)} copy(bf16[81,64,13]{2,1,0:T(8,128)(2,1)} %get-tuple-element.132) | data formatting | bytes 269568
  10.2 4.6 %collective-permute-start = (bf16[81,64,13]{0,1,2:T(8,128)(2,1)S(1)}, bf16[81,64,13]{0,1,2:T(8,128)(2,1)S(1)}, u32[]{:S(2)}, u32[]{:S(2)}) collective-permute-start(bf16[81,64,13]{0,1,2:T(8,128)(2,1)S(1)} %copy.7), channel_id=1, source_target_pairs={{0,1},{1,2},{2,3},{3,4},{4,5},{5,6},{6,7},{8,9},{9,10},{10,11},{11... | collective-permute-start | bytes 404360 | tf_op jit(solution)/shard_map/ppermute | solution.py:28
  14.9 2.7 %collective-permute-done = bf16[81,64,13]{0,1,2:T(8,128)(2,1)S(1)} collective-permute-done((bf16[81,64,13]{0,1,2:T(8,128)(2,1)S(1)}, bf16[81,64,13]{0,1,2:T(8,128)(2,1)S(1)}, u32[]{:S(2)}, u32[]{:S(2)}) %collective-permute-start) | collective-permute-done | bytes 134816 | tf_op jit(solution)/shard_map/ppermute | solution.py:28
  17.6 3.2 %copy.5 = bf16[81,64,13]{2,1,0:T(8,128)(2,1)} copy(bf16[81,64,13]{0,1,2:T(8,128)(2,1)S(1)} %collective-permute-done) | data formatting | bytes 269568 | tf_op jit(solution)/shard_map/ppermute | solution.py:28
  20.8 3.2 %copy.6 = bf16[81,64,13]{2,1,0:T(8,128)(2,1)} copy(bf16[81,64,13]{0,1,2:T(8,128)(2,1)S(1)} %collective-permute-done.1) | data formatting | bytes 269568 | tf_op jit(solution)/shard_map/ppermute | solution.py:29
  24.0 1.0 pad_maximum_fusion.37
  25.0 0.3 copy-done.1
  25.4 0.4 copy-done.2
  25.8 0.1 pad_maximum_fusion.34
  25.9 0.1 pad_maximum_fusion.27
  26.0 0.2 pad_maximum_fusion.3
  26.2 2.8 %pad_maximum_fusion = bf16[81,64,282]{2,1,0:T(8,128)(2,1)S(1)} fusion(bf16[81,64,13]{2,1,0:T(8,128)(2,1)S(1)} %copy-done.2, bf16[81,64,256]{2,1,0:T(8,128)(2,1)S(1)} %copy-done, bf16[81,64,13]{2,1,0:T(8,128)(2,1)S(1)} %copy-done.1), kind=kLoop, calls=%fused_computation | loop fusion | flops 8771328 | bytes 5847552 | tf_op jit(solution)/shard_map/concatenate | solution.py:30
  29.0 6.3 %collective-permute-start.3 = (bf16[9,1,282]{2,1,0:T(2,128)(2,1)S(1)}, bf16[9,1,282]{2,1,0:T(2,128)(2,1)S(1)}, u32[]{:S(2)}, u32[]{:S(2)}) collective-permute-start(bf16[9,1,282]{2,1,0:T(2,128)(2,1)S(1)} %get-tuple-element.121), channel_id=1, source_target_pairs={{0,8},{8,16},{16,24},{24,32},{32,40},{40,48},{48,56},{56,64},{64,7... | collective-permute-start | bytes 15236 | tf_op jit(solution)/shard_map/ppermute | solution.py:28
  35.3 1.9 collective-permute-start.4
  37.3 1.9 collective-permute-start.8
  39.2 3.6 %collective-permute-start.7 = (bf16[9,4,282]{2,1,0:T(4,128)(2,1)S(1)}, bf16[9,4,282]{2,1,0:T(4,128)(2,1)S(1)}, u32[]{:S(2)}, u32[]{:S(2)}) collective-permute-start(bf16[9,4,282]{2,1,0:T(4,128)(2,1)S(1)} %get-tuple-element.120), channel_id=1, source_target_pairs={{0,8},{8,16},{16,24},{24,32},{32,40},{40,48},{48,56},{56,64},{64,7... | collective-permute-start | bytes 60920 | tf_op jit(solution)/shard_map/ppermute | solution.py:28
  42.9 1.9 collective-permute-start.9
  44.8 0.6 fusion.426
  45.4 0.2 pad_maximum_fusion.2
  45.6 3.6 %collective-permute-start.6 = (bf16[9,7,282]{2,1,0:T(8,128)(2,1)S(1)}, bf16[9,7,282]{2,1,0:T(8,128)(2,1)S(1)}, u32[]{:S(2)}, u32[]{:S(2)}) collective-permute-start(bf16[9,7,282]{2,1,0:T(8,128)(2,1)S(1)} %get-tuple-element.118), channel_id=1, source_target_pairs={{0,8},{8,16},{16,24},{24,32},{32,40},{40,48},{48,56},{56,64},{64,7... | collective-permute-start | bytes 106604 | tf_op jit(solution)/shard_map/ppermute | solution.py:28
  49.2 1.9 collective-permute-start.10
  51.2 0.2 pad_maximum_fusion.1
  51.3 0.1 fusion.337
  51.5 0.1 fusion.1
  51.6 0.1 fusion.3
  51.8 3.6 %collective-permute-start.5 = (bf16[9,10,282]{2,1,0:T(8,128)(2,1)S(1)}, bf16[9,10,282]{2,1,0:T(8,128)(2,1)S(1)}, u32[]{:S(2)}, u32[]{:S(2)}) collective-permute-start(bf16[9,10,282]{2,1,0:T(8,128)(2,1)S(1)} %get-tuple-element.116), channel_id=1, source_target_pairs={{0,8},{8,16},{16,24},{24,32},{32,40},{40,48},{48,56},{56,64},{64,7... | collective-permute-start | bytes 152288 | tf_op jit(solution)/shard_map/ppermute | solution.py:28
  55.4 0.1 fusion.304
  55.6 1.9 collective-permute-start.11
  57.5 0.1 fusion.315
  57.6 3.8 %collective-permute-start.2 = (bf16[9,13,282]{2,1,0:T(8,128)(2,1)S(1)}, bf16[9,13,282]{2,1,0:T(8,128)(2,1)S(1)}, u32[]{:S(2)}, u32[]{:S(2)}) collective-permute-start(bf16[9,13,282]{2,1,0:T(8,128)(2,1)S(1)} %get-tuple-element.114), channel_id=1, source_target_pairs={{0,8},{8,16},{16,24},{24,32},{32,40},{40,48},{48,56},{56,64},{64,7... | collective-permute-start | bytes 197972 | tf_op jit(solution)/shard_map/ppermute | solution.py:28
  61.5 0.9 fusion.317
  62.4 1.0 fusion.302
  63.4 1.0 fusion.319
  64.4 1.0 fusion.292
  65.4 1.0 fusion.282
  66.3 1.0 fusion.329
  67.4 27.1 %subtract_multiply_fusion = (f32[64,256]{1,0:T(8,128)}, f32[64,256]{1,0:T(8,128)}, f32[64,256]{1,0:T(8,128)}, f32[64,256]{1,0:T(8,128)}, f32[64,256]{1,0:T(8,128...) fusion(f32[66,282]{1,0:T(8,128)} %get-tuple-element.169, ...), kind=kLoop, calls=%fused_computation.594 | loop fusion | flops 14188544 | bytes 31981568 | tf_op jit(solution)/shard_map/div | solution.py:92
  94.5 7.2 %fusion.344 = (f32[64,256]{1,0:T(8,128)S(1)}, f32[64,256]{1,0:T(8,128)S(1)}, f32[64,256]{1,0:T(8,128)S(1)}) fusion(f32[64,256]{1,0:T(8,128)} %get-tuple-element.31, f32[65,256]{1,0:T(8,128)S(1)} %fusion.3, f32[64,257]{1,0:T(8,128)S(1)} %fusion.1, f32[64,256]{1,0:T(8,128)} %get-tuple-element.112, f32[66,282]{1,0:T(8,128)} %get-tuple-element.134, ...), kind=kLoop, calls=%fused_computation.859 | loop fusion | flops 8077312 | bytes 11206656 | tf_op jit(solution)/shard_map/div | solution.py:108
  101.8 1.9 collective-permute-start.13
  103.7 3.6 %collective-permute-start.12 = (f32[1,256]{1,0:T(1,128)S(1)}, f32[1,256]{1,0:T(1,128)S(1)}, u32[]{:S(2)}, u32[]{:S(2)}) collective-permute-start(f32[1,256]{1,0:T(1,128)S(1)} %get-tuple-element.222), channel_id=1, source_target_pairs={{0,8},{8,16},{16,24},{24,32},{32,40},{40,48},{48,56},{56,64},{64,7... | collective-permute-start | bytes 3080 | tf_op jit(solution)/shard_map/ppermute | solution.py:28
  107.3 0.7 collective-permute-done.12
  108.1 1.3 collective-permute-start.14
  109.4 4.7 %collective-permute-start.15 = (f32[66,1]{1,0:T(8,128)S(1)}, f32[66,1]{1,0:T(8,128)S(1)}, u32[]{:S(2)}, u32[]{:S(2)}) collective-permute-start(f32[66,1]{1,0:T(8,128)S(1)} %get-tuple-element.218), channel_id=1, source_target_pairs={{0,1},{1,2},{2,3},{3,4},{4,5},{5,6},{6,7},{8,9},{9,10},{10,11},{11... | collective-permute-start | bytes 800 | tf_op jit(solution)/shard_map/ppermute | solution.py:28
  114.2 1.0 collective-permute-done.15
  115.2 0.8 multiply_reduce_fusion.2
  116.0 1.9 collective-permute-start.17
  117.9 5.0 %collective-permute-start.16 = (f32[1,256]{1,0:T(1,128)S(1)}, f32[1,256]{1,0:T(1,128)S(1)}, u32[]{:S(2)}, u32[]{:S(2)}) collective-permute-start(f32[1,256]{1,0:T(1,128)S(1)} %get-tuple-element.220), channel_id=1, source_target_pairs={{0,8},{8,16},{16,24},{24,32},{32,40},{40,48},{48,56},{56,64},{64,7... | collective-permute-start | bytes 3080 | tf_op jit(solution)/shard_map/ppermute | solution.py:28
  123.0 24.7 %all-reduce.5 = (f32[]{:T(128)}, f32[]{:T(128)}) all-reduce(f32[]{:T(128)} %get-tuple-element.5, f32[]{:T(128)} %get-tuple-element.4), channel_id=1, replica_groups=mesh['row_0'=4,'row_1'=4,'row_2'=2,'col_0'=2,'col_1'=4] {'row_0'}, use_global_device_ids=true, to_apply=%region_1.2 | all-reduce | flops 2 | bytes 16 | tf_op jit(solution)/shard_map/psum | solution.py:36
  147.7 9.4 %all-reduce.3 = (f32[]{:T(128)}, f32[]{:T(128)}) all-reduce(f32[]{:T(128)} %get-tuple-element.16, f32[]{:T(128)} %get-tuple-element.17), channel_id=1, replica_groups=mesh['row_0'=4,'row_1'=4,'row_2'=2,'col_0'=2,'col_1'=4] {'row_1'}, use_global_device_ids=true, to_apply=%region_2.3 | all-reduce | flops 2 | bytes 16 | tf_op jit(solution)/shard_map/psum | solution.py:36
  157.1 4.6 %all-reduce.9 = (f32[]{:T(128)}, f32[]{:T(128)}) all-reduce(f32[]{:T(128)} %get-tuple-element.12, f32[]{:T(128)} %get-tuple-element.13), channel_id=1, replica_groups=mesh['row_0'=4,'row_1'=4,'row_2'=2,'col_0'=2,'col_1'=4] {'row_2'}, use_global_device_ids=true, to_apply=%region_3.4 | all-reduce | flops 2 | bytes 16 | tf_op jit(solution)/shard_map/psum | solution.py:36
  161.8 23.2 %all-reduce.7 = (f32[]{:T(128)}, f32[]{:T(128)}) all-reduce(f32[]{:T(128)} %get-tuple-element.24, f32[]{:T(128)} %get-tuple-element.25), channel_id=1, replica_groups=mesh['row_0'=4,'row_1'=4,'row_2'=2,'col_0'=2,'col_1'=4] {'col_0'}, use_global_device_ids=true, to_apply=%region_4.5 | all-reduce | flops 2 | bytes 16 | tf_op jit(solution)/shard_map/psum | solution.py:36
  185.1 1.3 collective-permute-start.18
  186.4 4.0 %collective-permute-start.19 = (f32[66,1]{1,0:T(8,128)S(1)}, f32[66,1]{1,0:T(8,128)S(1)}, u32[]{:S(2)}, u32[]{:S(2)}) collective-permute-start(f32[66,1]{1,0:T(8,128)S(1)} %get-tuple-element.216), channel_id=1, source_target_pairs={{0,1},{1,2},{2,3},{3,4},{4,5},{5,6},{6,7},{8,9},{9,10},{10,11},{11... | collective-permute-start | bytes 800 | tf_op jit(solution)/shard_map/ppermute | solution.py:28
  190.4 12.9 %all-reduce.1 = (f32[]{:T(128)}, f32[]{:T(128)}) all-reduce(f32[]{:T(128)} %get-tuple-element.20, f32[]{:T(128)} %get-tuple-element.21), channel_id=1, replica_groups=mesh['row_0'=4,'row_1'=4,'row_2'=2,'col_0'=2,'col_1'=4] {'col_1'}, use_global_device_ids=true, to_apply=%region_5.6 | all-reduce | flops 2 | bytes 16 | tf_op jit(solution)/shard_map/psum | solution.py:36
  204.7 1.7 multiply_reduce_fusion
  206.4 6.6 %all-reduce.4 = (f32[]{:T(128)}, f32[]{:T(128)}) all-reduce(f32[]{:T(128)} %get-tuple-element.3, f32[]{:T(128)} %get-tuple-element.2), channel_id=1, replica_groups=mesh['row_0'=4,'row_1'=4,'row_2'=2,'col_0'=2,'col_1'=4] {'row_0'}, use_global_device_ids=true, to_apply=%region_13.14 | all-reduce | flops 2 | bytes 16 | tf_op jit(solution)/shard_map/psum | solution.py:36
  213.0 9.0 %all-reduce.2 = (f32[]{:T(128)}, f32[]{:T(128)}) all-reduce(f32[]{:T(128)} %get-tuple-element.14, f32[]{:T(128)} %get-tuple-element.15), channel_id=1, replica_groups=mesh['row_0'=4,'row_1'=4,'row_2'=2,'col_0'=2,'col_1'=4] {'row_1'}, use_global_device_ids=true, to_apply=%region_14.15 | all-reduce | flops 2 | bytes 16 | tf_op jit(solution)/shard_map/psum | solution.py:36
  222.0 10.3 %all-reduce.8 = (f32[]{:T(128)}, f32[]{:T(128)}) all-reduce(f32[]{:T(128)} %get-tuple-element.10, f32[]{:T(128)} %get-tuple-element.11), channel_id=1, replica_groups=mesh['row_0'=4,'row_1'=4,'row_2'=2,'col_0'=2,'col_1'=4] {'row_2'}, use_global_device_ids=true, to_apply=%region_15.16 | all-reduce | flops 2 | bytes 16 | tf_op jit(solution)/shard_map/psum | solution.py:36
  232.3 8.3 %all-reduce.6 = (f32[]{:T(128)}, f32[]{:T(128)}) all-reduce(f32[]{:T(128)} %get-tuple-element.22, f32[]{:T(128)} %get-tuple-element.23), channel_id=1, replica_groups=mesh['row_0'=4,'row_1'=4,'row_2'=2,'col_0'=2,'col_1'=4] {'col_0'}, use_global_device_ids=true, to_apply=%region_16.17 | all-reduce | flops 2 | bytes 16 | tf_op jit(solution)/shard_map/psum | solution.py:36
  240.6 6.6 %all-reduce = (f32[]{:T(128)}, f32[]{:T(128)}) all-reduce(f32[]{:T(128)} %get-tuple-element.18, f32[]{:T(128)} %get-tuple-element.19), channel_id=1, replica_groups=mesh['row_0'=4,'row_1'=4,'row_2'=2,'col_0'=2,'col_1'=4] {'col_1'}, use_global_device_ids=true, to_apply=%region_17.18 | all-reduce | flops 2 | bytes 16 | tf_op jit(solution)/shard_map/psum | solution.py:36
  251.9 1.5 multiply_subtract_fusion
  (35 shorter events, 0.4 us)
Async XLA Ops:
  5.8 18.2 %copy-start = (bf16[81,64,256]{2,1,0:T(8,128)(2,1)S(1)}, bf16[81,64,256]{2,1,0:T(8,128)(2,1)}, u32[]{:S(2)}) copy-start(bf16[81,64,256]{2,1,0:T(8,128)(2,1)} %param.1) | copy-start | bytes 7962628
  5.8 15.0 %collective-permute-start.1 = (bf16[81,64,13]{0,1,2:T(8,128)(2,1)S(1)}, bf16[81,64,13]{0,1,2:T(8,128)(2,1)S(1)}, u32[]{:S(2)}, u32[]{:S(2)}) collective-permute-start(bf16[81,64,13]{0,1,2:T(8,128)(2,1)S(1)} %copy.8), channel_id=1, source_target_pairs={{1,0},{2,1},{3,2},{4,3},{5,4},{6,5},{7,6},{9,8},{10,9},{11,10},{12... | collective-permute-start | bytes 404360 | tf_op jit(solution)/shard_map/ppermute | solution.py:29
  10.2 7.4 %collective-permute-start = (bf16[81,64,13]{0,1,2:T(8,128)(2,1)S(1)}, bf16[81,64,13]{0,1,2:T(8,128)(2,1)S(1)}, u32[]{:S(2)}, u32[]{:S(2)}) collective-permute-start(bf16[81,64,13]{0,1,2:T(8,128)(2,1)S(1)} %copy.7), channel_id=1, source_target_pairs={{0,1},{1,2},{2,3},{3,4},{4,5},{5,6},{6,7},{8,9},{9,10},{10,11},{11... | collective-permute-start | bytes 404360 | tf_op jit(solution)/shard_map/ppermute | solution.py:28
  24.0 1.4 copy-start.1
  24.0 1.8 copy-start.2
  29.0 16.6 %collective-permute-start.3 = (bf16[9,1,282]{2,1,0:T(2,128)(2,1)S(1)}, bf16[9,1,282]{2,1,0:T(2,128)(2,1)S(1)}, u32[]{:S(2)}, u32[]{:S(2)}) collective-permute-start(bf16[9,1,282]{2,1,0:T(2,128)(2,1)S(1)} %get-tuple-element.121), channel_id=1, source_target_pairs={{0,8},{8,16},{16,24},{24,32},{32,40},{40,48},{48,56},{56,64},{64,7... | collective-permute-start | bytes 15236 | tf_op jit(solution)/shard_map/ppermute | solution.py:28
  35.3 13.9 %collective-permute-start.4 = (bf16[9,1,282]{2,1,0:T(2,128)(2,1)S(1)}, bf16[9,1,282]{2,1,0:T(2,128)(2,1)S(1)}, u32[]{:S(2)}, u32[]{:S(2)}) collective-permute-start(bf16[9,1,282]{2,1,0:T(2,128)(2,1)S(1)} %get-tuple-element.122), channel_id=1, source_target_pairs={{8,0},{16,8},{24,16},{32,24},{40,32},{48,40},{56,48},{64,56},{72,6... | collective-permute-start | bytes 15236 | tf_op jit(solution)/shard_map/ppermute | solution.py:29
  37.3 14.5 %collective-permute-start.8 = (bf16[9,4,282]{2,1,0:T(4,128)(2,1)S(1)}, bf16[9,4,282]{2,1,0:T(4,128)(2,1)S(1)}, u32[]{:S(2)}, u32[]{:S(2)}) collective-permute-start(bf16[9,4,282]{2,1,0:T(4,128)(2,1)S(1)} %get-tuple-element.119), channel_id=1, source_target_pairs={{8,0},{16,8},{24,16},{32,24},{40,32},{48,40},{56,48},{64,56},{72,6... | collective-permute-start | bytes 60920 | tf_op jit(solution)/shard_map/ppermute | solution.py:29
  39.2 16.3 %collective-permute-start.7 = (bf16[9,4,282]{2,1,0:T(4,128)(2,1)S(1)}, bf16[9,4,282]{2,1,0:T(4,128)(2,1)S(1)}, u32[]{:S(2)}, u32[]{:S(2)}) collective-permute-start(bf16[9,4,282]{2,1,0:T(4,128)(2,1)S(1)} %get-tuple-element.120), channel_id=1, source_target_pairs={{0,8},{8,16},{16,24},{24,32},{32,40},{40,48},{48,56},{56,64},{64,7... | collective-permute-start | bytes 60920 | tf_op jit(solution)/shard_map/ppermute | solution.py:28
  42.9 19.5 %collective-permute-start.9 = (bf16[9,7,282]{2,1,0:T(8,128)(2,1)S(1)}, bf16[9,7,282]{2,1,0:T(8,128)(2,1)S(1)}, u32[]{:S(2)}, u32[]{:S(2)}) collective-permute-start(bf16[9,7,282]{2,1,0:T(8,128)(2,1)S(1)} %get-tuple-element.117), channel_id=1, source_target_pairs={{8,0},{16,8},{24,16},{32,24},{40,32},{48,40},{56,48},{64,56},{72,6... | collective-permute-start | bytes 106604 | tf_op jit(solution)/shard_map/ppermute | solution.py:29
  45.6 12.0 %collective-permute-start.6 = (bf16[9,7,282]{2,1,0:T(8,128)(2,1)S(1)}, bf16[9,7,282]{2,1,0:T(8,128)(2,1)S(1)}, u32[]{:S(2)}, u32[]{:S(2)}) collective-permute-start(bf16[9,7,282]{2,1,0:T(8,128)(2,1)S(1)} %get-tuple-element.118), channel_id=1, source_target_pairs={{0,8},{8,16},{16,24},{24,32},{32,40},{40,48},{48,56},{56,64},{64,7... | collective-permute-start | bytes 106604 | tf_op jit(solution)/shard_map/ppermute | solution.py:28
  49.2 15.1 %collective-permute-start.10 = (bf16[9,10,282]{2,1,0:T(8,128)(2,1)S(1)}, bf16[9,10,282]{2,1,0:T(8,128)(2,1)S(1)}, u32[]{:S(2)}, u32[]{:S(2)}) collective-permute-start(bf16[9,10,282]{2,1,0:T(8,128)(2,1)S(1)} %get-tuple-element.115), channel_id=1, source_target_pairs={{8,0},{16,8},{24,16},{32,24},{40,32},{48,40},{56,48},{64,56},{72,6... | collective-permute-start | bytes 152288 | tf_op jit(solution)/shard_map/ppermute | solution.py:29
  51.8 11.6 %collective-permute-start.5 = (bf16[9,10,282]{2,1,0:T(8,128)(2,1)S(1)}, bf16[9,10,282]{2,1,0:T(8,128)(2,1)S(1)}, u32[]{:S(2)}, u32[]{:S(2)}) collective-permute-start(bf16[9,10,282]{2,1,0:T(8,128)(2,1)S(1)} %get-tuple-element.116), channel_id=1, source_target_pairs={{0,8},{8,16},{16,24},{24,32},{32,40},{40,48},{48,56},{56,64},{64,7... | collective-permute-start | bytes 152288 | tf_op jit(solution)/shard_map/ppermute | solution.py:28
  55.6 9.8 %collective-permute-start.11 = (bf16[9,13,282]{2,1,0:T(8,128)(2,1)S(1)}, bf16[9,13,282]{2,1,0:T(8,128)(2,1)S(1)}, u32[]{:S(2)}, u32[]{:S(2)}) collective-permute-start(bf16[9,13,282]{2,1,0:T(8,128)(2,1)S(1)} %get-tuple-element.113), channel_id=1, source_target_pairs={{8,0},{16,8},{24,16},{32,24},{40,32},{48,40},{56,48},{64,56},{72,6... | collective-permute-start | bytes 197972 | tf_op jit(solution)/shard_map/ppermute | solution.py:29
  57.6 8.7 %collective-permute-start.2 = (bf16[9,13,282]{2,1,0:T(8,128)(2,1)S(1)}, bf16[9,13,282]{2,1,0:T(8,128)(2,1)S(1)}, u32[]{:S(2)}, u32[]{:S(2)}) collective-permute-start(bf16[9,13,282]{2,1,0:T(8,128)(2,1)S(1)} %get-tuple-element.114), channel_id=1, source_target_pairs={{0,8},{8,16},{16,24},{24,32},{32,40},{40,48},{48,56},{56,64},{64,7... | collective-permute-start | bytes 197972 | tf_op jit(solution)/shard_map/ppermute | solution.py:28
  94.5 20.7 %copy-start.3 = (f32[64,256]{1,0:T(8,128)S(1)}, f32[64,256]{1,0:T(8,128)}, u32[]{:S(2)}) copy-start(f32[64,256]{1,0:T(8,128)} %get-tuple-element.31) | copy-start | bytes 196612
  101.7 14.2 %copy-start.4 = (f32[64,256]{1,0:T(8,128)}, f32[64,256]{1,0:T(8,128)S(1)}, u32[]{:S(2)}) copy-start(f32[64,256]{1,0:T(8,128)S(1)} %get-tuple-element.30) | copy-start | bytes 196612
  101.8 5.6 %collective-permute-start.13 = (f32[1,256]{1,0:T(1,128)S(1)}, f32[1,256]{1,0:T(1,128)S(1)}, u32[]{:S(2)}, u32[]{:S(2)}) collective-permute-start(f32[1,256]{1,0:T(1,128)S(1)} %get-tuple-element.221), channel_id=1, source_target_pairs={{8,0},{16,8},{24,16},{32,24},{40,32},{48,40},{56,48},{64,56},{72,6... | collective-permute-start | bytes 3080 | tf_op jit(solution)/shard_map/ppermute | solution.py:29
  103.7 4.4 %collective-permute-start.12 = (f32[1,256]{1,0:T(1,128)S(1)}, f32[1,256]{1,0:T(1,128)S(1)}, u32[]{:S(2)}, u32[]{:S(2)}) collective-permute-start(f32[1,256]{1,0:T(1,128)S(1)} %get-tuple-element.222), channel_id=1, source_target_pairs={{0,8},{8,16},{16,24},{24,32},{32,40},{40,48},{48,56},{56,64},{64,7... | collective-permute-start | bytes 3080 | tf_op jit(solution)/shard_map/ppermute | solution.py:28
  108.1 6.0 %collective-permute-start.14 = (f32[66,1]{1,0:T(8,128)S(1)}, f32[66,1]{1,0:T(8,128)S(1)}, u32[]{:S(2)}, u32[]{:S(2)}) collective-permute-start(f32[66,1]{1,0:T(8,128)S(1)} %get-tuple-element.217), channel_id=1, source_target_pairs={{1,0},{2,1},{3,2},{4,3},{5,4},{6,5},{7,6},{9,8},{10,9},{11,10},{12... | collective-permute-start | bytes 800 | tf_op jit(solution)/shard_map/ppermute | solution.py:29
  109.4 5.8 %collective-permute-start.15 = (f32[66,1]{1,0:T(8,128)S(1)}, f32[66,1]{1,0:T(8,128)S(1)}, u32[]{:S(2)}, u32[]{:S(2)}) collective-permute-start(f32[66,1]{1,0:T(8,128)S(1)} %get-tuple-element.218), channel_id=1, source_target_pairs={{0,1},{1,2},{2,3},{3,4},{4,5},{5,6},{6,7},{8,9},{9,10},{10,11},{11... | collective-permute-start | bytes 800 | tf_op jit(solution)/shard_map/ppermute | solution.py:28
  116.0 69.0 %collective-permute-start.17 = (f32[1,256]{1,0:T(1,128)S(1)}, f32[1,256]{1,0:T(1,128)S(1)}, u32[]{:S(2)}, u32[]{:S(2)}) collective-permute-start(f32[1,256]{1,0:T(1,128)S(1)} %get-tuple-element.219), channel_id=1, source_target_pairs={{8,0},{16,8},{24,16},{32,24},{40,32},{48,40},{56,48},{64,56},{72,6... | collective-permute-start | bytes 3080 | tf_op jit(solution)/shard_map/ppermute | solution.py:29
  117.9 67.0 %collective-permute-start.16 = (f32[1,256]{1,0:T(1,128)S(1)}, f32[1,256]{1,0:T(1,128)S(1)}, u32[]{:S(2)}, u32[]{:S(2)}) collective-permute-start(f32[1,256]{1,0:T(1,128)S(1)} %get-tuple-element.220), channel_id=1, source_target_pairs={{0,8},{8,16},{16,24},{24,32},{32,40},{40,48},{48,56},{56,64},{64,7... | collective-permute-start | bytes 3080 | tf_op jit(solution)/shard_map/ppermute | solution.py:28
  185.1 19.6 %collective-permute-start.18 = (f32[66,1]{1,0:T(8,128)S(1)}, f32[66,1]{1,0:T(8,128)S(1)}, u32[]{:S(2)}, u32[]{:S(2)}) collective-permute-start(f32[66,1]{1,0:T(8,128)S(1)} %get-tuple-element.215), channel_id=1, source_target_pairs={{1,0},{2,1},{3,2},{4,3},{5,4},{6,5},{7,6},{9,8},{10,9},{11,10},{12... | collective-permute-start | bytes 800 | tf_op jit(solution)/shard_map/ppermute | solution.py:29
  186.4 18.4 %collective-permute-start.19 = (f32[66,1]{1,0:T(8,128)S(1)}, f32[66,1]{1,0:T(8,128)S(1)}, u32[]{:S(2)}, u32[]{:S(2)}) collective-permute-start(f32[66,1]{1,0:T(8,128)S(1)} %get-tuple-element.216), channel_id=1, source_target_pairs={{0,1},{1,2},{2,3},{3,4},{4,5},{5,6},{6,7},{8,9},{9,10},{10,11},{11... | collective-permute-start | bytes 800 | tf_op jit(solution)/shard_map/ppermute | solution.py:28
where the time goes:
time: 257 us; the launch traced here: 253 us
  blocking collectives  116 us (45%)
  starting transfers between devices  60.7 us (24%)
  other arithmetic  49.4 us (19%)
  local copies, waits for them, and re-layouts  16 us (6%)
  between operations  7.14 us (3%)
  waiting for transfers between devices  4.49 us (2%)
    psum x10, blocking collectives, by_axis(): array = lax.psum(array, axis)  116 us
    ppermute x10, starting transfers between devices, with_halo(): before = lax.ppermute(last, axis, up)  43.1 us
    div x1, other arithmetic, shards(): source = source_sum / VIEWS  27.1 us
    ppermute x10, starting transfers between devices, with_halo(): after = lax.ppermute(leading, axis, down)  17.6 us
    div x1, other arithmetic, shards(): scaled_res = residual / precond  7.21 us
    convert_element_type x9, other arithmetic, shards(): image = band[tindex].astype(jnp.float32)  6.21 us
    unnamed x12, local copies, waits for them, and re-layouts  5.38 us
  transfers between devices with their start and end apart: 20, of which 3 were waited for; matrix products, arithmetic and copies ran while one was open for 5% of the time, Pallas kernels for 0%

commit v1 on v0

v1 whole, which is shorter than its diff:
```python
import functools

import jax
import jax.numpy as jnp
import ml_dtypes
import numpy as np
from jax import lax
from jax.experimental import pallas as pl
from jax.experimental.pallas import tpu as pltpu
from jax.sharding import PartitionSpec as P

ANG = 9
VIEWS = 81
HALF = ANG // 2
D0 = 3
ROWS = 64
COLS = 256
EDGE = 16
OUT = 72
SLAB = 96
PACKED = ANG * ROWS + 10 * EDGE
LANES = 128
SMOOTH = 2.0
DAMPING = 0.1
ALL = ("row", "col")
F32 = jnp.float32


def lane_first(t, c):
    return D0 * t * (t + 1) // 2 + c


def lane_last(t, c):
    a = abs(t)
    return 64 + D0 * a * (a + 1) // 2 + c - (COLS - D0 * a - D0)


def ghost_source(t, c):
    if c < 0:
        return lane_last(t, COLS + c)
    if c >= COLS:
        return 2 * LANES + lane_first(t, c - COLS)
    if t >= 0 and c <= D0 * t + D0 - 1:
        return LANES + lane_first(t, c)
    return LANES + lane_last(t, c)


def tables():
    pack = np.zeros((ANG, COLS, LANES), np.float32)
    for t in range(-HALF, HALF + 1):
        if t >= 0:
            for c in range(D0 * t + D0):
                pack[t + HALF, c, lane_first(t, c)] = 1
        if t <= 0:
            for c in range(COLS - D0 * abs(t) - D0, COLS):
                pack[t + HALF, c, lane_last(t, c)] = 1
    inner = np.zeros((2, HALF, COLS, 2 * LANES), np.float32)
    outer = np.zeros((2, HALF, COLS, 2 * LANES), np.float32)
    for a in range(1, HALF + 1):
        for sign in (0, 1):
            t = a if sign else -a
            for j in range(LANES):
                for shift, out, value in ((0, 0, 1), (1, LANES, t), (-1, LANES, -t)):
                    c = j + D0 * t + shift
                    inner[sign, a - 1, c if sign else c + LANES, j + out] += value
                    if sign:
                        k = c if c < LANES else LANES + lane_first(t, c - LANES)
                    else:
                        k = LANES + c if c >= 0 else lane_last(t, COLS + c)
                    outer[sign, a - 1, k, j + out] += value
    ghost = np.zeros((3 * LANES, 2 * LANES), np.float32)
    center = np.zeros((3 * LANES, 2 * LANES), np.float32)
    for t in range(-HALF, HALF + 1):
        for g, col in enumerate((-2, -1, COLS, COLS + 1)):
            lane = (4 * (t + HALF) + g - 2) % LANES
            c = col + D0 * t
            ghost[ghost_source(t, c), lane] += 1
            if t:
                ghost[ghost_source(t, c + 1), LANES + lane] += t
                ghost[ghost_source(t, c - 1), LANES + lane] -= t
            center[ghost_source(0, col), lane] = 1
    for col in (-3, -2, -1, COLS, COLS + 1, COLS + 2):
        center[ghost_source(0, col), LANES + (col % (3 * LANES)) % LANES] = 1
    return tuple(x.astype(ml_dtypes.bfloat16) for x in (pack, inner, outer, ghost, center))


def dot(a, b):
    return jnp.dot(a, b, preferred_element_type=F32)


def pack_own(views, pack, out):
    for si in range(ANG):
        total = dot(views[si * ANG], pack[0])
        for ti in range(1, ANG):
            total = total + dot(views[si * ANG + ti], pack[ti])
        out[si * ROWS : (si + 1) * ROWS, :] = total.astype(jnp.bfloat16)


def pack_edges(above, below, pack, own, out):
    out[: ANG * ROWS, :] = own[...]
    for side, ref in enumerate((above, below)):
        for i in range(HALF + 1):
            total = dot(ref[i * ANG], pack[0])
            for ti in range(1, ANG):
                total = total + dot(ref[i * ANG + ti], pack[ti])
            at = ANG * ROWS + side * 5 * EDGE + i * EDGE
            out[at : at + EDGE, :] = total.astype(jnp.bfloat16)


def pieces(s):
    if s > 0:
        return (("own", 0), ("below", ROWS))
    if s < 0:
        return (("above", 0), ("own", EDGE))
    return (("above", 0), ("own", EDGE), ("below", EDGE + ROWS))


def first_row(s):
    return D0 * s - 2 if s > 0 else EDGE - 2 + D0 * s


def packed_rows(kind, s):
    if kind == "own":
        return (s + HALF) * ROWS, ROWS
    if kind == "above":
        return ANG * ROWS + (s + HALF) * EDGE, EDGE
    return ANG * ROWS + 5 * EDGE + s * EDGE, EDGE


def view_rows(kind, s, ti, views, above, below):
    if kind == "own":
        return views.at[(s + HALF) * ANG + ti]
    if kind == "above":
        return above.at[(s + HALF) * ANG + ti]
    return below.at[s * ANG + ti]


def accumulate(s, warped, side, center, data, source):
    at = first_row(s)
    value = warped[pl.ds(at, OUT), :]
    slope = float(s) * (warped[pl.ds(at + 1, OUT), :] - warped[pl.ds(at - 1, OUT), :])
    if side is not None:
        side_part = side[pl.ds(at, OUT), :]
        slope = slope + side_part if s else side_part
    error = value - center
    robust = lax.rsqrt(1.0 + error * error)
    weighted = robust * slope
    return data + weighted * slope, source + weighted * error


def fill(slab, at, array):
    slab[pl.ds(at, array.shape[0]), :] = array


def zero_tails(slabs):
    for i in range(ANG):
        slabs[i, pl.ds(SLAB - EDGE, EDGE), :] = jnp.zeros((EDGE, LANES), F32)


def shifted_views(ti, matrix, lhs, center, warped, side, data, source):
    for s in range(-HALF, HALF + 1):
        w, d = warped.at[s + HALF], side.at[s + HALF]
        for kind, at in pieces(s):
            both = dot(lhs(kind, s, ti), matrix)
            fill(w, at, both[:, :LANES])
            fill(d, at, both[:, LANES:])
        data, source = accumulate(s, w, d, center, data, source)
    return data, source


def inner_sums(views, above, below, inner, data_out, source_out, warped, side, center_ref):
    zero_tails(warped)
    zero_tails(side)
    zero = jnp.zeros((OUT, LANES), F32)
    for tile in (0, 1):
        lanes = slice(tile * LANES, (tile + 1) * LANES)
        for s in (0, -4, -3, -2, -1, 1, 2, 3, 4):
            for kind, at in pieces(s):
                ref = view_rows(kind, s, HALF, views, above, below)
                fill(warped.at[s + HALF], at, ref[:, lanes].astype(F32))
            if s == 0:
                center_ref[...] = warped[HALF, pl.ds(first_row(0), OUT), :]
                data = source = zero
            data, source = accumulate(
                s, warped.at[s + HALF], None, center_ref[...], data, source
            )
        data_out[tile] = data
        source_out[tile] = source
        sign = 1 - tile

        def body(a, carry, tile=tile, sign=sign):
            ti = HALF + 1 + a if sign else HALF - 1 - a
            data, source = shifted_views(
                ti,
                inner[sign, a],
                lambda kind, s, ti: view_rows(kind, s, ti, views, above, below)[...],
                center_ref[...],
                warped,
                side,
                zero,
                zero,
            )
            data_out[tile] += data
            source_out[tile] += source
            return carry

        lax.fori_loop(0, HALF, body, 0)


def outer_sums(
    total_rows,
    total_cols,
    views,
    above,
    below,
    own,
    left,
    right,
    data_in,
    source_in,
    outer,
    ghost,
    ghost_center,
    zed_out,
    near_out,
    next_out,
    precond_out,
    message,
    data_acc,
    source_acc,
    warped,
    side,
    center_ref,
    center_slab,
):
    zero_tails(warped)
    zero_tails(side)
    zero = jnp.zeros((OUT, LANES), F32)
    for kind, at in pieces(0):
        ref = view_rows(kind, 0, HALF, views, above, below)
        fill(center_slab.at[0], at, ref[:, :LANES].astype(F32))
        fill(center_slab.at[1], at, ref[:, LANES:].astype(F32))
        row, count = packed_rows(kind, 0)
        lhs = jnp.concatenate([x[pl.ds(row, count), :] for x in (left, own, right)], axis=1)
        both = dot(lhs, ghost_center[...])
        fill(warped.at[HALF], at, both[:, :LANES])
        fill(center_slab.at[2], at, both[:, LANES:])
    for tile in (0, 1):
        data_acc[tile] = data_in[tile]
        source_acc[tile] = source_in[tile]
    center_ref[...] = warped[HALF, pl.ds(first_row(0), OUT), :]
    data = source = zero
    for s in range(-HALF, HALF + 1):
        w, d = warped.at[s + HALF], side.at[s + HALF]
        for kind, at in pieces(s):
            row, count = packed_rows(kind, s)
            lhs = jnp.concatenate([x[pl.ds(row, count), :] for x in (left, own, right)], axis=1)
            both = dot(lhs, ghost[...])
            fill(w, at, both[:, :LANES])
            fill(d, at, both[:, LANES:])
        data, source = accumulate(s, w, d, center_ref[...], data, source)
    for step in (4, 8, 16, 32):
        data = data + pltpu.roll(data, LANES - step, 1)
        source = source + pltpu.roll(source, LANES - step, 1)
    data_acc[2] = data
    source_acc[2] = source
    for tile in (0, 1):
        sign = tile
        center_ref[...] = center_slab[tile, pl.ds(first_row(0), OUT), :]

        def lhs_of(kind, s, ti, sign=sign):
            ref = view_rows(kind, s, ti, views, above, below)
            row, count = packed_rows(kind, s)
            if sign:
                return jnp.concatenate([ref[:, LANES:], right[pl.ds(row, count), :]], axis=1)
            return jnp.concatenate([left[pl.ds(row, count), :], ref[:, :LANES]], axis=1)

        def body(a, carry, tile=tile, sign=sign, lhs_of=lhs_of):
            ti = HALF + 1 + a if sign else HALF - 1 - a
            data, source = shifted_views(
                ti, outer[sign, a], lhs_of, center_ref[...], warped, side, zero, zero
            )
            data_acc[tile] += data
            source_acc[tile] += source
            return carry

        lax.fori_loop(0, HALF, body, 0)

    def joined(ref):
        return jnp.concatenate([ref[0], ref[1], ref[2]], axis=1)

    wide = 3 * LANES

    def before(x):
        return pltpu.roll(x, 1, 1)

    def after(x):
        return pltpu.roll(x, wide - 1, 1)

    def over(x):
        return pltpu.roll(x, 1, 0)

    def under(x):
        return pltpu.roll(x, OUT - 1, 0)

    at = first_row(0)
    here = jnp.concatenate([center_slab[i, pl.ds(at, OUT), :] for i in range(3)], axis=1)
    higher = jnp.concatenate([center_slab[i, pl.ds(at - 1, OUT), :] for i in range(3)], axis=1)
    lane = lax.broadcasted_iota(jnp.int32, (OUT, wide), 1)
    local_row = lax.broadcasted_iota(jnp.int32, (OUT, wide), 0) - 2
    column = jnp.where(lane < wide - 64, lane, lane - wide) + lax.axis_index("col") * COLS
    row = local_row + lax.axis_index("row") * ROWS
    across = here - before(here)
    vertical = here - higher
    h_left = jnp.where((column >= 1) & (column <= total_cols - 1), jnp.exp(-across * across), 0.0)
    v_up = jnp.where((row >= 1) & (row <= total_rows - 1), jnp.exp(-vertical * vertical), 0.0)
    h_right = after(h_left)
    v_down = under(v_up)
    coeff = DAMPING + joined(data_acc) * (0.25 / VIEWS)
    source = joined(source_acc) * (-0.5 / VIEWS)
    precond = coeff + SMOOTH * (h_left + h_right + v_up + v_down)
    inverse = 1.0 / precond

    def neighbours(x):
        total = h_left * before(x) + h_right * after(x) + v_up * over(x) + v_down * under(x)
        return SMOOTH * inverse * total

    zed = source * inverse
    near = neighbours(zed)
    nxt = neighbours(near)

    def block(x):
        return x[:, :COLS]

    zed, near, nxt, precond = block(zed), block(near), block(nxt), block(precond)
    zed_out[...] = zed
    near_out[...] = near
    next_out[...] = nxt
    precond_out[...] = precond
    mine = (block(local_row) >= 0) & (block(local_row) < ROWS)

    def inner(x, y):
        return jnp.sum(jnp.where(mine, precond * x * y, 0.0), keepdims=True)

    zz = inner(zed, zed)
    zn = inner(zed, near)
    kappa = jnp.clip(zn / jnp.where(zz > 0, zz, 1.0), -1.0, 1.0)
    y = near - kappa * zed
    g = nxt - kappa * near
    numbers = (
        (0, inner(y, y)),
        (1, inner(y, g)),
        (32, 2.0 * inner(y, zed)),
        (33, inner(y, near) + inner(zed, g)),
        (64, zz),
        (65, zn),
        (96, kappa),
        (97, kappa),
    )
    place = lax.broadcasted_iota(jnp.int32, (1, LANES), 1)
    out = jnp.zeros((1, LANES), F32)
    for where, number in numbers:
        out = jnp.where(place == where, number, out)
    message[...] = out


def finish(messages, zed_ref, near_ref, next_ref, precond_ref, increment, residual):
    all_of = messages[...]
    total = jnp.sum(all_of, axis=0, keepdims=True)
    zz = total[:, 64:65]
    zn = total[:, 65:66]
    kappa = zn / zz
    delta = pltpu.roll(all_of, 32, 1) - kappa
    linear = pltpu.roll(all_of, 96, 1)
    quad = pltpu.roll(all_of, 64, 1)
    moved = jnp.sum(all_of + delta * (linear + delta * quad), axis=0, keepdims=True)
    yy = moved[:, 0:1]
    yny = moved[:, 1:2]
    step0 = zz / (zz - zn)
    beta = step0 * step0 * yy / zz
    step1 = yy / (yy - yny - step0 * yy * yy / zz)
    rows = pl.ds(2, ROWS)
    zed = zed_ref[rows, :]
    near = near_ref[rows, :]
    nxt = next_ref[rows, :]
    y = near - kappa * zed
    g = nxt - kappa * near
    increment[...] = step0 * zed + step1 * (step0 * y + beta * zed)
    residual[...] = precond_ref[rows, :] * (
        step0 * y - step1 * (step0 * (y - g) + beta * (zed - near))
    )


def call(kernel, outs, scratch=(), name=None):
    return pl.pallas_call(
        kernel,
        out_shape=outs,
        scratch_shapes=list(scratch),
        compiler_params=pltpu.CompilerParams(vmem_limit_bytes=24 * 1024 * 1024),
        name=name,
    )


def shards(views):
    rows, cols = lax.axis_size("row"), lax.axis_size("col")
    pack, inner, outer, ghost, center = (jnp.asarray(x) for x in tables())
    bf16 = jnp.bfloat16
    struct = jax.ShapeDtypeStruct

    def towards(array, axis, step):
        n = lax.axis_size(axis)
        pairs = [(i, i + step) for i in range(n) if 0 <= i + step < n]
        return lax.ppermute(array, axis, pairs)

    below = towards(views[HALF * ANG :, :EDGE, :], "row", -1)
    above = towards(views[: (HALF + 1) * ANG, ROWS - EDGE :, :], "row", 1)
    own = call(pack_own, struct((ANG * ROWS, LANES), bf16), name="pack_own")(views, pack)
    own = call(pack_edges, struct((PACKED, LANES), bf16), name="pack_edges")(
        above, below, pack, own
    )
    left = towards(own, "col", 1)
    right = towards(own, "col", -1)
    slab = pltpu.VMEM((ANG, SLAB, LANES), F32)
    tile = pltpu.VMEM((OUT, LANES), F32)
    sums = struct((2, OUT, LANES), F32)
    data, source = call(inner_sums, (sums, sums), (slab, slab, tile), name="inner_sums")(
        views, above, below, inner
    )
    field = struct((OUT, COLS), F32)
    acc = pltpu.VMEM((3, OUT, LANES), F32)
    zed, near, nxt, precond, message = call(
        functools.partial(outer_sums, rows * ROWS, cols * COLS),
        (field, field, field, field, struct((1, LANES), F32)),
        (acc, acc, slab, slab, tile, pltpu.VMEM((3, SLAB, LANES), F32)),
        name="outer_sums",
    )(views, above, below, own, left, right, data, source, outer, ghost, center)
    n = rows * cols
    messages = lax.all_to_all(
        jnp.broadcast_to(message[None], (n, 1, LANES)), ALL, 0, 0, tiled=True
    ).reshape(n, LANES)
    block = struct((ROWS, COLS), F32)
    return call(finish, (block, block), name="finish")(messages, zed, near, nxt, precond)


def solution(mesh):
    return jax.shard_map(
        shards,
        mesh=mesh,
        in_specs=(P(None, "row", "col"),),
        out_specs=(P("row", "col"), P("row", "col")),
        check_vma=False,
    )
```

time: 257 us -> 72.2 us (0.28); the launches traced: 253 us -> 71.9 us
  blocking collectives: 116 us -> 40.1 us
  other arithmetic: 49.4 us -> 0 us
  starting transfers between devices: 60.7 us -> 12.4 us
  Pallas kernels: 0 us -> 14 us
  local copies, waits for them, and re-layouts: 16 us -> 4.16 us
  between operations: 7.14 us -> 0.81 us
  waiting for transfers between devices: 4.49 us -> 0.53 us
    psum x10 -> x0, blocking collectives: 116 us -> none  [by_axis(): array = lax.psum(array, axis)]
    ppermute x20 -> x4, starting transfers between devices: 60.7 us -> 12.4 us  [towards(): return lax.ppermute(array, axis, pairs)]
    all_to_all x0 -> x1, blocking collectives: none -> 40.1 us  [shards(): lax.all_to_all(jnp.broadcast_to(message[None], (n, 1, LANES)), ALL, 0, 0,...]
    div x3 -> x0, other arithmetic: 34.4 us -> none  [the longest x1 27.1 us: shards(): source = source_sum / VIEWS]
    pallas_call x0 -> x5, Pallas kernels: none -> 14 us  [the longest x1 6.14 us: shards(): call(functools.partial(outer_sums, rows * ROWS, cols * COLS), (field, fie...]
    ppermute x2 -> x0, local copies, waits for them, and re-layouts: 6.41 us -> none  [the longest x1 3.22 us: with_halo(): after = lax.ppermute(leading, axis, down)]
    convert_element_type x10 -> x0, other arithmetic: 6.3 us -> none  [the longest x9 6.21 us: shards(): image = band[tindex].astype(jnp.float32)]
    ppermute x20 -> x4, waiting for transfers between devices: 4.49 us -> 0.53 us  [towards(): return lax.ppermute(array, axis, pairs)]
  transfers between devices with their start and end apart: 20 -> 4, of which waited for: 3 -> 1; matrix products, arithmetic and copies ran while one was open for 5% -> 0% of each run, Pallas kernels for 0% -> 8%
where the time goes in v1:
time: 72.2 us; the launch traced here: 71.9 us
  blocking collectives  40.1 us (56%)
  Pallas kernels  14 us (19%)
  starting transfers between devices  12.4 us (17%)
  local copies, waits for them, and re-layouts  4.16 us (6%)
  between operations  0.81 us (1%)
    all_to_all x1, blocking collectives, shards(): lax.all_to_all(jnp.broadcast_to(message[None], (n, 1, LANES)), ALL, 0, 0,...  40.1 us
    ppermute x4, starting transfers between devices, towards(): return lax.ppermute(array, axis, pairs)  12.4 us
    pallas_call x1, Pallas kernels, shards(): call(functools.partial(outer_sums, rows * ROWS, cols * COLS), (field, fie...  6.14 us
    pallas_call x1, Pallas kernels, shards(): call(inner_sums, (sums, sums), (slab, slab, tile), name='inner_sums')  4.77 us
    unnamed x14, local copies, waits for them, and re-layouts  2.84 us
  transfers between devices with their start and end apart: 4, of which 1 were waited for; matrix products, arithmetic and copies ran while one was open for 0% of the time, Pallas kernels for 8%

profile of v1, /device:TPU:1, one launch (start us, length us, event | category | flops | bytes accessed | tf_op | source)
XLA Modules:
  0.0 71.9 jit_solution(2294559714427641618)
XLA Ops:
  0.6 0.0 copy-start.4
  0.6 1.2 %fusion = (bf16[45,16,256]{2,1,0:T(8,128)(2,1)S(1)}, bf16[45,16,256]{2,1,0:T(8,128)(2,1)S(1)}) fusion(bf16[81,64,256]{2,1,0:T(8,128)(2,1)} %views.5), kind=kLoop, calls=%fused_computation | loop fusion | bytes 1474560 | tf_op jit(solution)/shard_map/slice | solution.py:415
  1.9 5.1 %collective-permute-start.1 = (bf16[45,16,256]{2,1,0:T(8,128)(2,1)S(1)}, bf16[45,16,256]{2,1,0:T(8,128)(2,1)S(1)}, u32[]{:S(2)}, u32[]{:S(2)}) collective-permute-start(bf16[45,16,256]{2,1,0:T(8,128)(2,1)S(1)} %get-tuple-element.16), channel_id=1, source_target_pairs={{8,0},{16,8},{24,16},{32,24},{40,32},{48,40},{56,48},{64,56},{72,6... | collective-permute-start | bytes 1105928 | tf_op jit(solution)/shard_map/ppermute | solution.py:413
  7.1 1.9 %collective-permute-start = (bf16[45,16,256]{2,1,0:T(8,128)(2,1)S(1)}, bf16[45,16,256]{2,1,0:T(8,128)(2,1)S(1)}, u32[]{:S(2)}, u32[]{:S(2)}) collective-permute-start(bf16[45,16,256]{2,1,0:T(8,128)(2,1)S(1)} %get-tuple-element.17), channel_id=1, source_target_pairs={{0,8},{8,16},{16,24},{24,32},{32,40},{40,48},{48,56},{56,64},{64,7... | collective-permute-start | bytes 1105928 | tf_op jit(solution)/shard_map/ppermute | solution.py:413
  9.0 0.0 copy-start
  9.0 1.7 %copy-done = bf16[81,64,256]{2,1,0:T(8,128)(2,1)S(1)} copy-done((bf16[81,64,256]{2,1,0:T(8,128)(2,1)S(1)}, bf16[81,64,256]{2,1,0:T(8,128)(2,1)}, u32[]{:S(2)}) %copy-start) | copy-done | bytes 2654232
  10.7 0.0 copy-start.2
  10.7 1.1 %copy-done.2 = bf16[9,256,128]{2,1,0:T(8,128)(2,1)S(1)} copy-done((bf16[9,256,128]{2,1,0:T(8,128)(2,1)S(1)}, bf16[9,256,128]{2,1,0:T(8,128)(2,1)}, u32[]{:S(2)}) %copy-start.2) | copy-done | bytes 589848
  11.8 0.0 copy-start.1
  11.8 1.0 %pack_own.1.own = bf16[576,128]{1,0:T(8,128)(2,1)S(1)} custom-call(bf16[81,64,256]{2,1,0:T(8,128)(2,1)S(1)} %copy-done, bf16[9,256,128]{2,1,0:T(8,128)(2,1)S(1)} %copy-done.2), custom_call_target="tpu_custom_call" | custom-call | tf_op jit(solution)/shard_map/pack_own/pallas_call | solution.py:417
  12.8 0.0 copy-start.3
  12.9 0.0 copy-start.5
  12.9 0.0 copy-start.6
  12.9 0.0 collective-permute-done.1.below
  12.9 0.5 collective-permute-done.above
  13.4 0.9 %pack_edges.1.own = bf16[736,128]{1,0:T(8,128)(2,1)S(1)} custom-call(bf16[45,16,256]{2,1,0:T(8,128)(2,1)S(1)} %collective-permute-done.above, bf16[45,16,256]{2,1,0:T(8,128)(2,1)S(1)} %collective-permute-done.1.below, bf16[9,256,128]{2,1,0:T(8,128)(2,1)S(1)} %copy-done.2, bf16[576,128]{1,0:T(8,128)(2,1)S(1)} %pack_own.1.own), custom_call_target="tpu_custom_call" | custom-call | tf_op jit(solution)/shard_map/pack_edges/pallas_call | solution.py:418
  14.3 1.3 %collective-permute-start.3 = (bf16[736,128]{1,0:T(8,128)(2,1)S(1)}, bf16[736,128]{1,0:T(8,128)(2,1)S(1)}, u32[]{:S(2)}, u32[]{:S(2)}) collective-permute-start(bf16[736,128]{1,0:T(8,128)(2,1)S(1)} %pack_edges.1.own), channel_id=1, source_target_pairs={{1,0},{2,1},{3,2},{4,3},{5,4},{6,5},{7,6},{9,8},{10,9},{11,10},{12... | collective-permute-start | bytes 565256 | tf_op jit(solution)/shard_map/ppermute | solution.py:413
  15.6 4.0 %collective-permute-start.2 = (bf16[736,128]{1,0:T(8,128)(2,1)S(1)}, bf16[736,128]{1,0:T(8,128)(2,1)S(1)}, u32[]{:S(2)}, u32[]{:S(2)}) collective-permute-start(bf16[736,128]{1,0:T(8,128)(2,1)S(1)} %pack_edges.1.own), channel_id=1, source_target_pairs={{0,1},{1,2},{2,3},{3,4},{4,5},{5,6},{6,7},{8,9},{9,10},{10,11},{11... | collective-permute-start | bytes 565256 | tf_op jit(solution)/shard_map/ppermute | solution.py:413
  19.6 0.0 copy-done.4
  19.7 0.0 copy-done.1
  19.7 4.8 %inner_sums.1 = (f32[2,72,128]{2,1,0:T(8,128)S(1)}, f32[2,72,128]{2,1,0:T(8,128)S(1)}) custom-call(bf16[81,64,256]{2,1,0:T(8,128)(2,1)S(1)} %copy-done.1, bf16[45,16,256]{2,1,0:T(8,128)(2,1)S(1)} %collective-permute-done.above, bf16[45,16,256]{2,1,0:T(8,128)(2,1)S(1)} %collective-permute-done.1.below, bf16[2,4,256,256]{3,2,1,0:T(8,128)(2,1)S(1)} %copy-done.4), custom_call_target="tpu_custom_call" | custom-call | tf_op jit(solution)/shard_map/inner_sums/pallas_call | solution.py:426
  24.4 0.0 collective-permute-done.3.right
  24.5 0.0 collective-permute-done.2.left
  24.5 0.0 copy-done.3
  24.5 0.0 copy-done.5
  24.5 0.0 copy-done.6
  24.5 6.1 %outer_sums.1 = (f32[72,256]{1,0:T(8,128)S(1)}, f32[72,256]{1,0:T(8,128)S(1)}, f32[72,256]{1,0:T(8,128)S(1)}, f32[72,256]{1,0:T(8,128)S(1)}, f32[1,128]{1,0:T(1,128)S(1)}) custom-call(bf16[81,64,256]{2,1,0:T(8,128)(2,1)S(1)} %copy-done.1, bf16[45,16,256]{2,1,0:T(8,128)(2,1)S(1)} %collective-permute-done.above, ...), custom_call_target="tpu_custom_call" | custom-call | tf_op jit(solution)/shard_map/outer_sums/pallas_call | solution.py:431
  30.6 0.1 broadcast_in_dim.9
  30.7 40.1 %all_to_all.5 = f32[256,1,128]{2,1,0:T(1,128)S(1)} all-to-all(f32[256,1,128]{2,1,0:T(1,128)S(1)} %broadcast_in_dim.9), channel_id=1, replica_groups=mesh['row'=32,'col'=8] {'row','col'}, dimensions={0} | all-to-all | bytes 262144 | tf_op jit(solution)/shard_map/all_to_all | solution.py:438
  70.8 1.1 %finish.1 = (f32[64,256]{1,0:T(8,128)}, f32[64,256]{1,0:T(8,128)}) custom-call(f32[256,128]{1,0:T(8,128)S(1)} %bitcast.2, f32[72,256]{1,0:T(8,128)S(1)} %get-tuple-element.12.zed_ref, f32[72,256]{1,0:T(8,128)S(1)} %get-tuple-element.13.near_ref, f32[72,256]{1,0:T(8,128)S(1)} %get-tuple-element.14.next_ref, f32[72,256]{1,0:T(8,128)S(1)} %get-tuple-element.15.precond_ref), custom_call_target="tpu_custom_call" | custom-call | tf_op jit(solution)/shard_map/finish/pallas_call | solution.py:442
Async XLA Ops:
  0.6 19.0 %copy-start.4 = (bf16[2,4,256,256]{3,2,1,0:T(8,128)(2,1)S(1)}, bf16[2,4,256,256]{3,2,1,0:T(8,128)(2,1)}, u32[]{:S(2)}) copy-start(bf16[2,4,256,256]{3,2,1,0:T(8,128)(2,1)} %constant.11.clone.inner) | copy-start | bytes 3145732
  1.9 11.0 %collective-permute-start.1 = (bf16[45,16,256]{2,1,0:T(8,128)(2,1)S(1)}, bf16[45,16,256]{2,1,0:T(8,128)(2,1)S(1)}, u32[]{:S(2)}, u32[]{:S(2)}) collective-permute-start(bf16[45,16,256]{2,1,0:T(8,128)(2,1)S(1)} %get-tuple-element.16), channel_id=1, source_target_pairs={{8,0},{16,8},{24,16},{32,24},{40,32},{48,40},{56,48},{64,56},{72,6... | collective-permute-start | bytes 1105928 | tf_op jit(solution)/shard_map/ppermute | solution.py:413
  7.1 6.4 %collective-permute-start = (bf16[45,16,256]{2,1,0:T(8,128)(2,1)S(1)}, bf16[45,16,256]{2,1,0:T(8,128)(2,1)S(1)}, u32[]{:S(2)}, u32[]{:S(2)}) collective-permute-start(bf16[45,16,256]{2,1,0:T(8,128)(2,1)S(1)} %get-tuple-element.17), channel_id=1, source_target_pairs={{0,8},{8,16},{16,24},{24,32},{32,40},{40,48},{48,56},{56,64},{64,7... | collective-permute-start | bytes 1105928 | tf_op jit(solution)/shard_map/ppermute | solution.py:413
  9.0 1.8 %copy-start = (bf16[81,64,256]{2,1,0:T(8,128)(2,1)S(1)}, bf16[81,64,256]{2,1,0:T(8,128)(2,1)}, u32[]{:S(2)}) copy-start(bf16[81,64,256]{2,1,0:T(8,128)(2,1)} %views.5) | copy-start | bytes 7962628
  10.7 1.1 %copy-start.2 = (bf16[9,256,128]{2,1,0:T(8,128)(2,1)S(1)}, bf16[9,256,128]{2,1,0:T(8,128)(2,1)}, u32[]{:S(2)}) copy-start(bf16[9,256,128]{2,1,0:T(8,128)(2,1)} %constant.10.clone.pack) | copy-start | bytes 1769476
  11.8 7.9 %copy-start.1 = (bf16[81,64,256]{2,1,0:T(8,128)(2,1)S(1)}, bf16[81,64,256]{2,1,0:T(8,128)(2,1)}, u32[]{:S(2)}) copy-start(bf16[81,64,256]{2,1,0:T(8,128)(2,1)} %views.5) | copy-start | bytes 7962628
  12.8 11.6 %copy-start.3 = (bf16[2,4,256,256]{3,2,1,0:T(8,128)(2,1)S(1)}, bf16[2,4,256,256]{3,2,1,0:T(8,128)(2,1)}, u32[]{:S(2)}) copy-start(bf16[2,4,256,256]{3,2,1,0:T(8,128)(2,1)} %constant.12.clone.outer) | copy-start | bytes 3145732
  12.9 11.6 %copy-start.5 = (bf16[384,256]{1,0:T(8,128)(2,1)S(1)}, bf16[384,256]{1,0:T(8,128)(2,1)}, u32[]{:S(2)}) copy-start(bf16[384,256]{1,0:T(8,128)(2,1)} %constant.14.clone.ghost_center) | copy-start | bytes 589828
  12.9 11.6 %copy-start.6 = (bf16[384,256]{1,0:T(8,128)(2,1)S(1)}, bf16[384,256]{1,0:T(8,128)(2,1)}, u32[]{:S(2)}) copy-start(bf16[384,256]{1,0:T(8,128)(2,1)} %constant.13.clone.ghost) | copy-start | bytes 589828
  14.3 10.1 %collective-permute-start.3 = (bf16[736,128]{1,0:T(8,128)(2,1)S(1)}, bf16[736,128]{1,0:T(8,128)(2,1)S(1)}, u32[]{:S(2)}, u32[]{:S(2)}) collective-permute-start(bf16[736,128]{1,0:T(8,128)(2,1)S(1)} %pack_edges.1.own), channel_id=1, source_target_pairs={{1,0},{2,1},{3,2},{4,3},{5,4},{6,5},{7,6},{9,8},{10,9},{11,10},{12... | collective-permute-start | bytes 565256 | tf_op jit(solution)/shard_map/ppermute | solution.py:413
  15.6 8.8 %collective-permute-start.2 = (bf16[736,128]{1,0:T(8,128)(2,1)S(1)}, bf16[736,128]{1,0:T(8,128)(2,1)S(1)}, u32[]{:S(2)}, u32[]{:S(2)}) collective-permute-start(bf16[736,128]{1,0:T(8,128)(2,1)S(1)} %pack_edges.1.own), channel_id=1, source_target_pairs={{0,1},{1,2},{2,3},{3,4},{4,5},{5,6},{6,7},{8,9},{9,10},{10,11},{11... | collective-permute-start | bytes 565256 | tf_op jit(solution)/shard_map/ppermute | solution.py:413

commit v2 on v1

--- a/solution.py
+++ b/solution.py
@@ -18,7 +18,10 @@
 EDGE = 16
 OUT = 72
 SLAB = 96
-PACKED = ANG * ROWS + 10 * EDGE
+PIECES = 3
+PACKED = ANG * ROWS + 2 * PIECES * EDGE
+PAIRS = ((-4, -3), (-2, -1), (1, 2), (3, 4), (0, 0))
+SENT = len(PAIRS) * ROWS + PIECES * EDGE
 LANES = 128
 SMOOTH = 2.0
 DAMPING = 0.1
@@ -46,14 +49,6 @@
 
 
 def tables():
-    pack = np.zeros((ANG, COLS, LANES), np.float32)
-    for t in range(-HALF, HALF + 1):
-        if t >= 0:
-            for c in range(D0 * t + D0):
-                pack[t + HALF, c, lane_first(t, c)] = 1
-        if t <= 0:
-            for c in range(COLS - D0 * abs(t) - D0, COLS):
-                pack[t + HALF, c, lane_last(t, c)] = 1
     inner = np.zeros((2, HALF, COLS, 2 * LANES), np.float32)
     outer = np.zeros((2, HALF, COLS, 2 * LANES), np.float32)
     for a in range(1, HALF + 1):
@@ -81,58 +76,180 @@
             center[ghost_source(0, col), lane] = 1
     for col in (-3, -2, -1, COLS, COLS + 1, COLS + 2):
         center[ghost_source(0, col), LANES + (col % (3 * LANES)) % LANES] = 1
-    return tuple(x.astype(ml_dtypes.bfloat16) for x in (pack, inner, outer, ghost, center))
+    return tuple(x.astype(ml_dtypes.bfloat16) for x in (inner, outer, ghost, center))
 
 
 def dot(a, b):
     return jnp.dot(a, b, preferred_element_type=F32)
 
 
-def pack_own(views, pack, out):
-    for si in range(ANG):
-        total = dot(views[si * ANG], pack[0])
-        for ti in range(1, ANG):
-            total = total + dot(views[si * ANG + ti], pack[ti])
-        out[si * ROWS : (si + 1) * ROWS, :] = total.astype(jnp.bfloat16)
-
-
-def pack_edges(above, below, pack, own, out):
-    out[: ANG * ROWS, :] = own[...]
-    for side, ref in enumerate((above, below)):
-        for i in range(HALF + 1):
-            total = dot(ref[i * ANG], pack[0])
+def is_even(axis):
+    return lax.rem(lax.axis_index(axis), 2) == 0
+
+
+def pack_rows(views, send_pair, send_next, local, sems):
+    order = (4, 3, 0, 2, 1, -4, -3, -2, -1)
+    copies = {}
+    for s in order:
+        span = pl.ds((s + HALF) * ANG, ANG)
+        copies[s] = pltpu.make_async_copy(
+            views.at[span], local.at[span], sems.at[s + HALF]
+        )
+        copies[s].start()
+    even = is_even("row")
+    index = lax.broadcasted_iota(jnp.int32, (EDGE, COLS), 0)
+
+    def put(ups, q, ti, rows):
+        rows = rows.astype(jnp.bfloat16)
+
+        @pl.when(even == ups)
+        def _():
+            send_next[q * ANG + ti] = rows
+
+        @pl.when(even != ups)
+        def _():
+            send_pair[q * ANG + ti] = rows
+
+    for s in order:
+        copies[s].wait()
+        if s in (3, 2, -4):
+            continue
+        for ti in range(ANG):
+
+            def rows_of(s, start):
+                return local[(s + HALF) * ANG + ti, pl.ds(start, EDGE), :].astype(F32)
+
+            first = functools.partial(rows_of, start=0)
+            last = functools.partial(rows_of, start=ROWS - EDGE)
+            if s == 4:
+                put(True, 0, ti, first(4))
+            elif s == 0:
+                put(True, 1, ti, jnp.where(index < 12, first(3), pltpu.roll(first(0), 12, 0)))
+            elif s == 1:
+                put(True, 2, ti, jnp.where(index < 9, first(2), pltpu.roll(first(1), 9, 0)))
+            elif s == -3:
+                put(False, 0, ti, last(-4))
+                put(False, 1, ti, jnp.where(index < 4, pltpu.roll(last(0), 4, 0), last(-3)))
+            elif s == -1:
+                put(False, 2, ti, jnp.where(index < 7, pltpu.roll(last(-1), 7, 0), last(-2)))
+
+
+PLACES = {
+    ("above", 0): ((-4, 0),),
+    ("above", 1): ((-3, 0), (0, 12)),
+    ("above", 2): ((-2, 0), (-1, 9)),
+    ("below", 0): ((4, ROWS),),
+    ("below", 1): ((3, ROWS), (0, EDGE + ROWS - 12)),
+    ("below", 2): ((2, ROWS), (1, ROWS - 9)),
+}
+
+
+def packed_piece(side, q):
+    return ANG * ROWS + ((0 if side == "above" else PIECES) + q) * EDGE
+
+
+def share(first_of, second_of, to_left, to_right, at):
+    low = lax.broadcasted_iota(jnp.int32, first_of.shape, 1) < 64
+    turned = pltpu.roll(second_of, 64, 1)
+    to_left[pl.ds(at, first_of.shape[0]), :] = jnp.where(low, first_of, turned).astype(
+        jnp.bfloat16
+    )
+    turned = pltpu.roll(first_of, 64, 1)
+    to_right[pl.ds(at, first_of.shape[0]), :] = jnp.where(low, turned, second_of).astype(
+        jnp.bfloat16
+    )
+
+
+def pack_own(views, own, to_left, to_right, pack):
+    column = lax.broadcasted_iota(jnp.int32, (COLS, LANES), 0)
+    lane = lax.broadcasted_iota(jnp.int32, (COLS, LANES), 1)
+    for t in range(-HALF, HALF + 1):
+        hit = jnp.zeros((COLS, LANES), F32)
+        if t >= 0:
+            bound = D0 * t + D0
+            hit = jnp.where((column < bound) & (lane - column == lane_first(t, 0)), 1.0, hit)
+        if t <= 0:
+            start = COLS - D0 * abs(t) - D0
+            apart = lane_last(t, start) - start
+            hit = jnp.where((column >= start) & (lane - column == apart), 1.0, hit)
+        pack[t + HALF] = hit.astype(jnp.bfloat16)
+    for p, pair in enumerate(PAIRS):
+        both = []
+        for s in pair:
+            total = dot(views[(s + HALF) * ANG], pack[0])
             for ti in range(1, ANG):
-                total = total + dot(ref[i * ANG + ti], pack[ti])
-            at = ANG * ROWS + side * 5 * EDGE + i * EDGE
-            out[at : at + EDGE, :] = total.astype(jnp.bfloat16)
-
-
-def pieces(s):
-    if s > 0:
-        return (("own", 0), ("below", ROWS))
-    if s < 0:
-        return (("above", 0), ("own", EDGE))
-    return (("above", 0), ("own", EDGE), ("below", EDGE + ROWS))
+                total = total + dot(views[(s + HALF) * ANG + ti], pack[ti])
+            own[(s + HALF) * ROWS : (s + HALF + 1) * ROWS, :] = total.astype(jnp.bfloat16)
+            both.append(total)
+        share(both[0], both[1], to_left, to_right, p * ROWS)
+
+
+def pack_edges(
+    got_pair, got_next, pack, own_in, left_in, right_in,
+    above, below, own, send_pair, send_next, to_left, to_right,
+):
+    even = is_even("row")
+
+    @pl.when(even)
+    def _():
+        below[...] = got_pair[...]
+        above[...] = got_next[...]
+
+    @pl.when(jnp.logical_not(even))
+    def _():
+        below[...] = got_next[...]
+        above[...] = got_pair[...]
+
+    own[: ANG * ROWS, :] = own_in[...]
+    for q in range(PIECES):
+        both = []
+        for side, ref in (("above", above), ("below", below)):
+            total = dot(ref[q * ANG], pack[0])
+            for ti in range(1, ANG):
+                total = total + dot(ref[q * ANG + ti], pack[ti])
+            own[pl.ds(packed_piece(side, q), EDGE), :] = total.astype(jnp.bfloat16)
+            both.append(total)
+        share(both[0], both[1], to_left, to_right, q * EDGE)
+    rows = len(PAIRS) * ROWS
+    even = is_even("col")
+
+    def send(out, block, piece):
+        out[:rows, :] = block[...]
+        out[rows:, :] = piece[...]
+
+    @pl.when(even)
+    def _():
+        send(send_pair, right_in, to_right)
+        send(send_next, left_in, to_left)
+
+    @pl.when(jnp.logical_not(even))
+    def _():
+        send(send_pair, left_in, to_left)
+        send(send_next, right_in, to_right)
+
+
+def unshare(source, high, out):
+    def move(at, to, count, half):
+        rows = source[pl.ds(at, count), :]
+        if half != high:
+            rows = pltpu.roll(rows.astype(F32), 64, 1).astype(jnp.bfloat16)
+        out[pl.ds(to, count), :] = rows
+
+    for p, pair in enumerate(PAIRS):
+        for half, s in enumerate(pair):
+            if s or not half:
+                move(p * ROWS, (s + HALF) * ROWS, ROWS, half)
+    for q in range(PIECES):
+        for half, side in enumerate(("above", "below")):
+            move(len(PAIRS) * ROWS + q * EDGE, packed_piece(side, q), EDGE, half)
 
 
 def first_row(s):
     return D0 * s - 2 if s > 0 else EDGE - 2 + D0 * s
 
 
-def packed_rows(kind, s):
-    if kind == "own":
-        return (s + HALF) * ROWS, ROWS
-    if kind == "above":
-        return ANG * ROWS + (s + HALF) * EDGE, EDGE
-    return ANG * ROWS + 5 * EDGE + s * EDGE, EDGE
-
-
-def view_rows(kind, s, ti, views, above, below):
-    if kind == "own":
-        return views.at[(s + HALF) * ANG + ti]
-    if kind == "above":
-        return above.at[(s + HALF) * ANG + ti]
-    return below.at[s * ANG + ti]
+def own_row(s):
+    return 0 if s > 0 else EDGE
 
 
 def accumulate(s, warped, side, center, data, source):
@@ -154,16 +271,28 @@
 
 def zero_tails(slabs):
     for i in range(ANG):
-        slabs[i, pl.ds(SLAB - EDGE, EDGE), :] = jnp.zeros((EDGE, LANES), F32)
-
-
-def shifted_views(ti, matrix, lhs, center, warped, side, data, source):
+        slabs[i, pl.ds(ROWS, SLAB - ROWS), :] = jnp.zeros((SLAB - ROWS, LANES), F32)
+
+
+def fill_pieces(parts_of, outs):
+    for (side, q), places in PLACES.items():
+        parts = parts_of(side, q)
+        for s, at in places:
+            for out, part in zip(outs, parts):
+                fill(out.at[s + HALF], at, part)
+
+
+def halves(both):
+    return both[:, :LANES], both[:, LANES:]
+
+
+def shifted_views(matrix, own, piece, center, warped, side, data, source):
+    fill_pieces(lambda name, q: halves(dot(piece(name, q), matrix)), (warped, side))
     for s in range(-HALF, HALF + 1):
         w, d = warped.at[s + HALF], side.at[s + HALF]
-        for kind, at in pieces(s):
-            both = dot(lhs(kind, s, ti), matrix)
-            fill(w, at, both[:, :LANES])
-            fill(d, at, both[:, LANES:])
+        both = dot(own(s), matrix)
+        fill(w, own_row(s), both[:, :LANES])
+        fill(d, own_row(s), both[:, LANES:])
         data, source = accumulate(s, w, d, center, data, source)
     return data, source
 
@@ -172,18 +301,19 @@
     zero_tails(warped)
     zero_tails(side)
     zero = jnp.zeros((OUT, LANES), F32)
+    edges = {"above": above, "below": below}
     for tile in (0, 1):
         lanes = slice(tile * LANES, (tile + 1) * LANES)
+        fill_pieces(
+            lambda name, q: (edges[name][q * ANG + HALF][:, lanes].astype(F32),), (warped,)
+        )
+        data = source = zero
         for s in (0, -4, -3, -2, -1, 1, 2, 3, 4):
-            for kind, at in pieces(s):
-                ref = view_rows(kind, s, HALF, views, above, below)
-                fill(warped.at[s + HALF], at, ref[:, lanes].astype(F32))
+            w = warped.at[s + HALF]
+            fill(w, own_row(s), views[(s + HALF) * ANG + HALF][:, lanes].astype(F32))
             if s == 0:
-                center_ref[...] = warped[HALF, pl.ds(first_row(0), OUT), :]
-                data = source = zero
-            data, source = accumulate(
-                s, warped.at[s + HALF], None, center_ref[...], data, source
-            )
+                center_ref[...] = w[pl.ds(first_row(0), OUT), :]
+            data, source = accumulate(s, w, None, center_ref[...], data, source)
         data_out[tile] = data
         source_out[tile] = source
         sign = 1 - tile
@@ -191,9 +321,9 @@
         def body(a, carry, tile=tile, sign=sign):
             ti = HALF + 1 + a if sign else HALF - 1 - a
             data, source = shifted_views(
-                ti,
                 inner[sign, a],
-                lambda kind, s, ti: view_rows(kind, s, ti, views, above, below)[...],
+                lambda s: views[(s + HALF) * ANG + ti],
+                lambda name, q: edges[name][q * ANG + ti],
                 center_ref[...],
                 warped,
                 side,
@@ -214,8 +344,8 @@
     above,
     below,
     own,
-    left,
-    right,
+    got_pair,
+    got_next,
     data_in,
     source_in,
     outer,
@@ -232,33 +362,53 @@
     side,
     center_ref,
     center_slab,
+    left,
+    right,
 ):
+    even = is_even("col")
+
+    @pl.when(even)
+    def _():
+        unshare(got_next, 1, left)
+        unshare(got_pair, 0, right)
+
+    @pl.when(jnp.logical_not(even))
+    def _():
+        unshare(got_pair, 1, left)
+        unshare(got_next, 0, right)
+
+    edges = {"above": above, "below": below}
     zero_tails(warped)
     zero_tails(side)
     zero = jnp.zeros((OUT, LANES), F32)
-    for kind, at in pieces(0):
-        ref = view_rows(kind, 0, HALF, views, above, below)
+
+    def ghost_rows(row, count):
+        return jnp.concatenate([x[pl.ds(row, count), :] for x in (left, own, right)], axis=1)
+
+    def fill_center(at, ref, row, count):
         fill(center_slab.at[0], at, ref[:, :LANES].astype(F32))
         fill(center_slab.at[1], at, ref[:, LANES:].astype(F32))
-        row, count = packed_rows(kind, 0)
-        lhs = jnp.concatenate([x[pl.ds(row, count), :] for x in (left, own, right)], axis=1)
-        both = dot(lhs, ghost_center[...])
+        both = dot(ghost_rows(row, count), ghost_center[...])
         fill(warped.at[HALF], at, both[:, :LANES])
         fill(center_slab.at[2], at, both[:, LANES:])
+
+    for name in ("above", "below"):
+        fill_center(PLACES[name, 1][1][1], edges[name][ANG + HALF], packed_piece(name, 1), EDGE)
+    fill_center(EDGE, views[HALF * ANG + HALF], HALF * ROWS, ROWS)
     for tile in (0, 1):
         data_acc[tile] = data_in[tile]
         source_acc[tile] = source_in[tile]
     center_ref[...] = warped[HALF, pl.ds(first_row(0), OUT), :]
-    data = source = zero
-    for s in range(-HALF, HALF + 1):
-        w, d = warped.at[s + HALF], side.at[s + HALF]
-        for kind, at in pieces(s):
-            row, count = packed_rows(kind, s)
-            lhs = jnp.concatenate([x[pl.ds(row, count), :] for x in (left, own, right)], axis=1)
-            both = dot(lhs, ghost[...])
-            fill(w, at, both[:, :LANES])
-            fill(d, at, both[:, LANES:])
-        data, source = accumulate(s, w, d, center_ref[...], data, source)
+    data, source = shifted_views(
+        ghost[...],
+        lambda s: ghost_rows((s + HALF) * ROWS, ROWS),
+        lambda name, q: ghost_rows(packed_piece(name, q), EDGE),
+        center_ref[...],
+        warped,
+        side,
+        zero,
+        zero,
+    )
     for step in (4, 8, 16, 32):
         data = data + pltpu.roll(data, LANES - step, 1)
         source = source + pltpu.roll(source, LANES - step, 1)
@@ -268,17 +418,23 @@
         sign = tile
         center_ref[...] = center_slab[tile, pl.ds(first_row(0), OUT), :]
 
-        def lhs_of(kind, s, ti, sign=sign):
-            ref = view_rows(kind, s, ti, views, above, below)
-            row, count = packed_rows(kind, s)
+        def lhs(ref, row, sign=sign):
+            count = ref.shape[0]
             if sign:
                 return jnp.concatenate([ref[:, LANES:], right[pl.ds(row, count), :]], axis=1)
             return jnp.concatenate([left[pl.ds(row, count), :], ref[:, :LANES]], axis=1)
 
-        def body(a, carry, tile=tile, sign=sign, lhs_of=lhs_of):
+        def body(a, carry, tile=tile, sign=sign, lhs=lhs):
             ti = HALF + 1 + a if sign else HALF - 1 - a
             data, source = shifted_views(
-                ti, outer[sign, a], lhs_of, center_ref[...], warped, side, zero, zero
+                outer[sign, a],
+                lambda s: lhs(views.at[(s + HALF) * ANG + ti], (s + HALF) * ROWS),
+                lambda name, q: lhs(edges[name].at[q * ANG + ti], packed_piece(name, q)),
+                center_ref[...],
+                warped,
+                side,
+                zero,
+                zero,
             )
             data_acc[tile] += data
             source_acc[tile] += source
@@ -391,35 +547,56 @@
     )
 
 
-def call(kernel, outs, scratch=(), name=None):
+def call(kernel, outs, scratch=(), name=None, **more):
     return pl.pallas_call(
         kernel,
         out_shape=outs,
         scratch_shapes=list(scratch),
         compiler_params=pltpu.CompilerParams(vmem_limit_bytes=24 * 1024 * 1024),
         name=name,
-    )
+        **more,
+    )
+
+
+def swap(array, axis, start):
+    pairs = []
+    for i in range(start, lax.axis_size(axis) - 1, 2):
+        pairs += [(i, i + 1), (i + 1, i)]
+    return lax.ppermute(array, axis, pairs)
 
 
 def shards(views):
     rows, cols = lax.axis_size("row"), lax.axis_size("col")
-    pack, inner, outer, ghost, center = (jnp.asarray(x) for x in tables())
+    inner, outer, ghost, center = (jnp.asarray(x) for x in tables())
     bf16 = jnp.bfloat16
     struct = jax.ShapeDtypeStruct
 
-    def towards(array, axis, step):
-        n = lax.axis_size(axis)
-        pairs = [(i, i + step) for i in range(n) if 0 <= i + step < n]
-        return lax.ppermute(array, axis, pairs)
-
-    below = towards(views[HALF * ANG :, :EDGE, :], "row", -1)
-    above = towards(views[: (HALF + 1) * ANG, ROWS - EDGE :, :], "row", 1)
-    own = call(pack_own, struct((ANG * ROWS, LANES), bf16), name="pack_own")(views, pack)
-    own = call(pack_edges, struct((PACKED, LANES), bf16), name="pack_edges")(
-        above, below, pack, own
-    )
-    left = towards(own, "col", 1)
-    right = towards(own, "col", -1)
+    edge = struct((PIECES * ANG, EDGE, COLS), bf16)
+    pair, after, views = call(
+        pack_rows,
+        (edge, edge, struct(views.shape, bf16)),
+        (pltpu.SemaphoreType.DMA((ANG,)),),
+        name="pack_rows",
+        in_specs=[pl.BlockSpec(memory_space=pltpu.HBM)],
+    )(views)
+    pair = swap(pair, "row", 0)
+    after = swap(after, "row", 1)
+    shared = struct((len(PAIRS) * ROWS, LANES), bf16)
+    own, to_left, to_right, pack = call(
+        pack_own,
+        (struct((ANG * ROWS, LANES), bf16), shared, shared, struct((ANG, COLS, LANES), bf16)),
+        name="pack_own",
+    )(views)
+    sent = struct((SENT, LANES), bf16)
+    small = pltpu.VMEM((PIECES * EDGE, LANES), bf16)
+    above, below, own, pair, after = call(
+        pack_edges,
+        (edge, edge, struct((PACKED, LANES), bf16), sent, sent),
+        (small, small),
+        name="pack_edges",
+    )(pair, after, pack, own, to_left, to_right)
+    pair = swap(pair, "col", 0)
+    after = swap(after, "col", 1)
     slab = pltpu.VMEM((ANG, SLAB, LANES), F32)
     tile = pltpu.VMEM((OUT, LANES), F32)
     sums = struct((2, OUT, LANES), F32)
@@ -431,9 +608,18 @@
     zed, near, nxt, precond, message = call(
         functools.partial(outer_sums, rows * ROWS, cols * COLS),
         (field, field, field, field, struct((1, LANES), F32)),
-        (acc, acc, slab, slab, tile, pltpu.VMEM((3, SLAB, LANES), F32)),
+        (
+            acc,
+            acc,
+            slab,
+            slab,
+            tile,
+            pltpu.VMEM((3, SLAB, LANES), F32),
+            pltpu.VMEM((PACKED, LANES), bf16),
+            pltpu.VMEM((PACKED, LANES), bf16),
+        ),
         name="outer_sums",
-    )(views, above, below, own, left, right, data, source, outer, ghost, center)
+    )(views, above, below, own, pair, after, data, source, outer, ghost, center)
     n = rows * cols
     messages = lax.all_to_all(
         jnp.broadcast_to(message[None], (n, 1, LANES)), ALL, 0, 0, tiled=True

time: 72.2 us -> 62.4 us (0.86)
  blocking collectives: 40.1 us -> 33.6 us
  starting transfers between devices: 12.4 us -> 5.94 us
  waiting for transfers between devices: 0.53 us -> 6.06 us
  local copies, waits for them, and re-layouts: 4.16 us -> 1.83 us
    all_to_all x1, blocking collectives: 40.1 us -> 33.6 us  [shards(): lax.all_to_all(jnp.broadcast_to(message[None], (n, 1, LANES)), ALL, 0, 0,...]
    ppermute x4, starting transfers between devices: 12.4 us -> 5.94 us  [swap(): return lax.ppermute(array, axis, pairs)]
    ppermute x4, waiting for transfers between devices: 0.53 us -> 6.06 us  [swap(): return lax.ppermute(array, axis, pairs)]
    slice x1 -> x0, local copies, waits for them, and re-layouts: 1.25 us -> none  [shards(): below = towards(views[HALF * ANG:, :EDGE, :], 'row', -1)]
    unnamed x14 -> x10, local copies, waits for them, and re-layouts: 2.84 us -> 1.76 us
    pallas_call x2 -> x3, Pallas kernels: 1.96 us -> 3.04 us  [the longest x1 1.34 us: shards(): call(pack_own, (struct((ANG * ROWS, LANES), bf16), shared, shared, struct...]
  transfers between devices with their start and end apart: 4 -> 4, of which waited for: 1 -> 1; matrix products, arithmetic and copies ran while one was open for 0% -> 0% of each run, Pallas kernels for 8% -> 9%
where the time goes in v2:
time: 62.4 us; the launch traced here: 62.2 us
  blocking collectives  33.6 us (54%)
  Pallas kernels  14 us (22%)
  waiting for transfers between devices  6.06 us (10%)
  starting transfers between devices  5.94 us (10%)
  local copies, waits for them, and re-layouts  1.83 us (3%)
  between operations  0.77 us (1%)
    all_to_all x1, blocking collectives, shards(): lax.all_to_all(jnp.broadcast_to(message[None], (n, 1, LANES)), ALL, 0, 0,...  33.6 us
    ppermute x4, waiting for transfers between devices, swap(): return lax.ppermute(array, axis, pairs)  6.06 us
    ppermute x4, starting transfers between devices, swap(): return lax.ppermute(array, axis, pairs)  5.94 us
    pallas_call x1, Pallas kernels, shards(): call(functools.partial(outer_sums, rows * ROWS, cols * COLS), (field, fie...  5.63 us
    pallas_call x1, Pallas kernels, shards(): call(inner_sums, (sums, sums), (slab, slab, tile), name='inner_sums')  4.24 us
    unnamed x10, local copies, waits for them, and re-layouts  1.76 us
    pallas_call x1, Pallas kernels, shards(): call(pack_own, (struct((ANG * ROWS, LANES), bf16), shared, shared, struct...  1.34 us
  transfers between devices with their start and end apart: 4, of which 1 were waited for; matrix products, arithmetic and copies ran while one was open for 0% of the time, Pallas kernels for 9%

profile of v2, /device:TPU:1, one launch (start us, length us, event | category | flops | bytes accessed | tf_op | source)
XLA Modules:
  0.0 62.2 jit_solution(11404299584436814310)
XLA Ops:
  0.6 0.0 copy-start
  0.6 1.7 %copy-done = bf16[81,64,256]{2,1,0:T(8,128)(2,1)S(1)} copy-done((bf16[81,64,256]{2,1,0:T(8,128)(2,1)S(1)}, bf16[81,64,256]{2,1,0:T(8,128)(2,1)}, u32[]{:S(2)}) %copy-start) | copy-done | bytes 2654232
  2.4 1.0 %pack_rows.1 = (bf16[27,16,256]{2,1,0:T(8,128)(2,1)S(1)}, bf16[27,16,256]{2,1,0:T(8,128)(2,1)S(1)}, bf16[81,64,256]{2,1,0:T(8,128)(2,1)S(1)}) custom-call(bf16[81,64,256]{2,1,0:T(8,128)(2,1)S(1)} %copy-done), custom_call_target="tpu_custom_call" | custom-call | tf_op jit(solution)/shard_map/pack_rows/pallas_call | solution.py:575
  3.4 0.0 copy-start.2
  3.4 3.3 %collective-permute-start = (bf16[27,16,256]{2,1,0:T(8,128)(2,1)S(1)}, bf16[27,16,256]{2,1,0:T(8,128)(2,1)S(1)}, u32[]{:S(2)}, u32[]{:S(2)}) collective-permute-start(bf16[27,16,256]{2,1,0:T(8,128)(2,1)S(1)} %get-tuple-element.22), channel_id=1, source_target_pairs={{0,8},{8,0},{16,24},{24,16},{32,40},{40,32},{48,56},{56,48},{64,72... | collective-permute-start | bytes 663560 | tf_op jit(solution)/shard_map/ppermute | solution.py:565
  6.7 1.9 %collective-permute-start.1 = (bf16[27,16,256]{2,1,0:T(8,128)(2,1)S(1)}, bf16[27,16,256]{2,1,0:T(8,128)(2,1)S(1)}, u32[]{:S(2)}, u32[]{:S(2)}) collective-permute-start(bf16[27,16,256]{2,1,0:T(8,128)(2,1)S(1)} %get-tuple-element.23), channel_id=1, source_target_pairs={{8,16},{16,8},{24,32},{32,24},{40,48},{48,40},{56,64},{64,56},{72,... | collective-permute-start | bytes 663560 | tf_op jit(solution)/shard_map/ppermute | solution.py:565
  8.6 1.3 %pack_own.1 = (bf16[576,128]{1,0:T(8,128)(2,1)S(1)}, bf16[320,128]{1,0:T(8,128)(2,1)S(1)}, bf16[320,128]{1,0:T(8,128)(2,1)S(1)}, bf16[9,256,128]{2,1,0:T(8,128)(2,1)S(1)}) custom-call(bf16[81,64,256]{2,1,0:T(8,128)(2,1)S(1)} %get-tuple-element.21.views), custom_call_target="tpu_custom_call" | custom-call | tf_op jit(solution)/shard_map/pack_own/pallas_call | solution.py:585
  10.0 0.0 collective-permute-done.got_pair
  10.0 6.1 %collective-permute-done.1.got_next = bf16[27,16,256]{2,1,0:T(8,128)(2,1)S(1)} collective-permute-done((bf16[27,16,256]{2,1,0:T(8,128)(2,1)S(1)}, bf16[27,16,256]{2,1,0:T(8,128)(2,1)S(1)}, u32[]{:S(2)}, u32[]{:S(2)}) %collective-permute-start.1) | collective-permute-done | bytes 221216 | tf_op jit(solution)/shard_map/ppermute | solution.py:565
  16.1 0.0 copy-start.1
  16.1 0.0 copy-start.3
  16.1 0.0 copy-start.4
  16.1 0.7 %pack_edges.1 = (bf16[27,16,256]{2,1,0:T(8,128)(2,1)S(1)}, bf16[27,16,256]{2,1,0:T(8,128)(2,1)S(1)}, bf16[672,128]{1,0:T(8,128)(2,1)S(1)}, bf16[368,128]{1,0:T(8,128)(2,1)S(1)}, bf16[368,128]{1,0:T(8,128)(2,1)S(1)}) custom-call(bf16[27,16,256]{2,1,0:T(8,128)(2,1)S(1)} %collective-permute-done.got_pair, ...), custom_call_target="tpu_custom_call" | custom-call | tf_op jit(solution)/shard_map/pack_edges/pallas_call | solution.py:592
  16.8 0.0 collective-permute-start.2
  16.8 0.7 %collective-permute-start.3 = (bf16[368,128]{1,0:T(8,128)(2,1)S(1)}, bf16[368,128]{1,0:T(8,128)(2,1)S(1)}, u32[]{:S(2)}, u32[]{:S(2)}) collective-permute-start(bf16[368,128]{1,0:T(8,128)(2,1)S(1)} %get-tuple-element.32), channel_id=1, source_target_pairs={{1,2},{2,1},{3,4},{4,3},{5,6},{6,5},{9,10},{10,9},{11,12},{12,11},... | collective-permute-start | bytes 282632 | tf_op jit(solution)/shard_map/ppermute | solution.py:565
  17.5 0.0 copy-done.2
  17.5 4.2 %inner_sums.1 = (f32[2,72,128]{2,1,0:T(8,128)S(1)}, f32[2,72,128]{2,1,0:T(8,128)S(1)}) custom-call(bf16[81,64,256]{2,1,0:T(8,128)(2,1)S(1)} %get-tuple-element.21.views, bf16[27,16,256]{2,1,0:T(8,128)(2,1)S(1)} %get-tuple-element.28.above, bf16[27,16,256]{2,1,0:T(8,128)(2,1)S(1)} %get-tuple-element.29.below, bf16[2,4,256,256]{3,2,1,0:T(8,128)(2,1)S(1)} %copy-done.2), custom_call_target="tpu_custom_call" | custom-call | tf_op jit(solution)/shard_map/inner_sums/pallas_call | solution.py:603
  21.7 0.0 collective-permute-done.2.got_pair
  21.8 0.0 collective-permute-done.3.got_next
  21.8 0.0 copy-done.1
  21.8 0.0 copy-done.3
  21.8 0.0 copy-done.4
  21.8 5.6 %outer_sums.1 = (f32[72,256]{1,0:T(8,128)S(1)}, f32[72,256]{1,0:T(8,128)S(1)}, f32[72,256]{1,0:T(8,128)S(1)}, f32[72,256]{1,0:T(8,128)S(1)}, f32[1,128]{1,0:T(1,128)S(1)}) custom-call(bf16[81,64,256]{2,1,0:T(8,128)(2,1)S(1)} %get-tuple-element.21.views, bf16[27,16,256]{2,1,0:T(8,128)(2,1)S(1)} %get-tuple-element.28.above, ...), custom_call_target="tpu_custom_call" | custom-call | tf_op jit(solution)/shard_map/outer_sums/pallas_call | solution.py:608
  27.4 0.1 broadcast_in_dim.9
  27.5 33.6 %all_to_all.5 = f32[256,1,128]{2,1,0:T(1,128)S(1)} all-to-all(f32[256,1,128]{2,1,0:T(1,128)S(1)} %broadcast_in_dim.9), channel_id=1, replica_groups=mesh['row'=32,'col'=8] {'row','col'}, dimensions={0} | all-to-all | bytes 262144 | tf_op jit(solution)/shard_map/all_to_all | solution.py:624
  61.1 1.1 %finish.1 = (f32[64,256]{1,0:T(8,128)}, f32[64,256]{1,0:T(8,128)}) custom-call(f32[256,128]{1,0:T(8,128)S(1)} %bitcast.2, f32[72,256]{1,0:T(8,128)S(1)} %get-tuple-element.36.zed_ref, f32[72,256]{1,0:T(8,128)S(1)} %get-tuple-element.37.near_ref, f32[72,256]{1,0:T(8,128)S(1)} %get-tuple-element.38.next_ref, f32[72,256]{1,0:T(8,128)S(1)} %get-tuple-element.39.precond_ref), custom_call_target="tpu_custom_call" | custom-call | tf_op jit(solution)/shard_map/finish/pallas_call | solution.py:628
Async XLA Ops:
  0.6 1.8 %copy-start = (bf16[81,64,256]{2,1,0:T(8,128)(2,1)S(1)}, bf16[81,64,256]{2,1,0:T(8,128)(2,1)}, u32[]{:S(2)}) copy-start(bf16[81,64,256]{2,1,0:T(8,128)(2,1)} %views.1) | copy-start | bytes 7962628
  3.4 14.1 %copy-start.2 = (bf16[2,4,256,256]{3,2,1,0:T(8,128)(2,1)S(1)}, bf16[2,4,256,256]{3,2,1,0:T(8,128)(2,1)}, u32[]{:S(2)}) copy-start(bf16[2,4,256,256]{3,2,1,0:T(8,128)(2,1)} %constant.8.clone.inner) | copy-start | bytes 3145732
  3.4 6.6 %collective-permute-start = (bf16[27,16,256]{2,1,0:T(8,128)(2,1)S(1)}, bf16[27,16,256]{2,1,0:T(8,128)(2,1)S(1)}, u32[]{:S(2)}, u32[]{:S(2)}) collective-permute-start(bf16[27,16,256]{2,1,0:T(8,128)(2,1)S(1)} %get-tuple-element.22), channel_id=1, source_target_pairs={{0,8},{8,0},{16,24},{24,16},{32,40},{40,32},{48,56},{56,48},{64,72... | collective-permute-start | bytes 663560 | tf_op jit(solution)/shard_map/ppermute | solution.py:565
  6.7 9.3 %collective-permute-start.1 = (bf16[27,16,256]{2,1,0:T(8,128)(2,1)S(1)}, bf16[27,16,256]{2,1,0:T(8,128)(2,1)S(1)}, u32[]{:S(2)}, u32[]{:S(2)}) collective-permute-start(bf16[27,16,256]{2,1,0:T(8,128)(2,1)S(1)} %get-tuple-element.23), channel_id=1, source_target_pairs={{8,16},{16,8},{24,32},{32,24},{40,48},{48,40},{56,64},{64,56},{72,... | collective-permute-start | bytes 663560 | tf_op jit(solution)/shard_map/ppermute | solution.py:565
  16.1 5.7 %copy-start.1 = (bf16[2,4,256,256]{3,2,1,0:T(8,128)(2,1)S(1)}, bf16[2,4,256,256]{3,2,1,0:T(8,128)(2,1)}, u32[]{:S(2)}) copy-start(bf16[2,4,256,256]{3,2,1,0:T(8,128)(2,1)} %constant.9.clone.outer) | copy-start | bytes 3145732
  16.1 5.7 %copy-start.3 = (bf16[384,256]{1,0:T(8,128)(2,1)S(1)}, bf16[384,256]{1,0:T(8,128)(2,1)}, u32[]{:S(2)}) copy-start(bf16[384,256]{1,0:T(8,128)(2,1)} %constant.11.clone.ghost_center) | copy-start | bytes 589828
  16.1 5.7 %copy-start.4 = (bf16[384,256]{1,0:T(8,128)(2,1)S(1)}, bf16[384,256]{1,0:T(8,128)(2,1)}, u32[]{:S(2)}) copy-start(bf16[384,256]{1,0:T(8,128)(2,1)} %constant.10.clone.ghost) | copy-start | bytes 589828
  16.8 5.0 %collective-permute-start.2 = (bf16[368,128]{1,0:T(8,128)(2,1)S(1)}, bf16[368,128]{1,0:T(8,128)(2,1)S(1)}, u32[]{:S(2)}, u32[]{:S(2)}) collective-permute-start(bf16[368,128]{1,0:T(8,128)(2,1)S(1)} %get-tuple-element.31), channel_id=1, source_target_pairs={{0,1},{1,0},{2,3},{3,2},{4,5},{5,4},{6,7},{7,6},{8,9},{9,8},{10,11... | collective-permute-start | bytes 282632 | tf_op jit(solution)/shard_map/ppermute | solution.py:565
  16.8 4.9 %collective-permute-start.3 = (bf16[368,128]{1,0:T(8,128)(2,1)S(1)}, bf16[368,128]{1,0:T(8,128)(2,1)S(1)}, u32[]{:S(2)}, u32[]{:S(2)}) collective-permute-start(bf16[368,128]{1,0:T(8,128)(2,1)S(1)} %get-tuple-element.32), channel_id=1, source_target_pairs={{1,2},{2,1},{3,4},{4,3},{5,6},{6,5},{9,10},{10,9},{11,12},{12,11},... | collective-permute-start | bytes 282632 | tf_op jit(solution)/shard_map/ppermute | solution.py:565

commit v3 on v2

--- a/solution.py
+++ b/solution.py
@@ -21,7 +21,7 @@
 PIECES = 3
 PACKED = ANG * ROWS + 2 * PIECES * EDGE
 PAIRS = ((-4, -3), (-2, -1), (1, 2), (3, 4), (0, 0))
-SENT = len(PAIRS) * ROWS + PIECES * EDGE
+SHARED = len(PAIRS) * ROWS
 LANES = 128
 SMOOTH = 2.0
 DAMPING = 0.1
@@ -87,51 +87,36 @@
     return lax.rem(lax.axis_index(axis), 2) == 0
 
 
-def pack_rows(views, send_pair, send_next, local, sems):
-    order = (4, 3, 0, 2, 1, -4, -3, -2, -1)
-    copies = {}
-    for s in order:
-        span = pl.ds((s + HALF) * ANG, ANG)
-        copies[s] = pltpu.make_async_copy(
-            views.at[span], local.at[span], sems.at[s + HALF]
-        )
-        copies[s].start()
+def pack_rows(views, send_pair, send_next, ups_out, downs_out):
     even = is_even("row")
     index = lax.broadcasted_iota(jnp.int32, (EDGE, COLS), 0)
 
     def put(ups, q, ti, rows):
-        rows = rows.astype(jnp.bfloat16)
-
-        @pl.when(even == ups)
-        def _():
-            send_next[q * ANG + ti] = rows
-
-        @pl.when(even != ups)
-        def _():
-            send_pair[q * ANG + ti] = rows
-
-    for s in order:
-        copies[s].wait()
-        if s in (3, 2, -4):
-            continue
-        for ti in range(ANG):
-
-            def rows_of(s, start):
-                return local[(s + HALF) * ANG + ti, pl.ds(start, EDGE), :].astype(F32)
-
-            first = functools.partial(rows_of, start=0)
-            last = functools.partial(rows_of, start=ROWS - EDGE)
-            if s == 4:
-                put(True, 0, ti, first(4))
-            elif s == 0:
-                put(True, 1, ti, jnp.where(index < 12, first(3), pltpu.roll(first(0), 12, 0)))
-            elif s == 1:
-                put(True, 2, ti, jnp.where(index < 9, first(2), pltpu.roll(first(1), 9, 0)))
-            elif s == -3:
-                put(False, 0, ti, last(-4))
-                put(False, 1, ti, jnp.where(index < 4, pltpu.roll(last(0), 4, 0), last(-3)))
-            elif s == -1:
-                put(False, 2, ti, jnp.where(index < 7, pltpu.roll(last(-1), 7, 0), last(-2)))
+        (ups_out if ups else downs_out)[q * ANG + ti] = rows.astype(jnp.bfloat16)
+
+    for ti in range(ANG):
+
+        def rows_of(s, start, ti=ti):
+            return views[(s + HALF) * ANG + ti, pl.ds(start, EDGE), :].astype(F32)
+
+        first = functools.partial(rows_of, start=0)
+        last = functools.partial(rows_of, start=ROWS - EDGE)
+        put(True, 0, ti, first(4))
+        put(True, 1, ti, jnp.where(index < 12, first(3), pltpu.roll(first(0), 12, 0)))
+        put(True, 2, ti, jnp.where(index < 9, first(2), pltpu.roll(first(1), 9, 0)))
+        put(False, 0, ti, last(-4))
+        put(False, 1, ti, jnp.where(index < 4, pltpu.roll(last(0), 4, 0), last(-3)))
+        put(False, 2, ti, jnp.where(index < 7, pltpu.roll(last(-1), 7, 0), last(-2)))
+
+    @pl.when(even)
+    def _():
+        send_pair[...] = downs_out[...]
+        send_next[...] = ups_out[...]
+
+    @pl.when(jnp.logical_not(even))
+    def _():
+        send_pair[...] = ups_out[...]
+        send_next[...] = downs_out[...]
 
 
 PLACES = {
@@ -160,7 +145,21 @@
     )
 
 
-def pack_own(views, own, to_left, to_right, pack):
+def by_pair(to_left, to_right, send_pair, send_next):
+    even = is_even("col")
+
+    @pl.when(even)
+    def _():
+        send_pair[...] = to_right[...]
+        send_next[...] = to_left[...]
+
+    @pl.when(jnp.logical_not(even))
+    def _():
+        send_pair[...] = to_left[...]
+        send_next[...] = to_right[...]
+
+
+def pack_own(views, own, send_pair, send_next, pack, to_left, to_right):
     column = lax.broadcasted_iota(jnp.int32, (COLS, LANES), 0)
     lane = lax.broadcasted_iota(jnp.int32, (COLS, LANES), 1)
     for t in range(-HALF, HALF + 1):
@@ -182,11 +181,12 @@
             own[(s + HALF) * ROWS : (s + HALF + 1) * ROWS, :] = total.astype(jnp.bfloat16)
             both.append(total)
         share(both[0], both[1], to_left, to_right, p * ROWS)
+    by_pair(to_left, to_right, send_pair, send_next)
 
 
 def pack_edges(
-    got_pair, got_next, pack, own_in, left_in, right_in,
-    above, below, own, send_pair, send_next, to_left, to_right,
+    got_pair, got_next, pack, own_in, above, below, own, send_pair, send_next,
+    to_left, to_right,
 ):
     even = is_even("row")
 
@@ -210,26 +210,11 @@
             own[pl.ds(packed_piece(side, q), EDGE), :] = total.astype(jnp.bfloat16)
             both.append(total)
         share(both[0], both[1], to_left, to_right, q * EDGE)
-    rows = len(PAIRS) * ROWS
-    even = is_even("col")
-
-    def send(out, block, piece):
-        out[:rows, :] = block[...]
-        out[rows:, :] = piece[...]
-
-    @pl.when(even)
-    def _():
-        send(send_pair, right_in, to_right)
-        send(send_next, left_in, to_left)
-
-    @pl.when(jnp.logical_not(even))
-    def _():
-        send(send_pair, left_in, to_left)
-        send(send_next, right_in, to_right)
-
-
-def unshare(source, high, out):
-    def move(at, to, count, half):
+    by_pair(to_left, to_right, send_pair, send_next)
+
+
+def unshare(blocks, pieces, high, out):
+    def move(source, at, to, count, half):
         rows = source[pl.ds(at, count), :]
         if half != high:
             rows = pltpu.roll(rows.astype(F32), 64, 1).astype(jnp.bfloat16)
@@ -238,10 +223,10 @@
     for p, pair in enumerate(PAIRS):
         for half, s in enumerate(pair):
             if s or not half:
-                move(p * ROWS, (s + HALF) * ROWS, ROWS, half)
+                move(blocks, p * ROWS, (s + HALF) * ROWS, ROWS, half)
     for q in range(PIECES):
         for half, side in enumerate(("above", "below")):
-            move(len(PAIRS) * ROWS + q * EDGE, packed_piece(side, q), EDGE, half)
+            move(pieces, q * EDGE, packed_piece(side, q), EDGE, half)
 
 
 def first_row(s):
@@ -346,6 +331,8 @@
     own,
     got_pair,
     got_next,
+    got_piece_pair,
+    got_piece_next,
     data_in,
     source_in,
     outer,
@@ -369,13 +356,13 @@
 
     @pl.when(even)
     def _():
-        unshare(got_next, 1, left)
-        unshare(got_pair, 0, right)
+        unshare(got_next, got_piece_next, 1, left)
+        unshare(got_pair, got_piece_pair, 0, right)
 
     @pl.when(jnp.logical_not(even))
     def _():
-        unshare(got_pair, 1, left)
-        unshare(got_next, 0, right)
+        unshare(got_pair, got_piece_pair, 1, left)
+        unshare(got_next, got_piece_next, 0, right)
 
     edges = {"above": above, "below": below}
     zero_tails(warped)
@@ -547,14 +534,13 @@
     )
 
 
-def call(kernel, outs, scratch=(), name=None, **more):
+def call(kernel, outs, scratch=(), name=None):
     return pl.pallas_call(
         kernel,
         out_shape=outs,
         scratch_shapes=list(scratch),
         compiler_params=pltpu.CompilerParams(vmem_limit_bytes=24 * 1024 * 1024),
         name=name,
-        **more,
     )
 
 
@@ -572,31 +558,30 @@
     struct = jax.ShapeDtypeStruct
 
     edge = struct((PIECES * ANG, EDGE, COLS), bf16)
-    pair, after, views = call(
-        pack_rows,
-        (edge, edge, struct(views.shape, bf16)),
-        (pltpu.SemaphoreType.DMA((ANG,)),),
-        name="pack_rows",
-        in_specs=[pl.BlockSpec(memory_space=pltpu.HBM)],
-    )(views)
+    room = pltpu.VMEM(edge.shape, bf16)
+    pair, after = call(pack_rows, (edge, edge), (room, room), name="pack_rows")(views)
     pair = swap(pair, "row", 0)
     after = swap(after, "row", 1)
-    shared = struct((len(PAIRS) * ROWS, LANES), bf16)
-    own, to_left, to_right, pack = call(
+    shared = struct((SHARED, LANES), bf16)
+    room = pltpu.VMEM((SHARED, LANES), bf16)
+    own, block_pair, block_next, pack = call(
         pack_own,
         (struct((ANG * ROWS, LANES), bf16), shared, shared, struct((ANG, COLS, LANES), bf16)),
+        (room, room),
         name="pack_own",
     )(views)
-    sent = struct((SENT, LANES), bf16)
+    block_next = swap(block_next, "col", 1)
+    block_pair = swap(block_pair, "col", 0)
+    sent = struct((PIECES * EDGE, LANES), bf16)
     small = pltpu.VMEM((PIECES * EDGE, LANES), bf16)
-    above, below, own, pair, after = call(
+    above, below, own, piece_pair, piece_next = call(
         pack_edges,
         (edge, edge, struct((PACKED, LANES), bf16), sent, sent),
         (small, small),
         name="pack_edges",
-    )(pair, after, pack, own, to_left, to_right)
-    pair = swap(pair, "col", 0)
-    after = swap(after, "col", 1)
+    )(pair, after, pack, own)
+    piece_next = swap(piece_next, "col", 1)
+    piece_pair = swap(piece_pair, "col", 0)
     slab = pltpu.VMEM((ANG, SLAB, LANES), F32)
     tile = pltpu.VMEM((OUT, LANES), F32)
     sums = struct((2, OUT, LANES), F32)
@@ -619,7 +604,10 @@
             pltpu.VMEM((PACKED, LANES), bf16),
         ),
         name="outer_sums",
-    )(views, above, below, own, pair, after, data, source, outer, ghost, center)
+    )(
+        views, above, below, own, block_pair, block_next, piece_pair, piece_next,
+        data, source, outer, ghost, center,
+    )
     n = rows * cols
     messages = lax.all_to_all(
         jnp.broadcast_to(message[None], (n, 1, LANES)), ALL, 0, 0, tiled=True

time: 62.4 us -> 60.7 us (0.973)
  waiting for transfers between devices: 6.06 us -> 3.9 us
  starting transfers between devices: 5.94 us -> 7.98 us
  Pallas kernels: 14 us -> 13.1 us
  blocking collectives: 33.6 us -> 32.9 us
    ppermute x4 -> x6, waiting for transfers between devices: 6.06 us -> 3.9 us  [swap(): return lax.ppermute(array, axis, pairs)]
    ppermute x4 -> x6, starting transfers between devices: 5.94 us -> 7.98 us  [swap(): return lax.ppermute(array, axis, pairs)]
    pallas_call x1, Pallas kernels: 0.99 us -> 0.11 us  [shards(): call(pack_rows, (edge, edge), (room, room), name='pack_rows')(views)]
    all_to_all x1, blocking collectives: 33.6 us -> 32.9 us  [shards(): lax.all_to_all(jnp.broadcast_to(message[None], (n, 1, LANES)), ALL, 0, 0,...]
    unnamed x10 -> x12, local copies, waits for them, and re-layouts: 1.76 us -> 1.76 us
  transfers between devices with their start and end apart: 4 -> 6, of which waited for: 1 -> 1; matrix products, arithmetic and copies ran while one was open for 0% -> 0% of each run, Pallas kernels for 9% -> 10%
where the time goes in v3:
time: 60.7 us; the launch traced here: 60.5 us
  blocking collectives  32.9 us (54%)
  Pallas kernels  13.1 us (22%)
  starting transfers between devices  7.98 us (13%)
  waiting for transfers between devices  3.9 us (6%)
  local copies, waits for them, and re-layouts  1.83 us (3%)
  between operations  0.79 us (1%)
    all_to_all x1, blocking collectives, shards(): lax.all_to_all(jnp.broadcast_to(message[None], (n, 1, LANES)), ALL, 0, 0,...  32.9 us
    ppermute x6, starting transfers between devices, swap(): return lax.ppermute(array, axis, pairs)  7.98 us
    pallas_call x1, Pallas kernels, shards(): call(functools.partial(outer_sums, rows * ROWS, cols * COLS), (field, fie...  5.61 us
    pallas_call x1, Pallas kernels, shards(): call(inner_sums, (sums, sums), (slab, slab, tile), name='inner_sums')  4.25 us
    ppermute x6, waiting for transfers between devices, swap(): return lax.ppermute(array, axis, pairs)  3.9 us
    unnamed x12, local copies, waits for them, and re-layouts  1.76 us
    pallas_call x1, Pallas kernels, shards(): call(pack_own, (struct((ANG * ROWS, LANES), bf16), shared, shared, struct...  1.33 us
  transfers between devices with their start and end apart: 6, of which 1 were waited for; matrix products, arithmetic and copies ran while one was open for 0% of the time, Pallas kernels for 10%

profile of v3, /device:TPU:1, one launch (start us, length us, event | category | flops | bytes accessed | tf_op | source)
XLA Modules:
  0.0 60.5 jit_solution(11163373210613809145)
XLA Ops:
  0.6 0.0 copy-start
  0.6 1.7 %copy-done = bf16[81,64,256]{2,1,0:T(8,128)(2,1)S(1)} copy-done((bf16[81,64,256]{2,1,0:T(8,128)(2,1)S(1)}, bf16[81,64,256]{2,1,0:T(8,128)(2,1)}, u32[]{:S(2)}) %copy-start) | copy-done | bytes 2654232
  2.4 0.0 copy-start.1
  2.4 0.0 copy-start.3
  2.4 0.1 pack_rows.1
  2.5 3.3 %collective-permute-start = (bf16[27,16,256]{2,1,0:T(8,128)(2,1)S(1)}, bf16[27,16,256]{2,1,0:T(8,128)(2,1)S(1)}, u32[]{:S(2)}, u32[]{:S(2)}) collective-permute-start(bf16[27,16,256]{2,1,0:T(8,128)(2,1)S(1)} %get-tuple-element.20), channel_id=1, source_target_pairs={{0,8},{8,0},{16,24},{24,16},{32,40},{40,32},{48,56},{56,48},{64,72... | collective-permute-start | bytes 663560 | tf_op jit(solution)/shard_map/ppermute | solution.py:551
  5.8 2.0 %collective-permute-start.1 = (bf16[27,16,256]{2,1,0:T(8,128)(2,1)S(1)}, bf16[27,16,256]{2,1,0:T(8,128)(2,1)S(1)}, u32[]{:S(2)}, u32[]{:S(2)}) collective-permute-start(bf16[27,16,256]{2,1,0:T(8,128)(2,1)S(1)} %get-tuple-element.21), channel_id=1, source_target_pairs={{8,16},{16,8},{24,32},{32,24},{40,48},{48,40},{56,64},{64,56},{72,... | collective-permute-start | bytes 663560 | tf_op jit(solution)/shard_map/ppermute | solution.py:551
  7.8 1.3 %pack_own.1 = (bf16[576,128]{1,0:T(8,128)(2,1)S(1)}, bf16[320,128]{1,0:T(8,128)(2,1)S(1)}, bf16[320,128]{1,0:T(8,128)(2,1)S(1)}, bf16[9,256,128]{2,1,0:T(8,128)(2,1)S(1)}) custom-call(bf16[81,64,256]{2,1,0:T(8,128)(2,1)S(1)} %copy-done), custom_call_target="tpu_custom_call" | custom-call | tf_op jit(solution)/shard_map/pack_own/pallas_call | solution.py:567
  9.1 1.3 %collective-permute-start.2 = (bf16[320,128]{1,0:T(8,128)(2,1)S(1)}, bf16[320,128]{1,0:T(8,128)(2,1)S(1)}, u32[]{:S(2)}, u32[]{:S(2)}) collective-permute-start(bf16[320,128]{1,0:T(8,128)(2,1)S(1)} %get-tuple-element.27), channel_id=1, source_target_pairs={{0,1},{1,0},{2,3},{3,2},{4,5},{5,4},{6,7},{7,6},{8,9},{9,8},{10,11... | collective-permute-start | bytes 245768 | tf_op jit(solution)/shard_map/ppermute | solution.py:551
  10.5 0.7 %collective-permute-start.3 = (bf16[320,128]{1,0:T(8,128)(2,1)S(1)}, bf16[320,128]{1,0:T(8,128)(2,1)S(1)}, u32[]{:S(2)}, u32[]{:S(2)}) collective-permute-start(bf16[320,128]{1,0:T(8,128)(2,1)S(1)} %get-tuple-element.28), channel_id=1, source_target_pairs={{1,2},{2,1},{3,4},{4,3},{5,6},{6,5},{9,10},{10,9},{11,12},{12,11},... | collective-permute-start | bytes 245768 | tf_op jit(solution)/shard_map/ppermute | solution.py:551
  11.1 0.0 collective-permute-done.got_pair
  11.1 3.9 %collective-permute-done.1.got_next = bf16[27,16,256]{2,1,0:T(8,128)(2,1)S(1)} collective-permute-done((bf16[27,16,256]{2,1,0:T(8,128)(2,1)S(1)}, bf16[27,16,256]{2,1,0:T(8,128)(2,1)S(1)}, u32[]{:S(2)}, u32[]{:S(2)}) %collective-permute-start.1) | collective-permute-done | bytes 221216 | tf_op jit(solution)/shard_map/ppermute | solution.py:551
  15.0 0.0 copy-start.2
  15.0 0.0 copy-start.4
  15.0 0.0 copy-start.5
  15.0 0.7 %pack_edges.1 = (bf16[27,16,256]{2,1,0:T(8,128)(2,1)S(1)}, bf16[27,16,256]{2,1,0:T(8,128)(2,1)S(1)}, bf16[672,128]{1,0:T(8,128)(2,1)S(1)}, bf16[48,128]{1,0:T(8,128)(2,1)S(1)}, bf16[48,128]{1,0:T(8,128)(2,1)S(1)}) custom-call(bf16[27,16,256]{2,1,0:T(8,128)(2,1)S(1)} %collective-permute-done.got_pair, ...), custom_call_target="tpu_custom_call" | custom-call | tf_op jit(solution)/shard_map/pack_edges/pallas_call | solution.py:577
  15.7 0.0 collective-permute-start.4
  15.8 0.7 %collective-permute-start.5 = (bf16[48,128]{1,0:T(8,128)(2,1)S(1)}, bf16[48,128]{1,0:T(8,128)(2,1)S(1)}, u32[]{:S(2)}, u32[]{:S(2)}) collective-permute-start(bf16[48,128]{1,0:T(8,128)(2,1)S(1)} %get-tuple-element.30), channel_id=1, source_target_pairs={{1,2},{2,1},{3,4},{4,3},{5,6},{6,5},{9,10},{10,9},{11,12},{12,11},... | collective-permute-start | bytes 36872 | tf_op jit(solution)/shard_map/ppermute | solution.py:551
  16.4 0.0 copy-done.1
  16.5 0.0 copy-done.3
  16.5 4.2 %inner_sums.1 = (f32[2,72,128]{2,1,0:T(8,128)S(1)}, f32[2,72,128]{2,1,0:T(8,128)S(1)}) custom-call(bf16[81,64,256]{2,1,0:T(8,128)(2,1)S(1)} %copy-done.1, bf16[27,16,256]{2,1,0:T(8,128)(2,1)S(1)} %get-tuple-element.24.above, bf16[27,16,256]{2,1,0:T(8,128)(2,1)S(1)} %get-tuple-element.25.below, bf16[2,4,256,256]{3,2,1,0:T(8,128)(2,1)S(1)} %copy-done.3), custom_call_target="tpu_custom_call" | custom-call | tf_op jit(solution)/shard_map/inner_sums/pallas_call | solution.py:588
  20.7 0.0 collective-permute-done.2.got_pair
  20.7 0.0 collective-permute-done.3.got_next
  20.7 0.0 collective-permute-done.4.got_piece_pair
  20.8 0.0 collective-permute-done.5.got_piece_next
  20.8 0.0 copy-done.2
  20.8 0.0 copy-done.4
  20.8 0.0 copy-done.5
  20.8 5.6 %outer_sums.1 = (f32[72,256]{1,0:T(8,128)S(1)}, f32[72,256]{1,0:T(8,128)S(1)}, f32[72,256]{1,0:T(8,128)S(1)}, f32[72,256]{1,0:T(8,128)S(1)}, f32[1,128]{1,0:T(1,128)S(1)}) custom-call(bf16[81,64,256]{2,1,0:T(8,128)(2,1)S(1)} %copy-done.1, bf16[27,16,256]{2,1,0:T(8,128)(2,1)S(1)} %get-tuple-element.24.above, ...), custom_call_target="tpu_custom_call" | custom-call | tf_op jit(solution)/shard_map/outer_sums/pallas_call | solution.py:593
  26.4 0.1 broadcast_in_dim.9
  26.5 32.9 %all_to_all.5 = f32[256,1,128]{2,1,0:T(1,128)S(1)} all-to-all(f32[256,1,128]{2,1,0:T(1,128)S(1)} %broadcast_in_dim.9), channel_id=1, replica_groups=mesh['row'=32,'col'=8] {'row','col'}, dimensions={0} | all-to-all | bytes 262144 | tf_op jit(solution)/shard_map/all_to_all | solution.py:612
  59.3 1.1 %finish.1 = (f32[64,256]{1,0:T(8,128)}, f32[64,256]{1,0:T(8,128)}) custom-call(f32[256,128]{1,0:T(8,128)S(1)} %bitcast.2, f32[72,256]{1,0:T(8,128)S(1)} %get-tuple-element.34.zed_ref, f32[72,256]{1,0:T(8,128)S(1)} %get-tuple-element.35.near_ref, f32[72,256]{1,0:T(8,128)S(1)} %get-tuple-element.36.next_ref, f32[72,256]{1,0:T(8,128)S(1)} %get-tuple-element.37.precond_ref), custom_call_target="tpu_custom_call" | custom-call | tf_op jit(solution)/shard_map/finish/pallas_call | solution.py:616
Async XLA Ops:
  0.6 1.8 %copy-start = (bf16[81,64,256]{2,1,0:T(8,128)(2,1)S(1)}, bf16[81,64,256]{2,1,0:T(8,128)(2,1)}, u32[]{:S(2)}) copy-start(bf16[81,64,256]{2,1,0:T(8,128)(2,1)} %views.7) | copy-start | bytes 7962628
  2.4 14.1 %copy-start.1 = (bf16[81,64,256]{2,1,0:T(8,128)(2,1)S(1)}, bf16[81,64,256]{2,1,0:T(8,128)(2,1)}, u32[]{:S(2)}) copy-start(bf16[81,64,256]{2,1,0:T(8,128)(2,1)} %views.7) | copy-start | bytes 7962628
  2.4 14.1 %copy-start.3 = (bf16[2,4,256,256]{3,2,1,0:T(8,128)(2,1)S(1)}, bf16[2,4,256,256]{3,2,1,0:T(8,128)(2,1)}, u32[]{:S(2)}) copy-start(bf16[2,4,256,256]{3,2,1,0:T(8,128)(2,1)} %constant.8.clone.inner) | copy-start | bytes 3145732
  2.5 8.6 %collective-permute-start = (bf16[27,16,256]{2,1,0:T(8,128)(2,1)S(1)}, bf16[27,16,256]{2,1,0:T(8,128)(2,1)S(1)}, u32[]{:S(2)}, u32[]{:S(2)}) collective-permute-start(bf16[27,16,256]{2,1,0:T(8,128)(2,1)S(1)} %get-tuple-element.20), channel_id=1, source_target_pairs={{0,8},{8,0},{16,24},{24,16},{32,40},{40,32},{48,56},{56,48},{64,72... | collective-permute-start | bytes 663560 | tf_op jit(solution)/shard_map/ppermute | solution.py:551
  5.8 9.2 %collective-permute-start.1 = (bf16[27,16,256]{2,1,0:T(8,128)(2,1)S(1)}, bf16[27,16,256]{2,1,0:T(8,128)(2,1)S(1)}, u32[]{:S(2)}, u32[]{:S(2)}) collective-permute-start(bf16[27,16,256]{2,1,0:T(8,128)(2,1)S(1)} %get-tuple-element.21), channel_id=1, source_target_pairs={{8,16},{16,8},{24,32},{32,24},{40,48},{48,40},{56,64},{64,56},{72,... | collective-permute-start | bytes 663560 | tf_op jit(solution)/shard_map/ppermute | solution.py:551
  9.1 11.6 %collective-permute-start.2 = (bf16[320,128]{1,0:T(8,128)(2,1)S(1)}, bf16[320,128]{1,0:T(8,128)(2,1)S(1)}, u32[]{:S(2)}, u32[]{:S(2)}) collective-permute-start(bf16[320,128]{1,0:T(8,128)(2,1)S(1)} %get-tuple-element.27), channel_id=1, source_target_pairs={{0,1},{1,0},{2,3},{3,2},{4,5},{5,4},{6,7},{7,6},{8,9},{9,8},{10,11... | collective-permute-start | bytes 245768 | tf_op jit(solution)/shard_map/ppermute | solution.py:551
  10.5 10.3 %collective-permute-start.3 = (bf16[320,128]{1,0:T(8,128)(2,1)S(1)}, bf16[320,128]{1,0:T(8,128)(2,1)S(1)}, u32[]{:S(2)}, u32[]{:S(2)}) collective-permute-start(bf16[320,128]{1,0:T(8,128)(2,1)S(1)} %get-tuple-element.28), channel_id=1, source_target_pairs={{1,2},{2,1},{3,4},{4,3},{5,6},{6,5},{9,10},{10,9},{11,12},{12,11},... | collective-permute-start | bytes 245768 | tf_op jit(solution)/shard_map/ppermute | solution.py:551
  15.0 5.7 %copy-start.2 = (bf16[2,4,256,256]{3,2,1,0:T(8,128)(2,1)S(1)}, bf16[2,4,256,256]{3,2,1,0:T(8,128)(2,1)}, u32[]{:S(2)}) copy-start(bf16[2,4,256,256]{3,2,1,0:T(8,128)(2,1)} %constant.9.clone.outer) | copy-start | bytes 3145732
  15.0 5.8 %copy-start.4 = (bf16[384,256]{1,0:T(8,128)(2,1)S(1)}, bf16[384,256]{1,0:T(8,128)(2,1)}, u32[]{:S(2)}) copy-start(bf16[384,256]{1,0:T(8,128)(2,1)} %constant.11.clone.ghost_center) | copy-start | bytes 589828
  15.0 5.8 %copy-start.5 = (bf16[384,256]{1,0:T(8,128)(2,1)S(1)}, bf16[384,256]{1,0:T(8,128)(2,1)}, u32[]{:S(2)}) copy-start(bf16[384,256]{1,0:T(8,128)(2,1)} %constant.10.clone.ghost) | copy-start | bytes 589828
  15.7 5.0 %collective-permute-start.4 = (bf16[48,128]{1,0:T(8,128)(2,1)S(1)}, bf16[48,128]{1,0:T(8,128)(2,1)S(1)}, u32[]{:S(2)}, u32[]{:S(2)}) collective-permute-start(bf16[48,128]{1,0:T(8,128)(2,1)S(1)} %get-tuple-element.29), channel_id=1, source_target_pairs={{0,1},{1,0},{2,3},{3,2},{4,5},{5,4},{6,7},{7,6},{8,9},{9,8},{10,11... | collective-permute-start | bytes 36872 | tf_op jit(solution)/shard_map/ppermute | solution.py:551
  15.8 5.0 %collective-permute-start.5 = (bf16[48,128]{1,0:T(8,128)(2,1)S(1)}, bf16[48,128]{1,0:T(8,128)(2,1)S(1)}, u32[]{:S(2)}, u32[]{:S(2)}) collective-permute-start(bf16[48,128]{1,0:T(8,128)(2,1)S(1)} %get-tuple-element.30), channel_id=1, source_target_pairs={{1,2},{2,1},{3,4},{4,3},{5,6},{6,5},{9,10},{10,9},{11,12},{12,11},... | collective-permute-start | bytes 36872 | tf_op jit(solution)/shard_map/ppermute | solution.py:551

commit v4 on v2

--- a/solution.py
+++ b/solution.py
@@ -38,45 +38,62 @@
     return 64 + D0 * a * (a + 1) // 2 + c - (COLS - D0 * a - D0)
 
 
-def ghost_source(t, c):
+def lane_here(t, c):
+    return 45 + 2 * (-t - 1) + c if t < 0 else 109 + 2 * (t - 1) + c - (COLS - 2)
+
+
+def edge_source(t, c):
     if c < 0:
         return lane_last(t, COLS + c)
     if c >= COLS:
         return 2 * LANES + lane_first(t, c - COLS)
     if t >= 0 and c <= D0 * t + D0 - 1:
         return LANES + lane_first(t, c)
-    return LANES + lane_last(t, c)
+    if t <= 0 and c >= COLS - D0 * abs(t) - D0:
+        return LANES + lane_last(t, c)
+    return LANES + lane_here(t, c)
+
+
+def edge_pixels():
+    for t in range(-HALF, HALF + 1):
+        for column in range(-2, D0 * -t + 1 if t < 0 else 0):
+            yield t, column
+        for column in range(COLS - 1 - D0 * t if t > 0 else COLS, COLS + 2):
+            yield t, column
 
 
 def tables():
-    inner = np.zeros((2, HALF, COLS, 2 * LANES), np.float32)
-    outer = np.zeros((2, HALF, COLS, 2 * LANES), np.float32)
-    for a in range(1, HALF + 1):
-        for sign in (0, 1):
-            t = a if sign else -a
-            for j in range(LANES):
-                for shift, out, value in ((0, 0, 1), (1, LANES, t), (-1, LANES, -t)):
-                    c = j + D0 * t + shift
-                    inner[sign, a - 1, c if sign else c + LANES, j + out] += value
-                    if sign:
-                        k = c if c < LANES else LANES + lane_first(t, c - LANES)
-                    else:
-                        k = LANES + c if c >= 0 else lane_last(t, COLS + c)
-                    outer[sign, a - 1, k, j + out] += value
-    ghost = np.zeros((3 * LANES, 2 * LANES), np.float32)
-    center = np.zeros((3 * LANES, 2 * LANES), np.float32)
-    for t in range(-HALF, HALF + 1):
-        for g, col in enumerate((-2, -1, COLS, COLS + 1)):
-            lane = (4 * (t + HALF) + g - 2) % LANES
-            c = col + D0 * t
-            ghost[ghost_source(t, c), lane] += 1
-            if t:
-                ghost[ghost_source(t, c + 1), LANES + lane] += t
-                ghost[ghost_source(t, c - 1), LANES + lane] -= t
-            center[ghost_source(0, col), lane] = 1
+    inner = np.zeros((2, 2, HALF, COLS, 2 * LANES), np.float32)
+    for tile in (0, 1):
+        for a in range(1, HALF + 1):
+            for sign in (0, 1):
+                t = a if sign else -a
+                for j in range(LANES):
+                    c = tile * LANES + j + D0 * t
+                    if 1 <= c < COLS - 1:
+                        inner[tile, sign, a - 1, c, j] += 1
+                        inner[tile, sign, a - 1, c + 1, LANES + j] += t
+                        inner[tile, sign, a - 1, c - 1, LANES + j] -= t
+    edge = np.zeros((3 * LANES, 2 * LANES), np.float32)
+    center = np.zeros((LANES + COLS + LANES, 2 * LANES), np.float32)
+    scatter = np.zeros((LANES, 3 * LANES), np.float32)
+
+    def center_source(c):
+        if c < 0:
+            return lane_last(0, COLS + c)
+        return LANES + c if c < COLS else LANES + COLS + lane_first(0, c - COLS)
+
+    for lane, (t, col) in enumerate(edge_pixels()):
+        c = col + D0 * t
+        edge[edge_source(t, c), lane] += 1
+        if t:
+            edge[edge_source(t, c + 1), LANES + lane] += t
+            edge[edge_source(t, c - 1), LANES + lane] -= t
+        center[center_source(col), lane] = 1
+        scatter[lane, col % (3 * LANES)] = 1
     for col in (-3, -2, -1, COLS, COLS + 1, COLS + 2):
-        center[ghost_source(0, col), LANES + (col % (3 * LANES)) % LANES] = 1
-    return tuple(x.astype(ml_dtypes.bfloat16) for x in (inner, outer, ghost, center))
+        center[center_source(col), LANES + col % LANES] = 1
+    return tuple(x.astype(ml_dtypes.bfloat16) for x in (inner, edge, center, scatter))
 
 
 def dot(a, b):
@@ -87,51 +104,50 @@
     return lax.rem(lax.axis_index(axis), 2) == 0
 
 
-def pack_rows(views, send_pair, send_next, local, sems):
-    order = (4, 3, 0, 2, 1, -4, -3, -2, -1)
-    copies = {}
-    for s in order:
-        span = pl.ds((s + HALF) * ANG, ANG)
-        copies[s] = pltpu.make_async_copy(
-            views.at[span], local.at[span], sems.at[s + HALF]
-        )
-        copies[s].start()
+def pack_rows(views, send_pair, send_next, tops, bottoms, ups, downs, sems):
+    count = (HALF + 1) * ANG
+    get_tops = pltpu.make_async_copy(
+        views.at[pl.ds(HALF * ANG, count), pl.ds(0, EDGE)], tops, sems.at[0]
+    )
+    get_bottoms = pltpu.make_async_copy(
+        views.at[pl.ds(0, count), pl.ds(ROWS - EDGE, EDGE)], bottoms, sems.at[1]
+    )
+    get_tops.start()
+    get_bottoms.start()
+    index = lax.broadcasted_iota(jnp.int32, (EDGE, COLS), 0)
+
+    def put(out, q, ti, rows):
+        out[q * ANG + ti] = rows.astype(jnp.bfloat16)
+
+    get_tops.wait()
+    for ti in range(ANG):
+
+        def first(s, ti=ti):
+            return tops[s * ANG + ti].astype(F32)
+
+        put(ups, 0, ti, first(4))
+        put(ups, 1, ti, jnp.where(index < 12, first(3), pltpu.roll(first(0), 12, 0)))
+        put(ups, 2, ti, jnp.where(index < 9, first(2), pltpu.roll(first(1), 9, 0)))
+    get_bottoms.wait()
+    for ti in range(ANG):
+
+        def last(s, ti=ti):
+            return bottoms[(s + HALF) * ANG + ti].astype(F32)
+
+        put(downs, 0, ti, last(-4))
+        put(downs, 1, ti, jnp.where(index < 4, pltpu.roll(last(0), 4, 0), last(-3)))
+        put(downs, 2, ti, jnp.where(index < 7, pltpu.roll(last(-1), 7, 0), last(-2)))
     even = is_even("row")
-    index = lax.broadcasted_iota(jnp.int32, (EDGE, COLS), 0)
-
-    def put(ups, q, ti, rows):
-        rows = rows.astype(jnp.bfloat16)
-
-        @pl.when(even == ups)
-        def _():
-            send_next[q * ANG + ti] = rows
-
-        @pl.when(even != ups)
-        def _():
-            send_pair[q * ANG + ti] = rows
-
-    for s in order:
-        copies[s].wait()
-        if s in (3, 2, -4):
-            continue
-        for ti in range(ANG):
-
-            def rows_of(s, start):
-                return local[(s + HALF) * ANG + ti, pl.ds(start, EDGE), :].astype(F32)
-
-            first = functools.partial(rows_of, start=0)
-            last = functools.partial(rows_of, start=ROWS - EDGE)
-            if s == 4:
-                put(True, 0, ti, first(4))
-            elif s == 0:
-                put(True, 1, ti, jnp.where(index < 12, first(3), pltpu.roll(first(0), 12, 0)))
-            elif s == 1:
-                put(True, 2, ti, jnp.where(index < 9, first(2), pltpu.roll(first(1), 9, 0)))
-            elif s == -3:
-                put(False, 0, ti, last(-4))
-                put(False, 1, ti, jnp.where(index < 4, pltpu.roll(last(0), 4, 0), last(-3)))
-            elif s == -1:
-                put(False, 2, ti, jnp.where(index < 7, pltpu.roll(last(-1), 7, 0), last(-2)))
+
+    @pl.when(even)
+    def _():
+        send_pair[...] = downs[...]
+        send_next[...] = ups[...]
+
+    @pl.when(jnp.logical_not(even))
+    def _():
+        send_pair[...] = ups[...]
+        send_next[...] = downs[...]
 
 
 PLACES = {
@@ -172,6 +188,10 @@
             start = COLS - D0 * abs(t) - D0
             apart = lane_last(t, start) - start
             hit = jnp.where((column >= start) & (lane - column == apart), 1.0, hit)
+        if t:
+            near = column < 2 if t < 0 else column >= COLS - 2
+            apart = lane_here(t, 0)
+            hit = jnp.where(near & (lane - column == apart), 1.0, hit)
         pack[t + HALF] = hit.astype(jnp.bfloat16)
     for p, pair in enumerate(PAIRS):
         both = []
@@ -316,12 +336,11 @@
             data, source = accumulate(s, w, None, center_ref[...], data, source)
         data_out[tile] = data
         source_out[tile] = source
-        sign = 1 - tile
-
-        def body(a, carry, tile=tile, sign=sign):
+
+        def body(a, carry, sign, tile=tile):
             ti = HALF + 1 + a if sign else HALF - 1 - a
             data, source = shifted_views(
-                inner[sign, a],
+                inner[tile, sign, a],
                 lambda s: views[(s + HALF) * ANG + ti],
                 lambda name, q: edges[name][q * ANG + ti],
                 center_ref[...],
@@ -334,7 +353,8 @@
             source_out[tile] += source
             return carry
 
-        lax.fori_loop(0, HALF, body, 0)
+        for sign in (0, 1):
+            lax.fori_loop(0, HALF, functools.partial(body, sign=sign), 0)
 
 
 def outer_sums(
@@ -348,16 +368,14 @@
     got_next,
     data_in,
     source_in,
-    outer,
-    ghost,
-    ghost_center,
+    edge,
+    edge_center,
+    scatter,
     zed_out,
     near_out,
     next_out,
     precond_out,
     message,
-    data_acc,
-    source_acc,
     warped,
     side,
     center_ref,
@@ -382,68 +400,43 @@
     zero_tails(side)
     zero = jnp.zeros((OUT, LANES), F32)
 
-    def ghost_rows(row, count):
+    def edge_rows(row, count):
         return jnp.concatenate([x[pl.ds(row, count), :] for x in (left, own, right)], axis=1)
 
     def fill_center(at, ref, row, count):
         fill(center_slab.at[0], at, ref[:, :LANES].astype(F32))
         fill(center_slab.at[1], at, ref[:, LANES:].astype(F32))
-        both = dot(ghost_rows(row, count), ghost_center[...])
+        around = (left[pl.ds(row, count), :], ref[...], right[pl.ds(row, count), :])
+        both = dot(jnp.concatenate(around, axis=1), edge_center[...])
         fill(warped.at[HALF], at, both[:, :LANES])
         fill(center_slab.at[2], at, both[:, LANES:])
 
     for name in ("above", "below"):
-        fill_center(PLACES[name, 1][1][1], edges[name][ANG + HALF], packed_piece(name, 1), EDGE)
-    fill_center(EDGE, views[HALF * ANG + HALF], HALF * ROWS, ROWS)
-    for tile in (0, 1):
-        data_acc[tile] = data_in[tile]
-        source_acc[tile] = source_in[tile]
+        at = PLACES[name, 1][1][1]
+        fill_center(at, edges[name].at[ANG + HALF], packed_piece(name, 1), EDGE)
+    fill_center(EDGE, views.at[HALF * ANG + HALF], HALF * ROWS, ROWS)
     center_ref[...] = warped[HALF, pl.ds(first_row(0), OUT), :]
-    data, source = shifted_views(
-        ghost[...],
-        lambda s: ghost_rows((s + HALF) * ROWS, ROWS),
-        lambda name, q: ghost_rows(packed_piece(name, q), EDGE),
+    sums = shifted_views(
+        edge[...],
+        lambda s: edge_rows((s + HALF) * ROWS, ROWS),
+        lambda name, q: edge_rows(packed_piece(name, q), EDGE),
         center_ref[...],
         warped,
         side,
         zero,
         zero,
     )
-    for step in (4, 8, 16, 32):
-        data = data + pltpu.roll(data, LANES - step, 1)
-        source = source + pltpu.roll(source, LANES - step, 1)
-    data_acc[2] = data
-    source_acc[2] = source
-    for tile in (0, 1):
-        sign = tile
-        center_ref[...] = center_slab[tile, pl.ds(first_row(0), OUT), :]
-
-        def lhs(ref, row, sign=sign):
-            count = ref.shape[0]
-            if sign:
-                return jnp.concatenate([ref[:, LANES:], right[pl.ds(row, count), :]], axis=1)
-            return jnp.concatenate([left[pl.ds(row, count), :], ref[:, :LANES]], axis=1)
-
-        def body(a, carry, tile=tile, sign=sign, lhs=lhs):
-            ti = HALF + 1 + a if sign else HALF - 1 - a
-            data, source = shifted_views(
-                outer[sign, a],
-                lambda s: lhs(views.at[(s + HALF) * ANG + ti], (s + HALF) * ROWS),
-                lambda name, q: lhs(edges[name].at[q * ANG + ti], packed_piece(name, q)),
-                center_ref[...],
-                warped,
-                side,
-                zero,
-                zero,
-            )
-            data_acc[tile] += data
-            source_acc[tile] += source
-            return carry
-
-        lax.fori_loop(0, HALF, body, 0)
-
-    def joined(ref):
-        return jnp.concatenate([ref[0], ref[1], ref[2]], axis=1)
+
+    def total(inside, x):
+        high = x.astype(jnp.bfloat16)
+        rest = x - high.astype(F32)
+        middle = rest.astype(jnp.bfloat16)
+        low = (rest - middle.astype(F32)).astype(jnp.bfloat16)
+        spread = dot(low, scatter[...]) + dot(middle, scatter[...]) + dot(high, scatter[...])
+        return jnp.concatenate([inside[0], inside[1], zero], axis=1) + spread
+
+    data_sum = total(data_in, sums[0])
+    source_sum = total(source_in, sums[1])
 
     wide = 3 * LANES
 
@@ -472,8 +465,8 @@
     v_up = jnp.where((row >= 1) & (row <= total_rows - 1), jnp.exp(-vertical * vertical), 0.0)
     h_right = after(h_left)
     v_down = under(v_up)
-    coeff = DAMPING + joined(data_acc) * (0.25 / VIEWS)
-    source = joined(source_acc) * (-0.5 / VIEWS)
+    coeff = DAMPING + data_sum * (0.25 / VIEWS)
+    source = source_sum * (-0.5 / VIEWS)
     precond = coeff + SMOOTH * (h_left + h_right + v_up + v_down)
     inverse = 1.0 / precond
 
@@ -547,12 +540,12 @@
     )
 
 
-def call(kernel, outs, scratch=(), name=None, **more):
+def call(kernel, outs, scratch=(), name=None, vmem=24, **more):
     return pl.pallas_call(
         kernel,
         out_shape=outs,
         scratch_shapes=list(scratch),
-        compiler_params=pltpu.CompilerParams(vmem_limit_bytes=24 * 1024 * 1024),
+        compiler_params=pltpu.CompilerParams(vmem_limit_bytes=vmem * 1024 * 1024),
         name=name,
         **more,
     )
@@ -567,16 +560,19 @@
 
 def shards(views):
     rows, cols = lax.axis_size("row"), lax.axis_size("col")
-    inner, outer, ghost, center = (jnp.asarray(x) for x in tables())
+    inner, edge_matrix, center, scatter = (jnp.asarray(x) for x in tables())
     bf16 = jnp.bfloat16
     struct = jax.ShapeDtypeStruct
 
     edge = struct((PIECES * ANG, EDGE, COLS), bf16)
-    pair, after, views = call(
+    room = pltpu.VMEM(edge.shape, bf16)
+    taken = pltpu.VMEM(((HALF + 1) * ANG, EDGE, COLS), bf16)
+    pair, after = call(
         pack_rows,
-        (edge, edge, struct(views.shape, bf16)),
-        (pltpu.SemaphoreType.DMA((ANG,)),),
+        (edge, edge),
+        (taken, taken, room, room, pltpu.SemaphoreType.DMA((2,))),
         name="pack_rows",
+        vmem=60,
         in_specs=[pl.BlockSpec(memory_space=pltpu.HBM)],
     )(views)
     pair = swap(pair, "row", 0)
@@ -604,13 +600,10 @@
         views, above, below, inner
     )
     field = struct((OUT, COLS), F32)
-    acc = pltpu.VMEM((3, OUT, LANES), F32)
     zed, near, nxt, precond, message = call(
         functools.partial(outer_sums, rows * ROWS, cols * COLS),
         (field, field, field, field, struct((1, LANES), F32)),
         (
-            acc,
-            acc,
             slab,
             slab,
             tile,
@@ -619,7 +612,7 @@
             pltpu.VMEM((PACKED, LANES), bf16),
         ),
         name="outer_sums",
-    )(views, above, below, own, pair, after, data, source, outer, ghost, center)
+    )(views, above, below, own, pair, after, data, source, edge_matrix, center, scatter)
     n = rows * cols
     messages = lax.all_to_all(
         jnp.broadcast_to(message[None], (n, 1, LANES)), ALL, 0, 0, tiled=True

time: 62.4 us -> 58.6 us (0.939)
  blocking collectives: 33.6 us -> 30.2 us
  local copies, waits for them, and re-layouts: 1.83 us -> 0.09 us
  Pallas kernels: 14 us -> 14.9 us
    pallas_call x1, Pallas kernels: 5.63 us -> 1.54 us  [shards(): call(functools.partial(outer_sums, rows * ROWS, cols * COLS), (field, fie...]
    pallas_call x1, Pallas kernels: 4.24 us -> 8.14 us  [shards(): call(inner_sums, (sums, sums), (slab, slab, tile), name='inner_sums')]
    all_to_all x1, blocking collectives: 33.6 us -> 30.2 us  [shards(): lax.all_to_all(jnp.broadcast_to(message[None], (n, 1, LANES)), ALL, 0, 0,...]
    unnamed x10, local copies, waits for them, and re-layouts: 1.76 us -> 0.02 us
    pallas_call x1, Pallas kernels: 0.99 us -> 2.12 us  [shards(): call(pack_rows, (edge, edge), (taken, taken, room, room, pltpu.SemaphoreT...]
  transfers between devices with their start and end apart: 4 -> 4, of which waited for: 1 -> 1; matrix products, arithmetic and copies ran while one was open for 0% -> 0% of each run, Pallas kernels for 9% -> 16%
where the time goes in v4:
time: 58.6 us; the launch traced here: 58.4 us
  blocking collectives  30.2 us (52%)
  Pallas kernels  14.9 us (25%)
  waiting for transfers between devices  6.28 us (11%)
  starting transfers between devices  6.12 us (10%)
  between operations  0.78 us (1%)
    all_to_all x1, blocking collectives, shards(): lax.all_to_all(jnp.broadcast_to(message[None], (n, 1, LANES)), ALL, 0, 0,...  30.2 us
    pallas_call x1, Pallas kernels, shards(): call(inner_sums, (sums, sums), (slab, slab, tile), name='inner_sums')  8.14 us
    ppermute x4, waiting for transfers between devices, swap(): return lax.ppermute(array, axis, pairs)  6.28 us
    ppermute x4, starting transfers between devices, swap(): return lax.ppermute(array, axis, pairs)  6.12 us
    pallas_call x1, Pallas kernels, shards(): call(pack_rows, (edge, edge), (taken, taken, room, room, pltpu.SemaphoreT...  2.12 us
    pallas_call x1, Pallas kernels, shards(): call(functools.partial(outer_sums, rows * ROWS, cols * COLS), (field, fie...  1.54 us
    pallas_call x1, Pallas kernels, shards(): call(pack_own, (struct((ANG * ROWS, LANES), bf16), shared, shared, struct...  1.32 us
  transfers between devices with their start and end apart: 4, of which 1 were waited for; matrix products, arithmetic and copies ran while one was open for 0% of the time, Pallas kernels for 16%

profile of v4, /device:TPU:1, one launch (start us, length us, event | category | flops | bytes accessed | tf_op | source)
XLA Modules:
  0.0 58.4 jit_solution(6329396205843886703)
XLA Ops:
  0.6 0.0 copy-start
  0.6 2.1 %pack_rows.1 = (bf16[27,16,256]{2,1,0:T(8,128)(2,1)}, bf16[27,16,256]{2,1,0:T(8,128)(2,1)}) custom-call(bf16[81,64,256]{2,1,0:T(8,128)(2,1)} %views.7), custom_call_target="tpu_custom_call" | custom-call | tf_op jit(solution)/shard_map/pack_rows/pallas_call | solution.py:570
  2.8 0.0 copy-start.1
  2.8 3.3 %collective-permute-start = (bf16[27,16,256]{2,1,0:T(8,128)(2,1)}, bf16[27,16,256]{2,1,0:T(8,128)(2,1)S(1)}, u32[]{:S(2)}, u32[]{:S(2)}) collective-permute-start(bf16[27,16,256]{2,1,0:T(8,128)(2,1)} %get-tuple-element.20), channel_id=1, source_target_pairs={{0,8},{8,0},{16,24},{24,16},{32,40},{40,32},{48,56},{56,48},{64,72... | collective-permute-start | bytes 663560 | tf_op jit(solution)/shard_map/ppermute | solution.py:558
  6.1 1.9 %collective-permute-start.1 = (bf16[27,16,256]{2,1,0:T(8,128)(2,1)}, bf16[27,16,256]{2,1,0:T(8,128)(2,1)S(1)}, u32[]{:S(2)}, u32[]{:S(2)}) collective-permute-start(bf16[27,16,256]{2,1,0:T(8,128)(2,1)} %get-tuple-element.21), channel_id=1, source_target_pairs={{8,16},{16,8},{24,32},{32,24},{40,48},{48,40},{56,64},{64,56},{72,... | collective-permute-start | bytes 663560 | tf_op jit(solution)/shard_map/ppermute | solution.py:558
  8.0 0.0 copy-done
  8.0 1.3 %pack_own.1 = (bf16[576,128]{1,0:T(8,128)(2,1)S(1)}, bf16[320,128]{1,0:T(8,128)(2,1)S(1)}, bf16[320,128]{1,0:T(8,128)(2,1)S(1)}, bf16[9,256,128]{2,1,0:T(8,128)(2,1)S(1)}) custom-call(bf16[81,64,256]{2,1,0:T(8,128)(2,1)S(1)} %copy-done), custom_call_target="tpu_custom_call" | custom-call | tf_op jit(solution)/shard_map/pack_own/pallas_call | solution.py:581
  9.4 0.0 collective-permute-done.got_pair
  9.4 6.3 %collective-permute-done.1.got_next = bf16[27,16,256]{2,1,0:T(8,128)(2,1)S(1)} collective-permute-done((bf16[27,16,256]{2,1,0:T(8,128)(2,1)}, bf16[27,16,256]{2,1,0:T(8,128)(2,1)S(1)}, u32[]{:S(2)}, u32[]{:S(2)}) %collective-permute-start.1) | collective-permute-done | bytes 221216 | tf_op jit(solution)/shard_map/ppermute | solution.py:558
  15.6 0.7 %pack_edges.1 = (bf16[27,16,256]{2,1,0:T(8,128)(2,1)S(1)}, bf16[27,16,256]{2,1,0:T(8,128)(2,1)S(1)}, bf16[672,128]{1,0:T(8,128)(2,1)S(1)}, bf16[368,128]{1,0:T(8,128)(2,1)S(1)}, bf16[368,128]{1,0:T(8,128)(2,1)S(1)}) custom-call(bf16[27,16,256]{2,1,0:T(8,128)(2,1)S(1)} %collective-permute-done.got_pair, ...), custom_call_target="tpu_custom_call" | custom-call | tf_op jit(solution)/shard_map/pack_edges/pallas_call | solution.py:588
  16.3 0.0 copy-start.2
  16.3 0.0 copy-start.3
  16.3 0.0 copy-start.4
  16.4 0.1 collective-permute-start.2
  16.5 0.8 %collective-permute-start.3 = (bf16[368,128]{1,0:T(8,128)(2,1)S(1)}, bf16[368,128]{1,0:T(8,128)(2,1)S(1)}, u32[]{:S(2)}, u32[]{:S(2)}) collective-permute-start(bf16[368,128]{1,0:T(8,128)(2,1)S(1)} %get-tuple-element.30), channel_id=1, source_target_pairs={{1,2},{2,1},{3,4},{4,3},{5,6},{6,5},{9,10},{10,9},{11,12},{12,11},... | collective-permute-start | bytes 282632 | tf_op jit(solution)/shard_map/ppermute | solution.py:558
  17.3 0.0 copy-done.1
  17.3 8.1 %inner_sums.1 = (f32[2,72,128]{2,1,0:T(8,128)S(1)}, f32[2,72,128]{2,1,0:T(8,128)S(1)}) custom-call(bf16[81,64,256]{2,1,0:T(8,128)(2,1)S(1)} %copy-done, bf16[27,16,256]{2,1,0:T(8,128)(2,1)S(1)} %get-tuple-element.26.above, bf16[27,16,256]{2,1,0:T(8,128)(2,1)S(1)} %get-tuple-element.27.below, bf16[2,2,4,256,256]{4,3,2,1,0:T(8,128)(2,1)S(1)} %copy-done.1), custom_call_target="tpu_custom_call" | custom-call | tf_op jit(solution)/shard_map/inner_sums/pallas_call | solution.py:599
  25.4 0.0 collective-permute-done.2.got_pair
  25.4 0.0 collective-permute-done.3.got_next
  25.4 0.0 copy-done.2
  25.5 0.0 copy-done.3
  25.5 0.0 copy-done.4
  25.5 1.5 %outer_sums.1 = (f32[72,256]{1,0:T(8,128)S(1)}, f32[72,256]{1,0:T(8,128)S(1)}, f32[72,256]{1,0:T(8,128)S(1)}, f32[72,256]{1,0:T(8,128)S(1)}, f32[1,128]{1,0:T(1,128)S(1)}) custom-call(bf16[81,64,256]{2,1,0:T(8,128)(2,1)S(1)} %copy-done, bf16[27,16,256]{2,1,0:T(8,128)(2,1)S(1)} %get-tuple-element.26.above, bf16[27,16,256]{2,1,0:T(8,128)(2,1)S(1)} %get-tuple-element.27.below, ...), custom_call_target="tpu_custom_call" | custom-call | tf_op jit(solution)/shard_map/outer_sums/pallas_call | solution.py:603
  27.0 0.1 broadcast_in_dim.9
  27.1 30.2 %all_to_all.5 = f32[256,1,128]{2,1,0:T(1,128)S(1)} all-to-all(f32[256,1,128]{2,1,0:T(1,128)S(1)} %broadcast_in_dim.9), channel_id=1, replica_groups=mesh['row'=32,'col'=8] {'row','col'}, dimensions={0} | all-to-all | bytes 262144 | tf_op jit(solution)/shard_map/all_to_all | solution.py:617
  57.3 1.1 %finish.1 = (f32[64,256]{1,0:T(8,128)}, f32[64,256]{1,0:T(8,128)}) custom-call(f32[256,128]{1,0:T(8,128)S(1)} %bitcast.2, f32[72,256]{1,0:T(8,128)S(1)} %get-tuple-element.34.zed_ref, f32[72,256]{1,0:T(8,128)S(1)} %get-tuple-element.35.near_ref, f32[72,256]{1,0:T(8,128)S(1)} %get-tuple-element.36.next_ref, f32[72,256]{1,0:T(8,128)S(1)} %get-tuple-element.37.precond_ref), custom_call_target="tpu_custom_call" | custom-call | tf_op jit(solution)/shard_map/finish/pallas_call | solution.py:621
Async XLA Ops:
  0.6 7.4 %copy-start = (bf16[81,64,256]{2,1,0:T(8,128)(2,1)S(1)}, bf16[81,64,256]{2,1,0:T(8,128)(2,1)}, u32[]{:S(2)}) copy-start(bf16[81,64,256]{2,1,0:T(8,128)(2,1)} %views.7) | copy-start | bytes 7962628
  2.8 14.5 %copy-start.1 = (bf16[2,2,4,256,256]{4,3,2,1,0:T(8,128)(2,1)S(1)}, bf16[2,2,4,256,256]{4,3,2,1,0:T(8,128)(2,1)}, u32[]{:S(2)}) copy-start(bf16[2,2,4,256,256]{4,3,2,1,0:T(8,128)(2,1)} %constant.8.clone.inner) | copy-start | bytes 6291460
  2.8 6.6 %collective-permute-start = (bf16[27,16,256]{2,1,0:T(8,128)(2,1)}, bf16[27,16,256]{2,1,0:T(8,128)(2,1)S(1)}, u32[]{:S(2)}, u32[]{:S(2)}) collective-permute-start(bf16[27,16,256]{2,1,0:T(8,128)(2,1)} %get-tuple-element.20), channel_id=1, source_target_pairs={{0,8},{8,0},{16,24},{24,16},{32,40},{40,32},{48,56},{56,48},{64,72... | collective-permute-start | bytes 663560 | tf_op jit(solution)/shard_map/ppermute | solution.py:558
  6.1 9.5 %collective-permute-start.1 = (bf16[27,16,256]{2,1,0:T(8,128)(2,1)}, bf16[27,16,256]{2,1,0:T(8,128)(2,1)S(1)}, u32[]{:S(2)}, u32[]{:S(2)}) collective-permute-start(bf16[27,16,256]{2,1,0:T(8,128)(2,1)} %get-tuple-element.21), channel_id=1, source_target_pairs={{8,16},{16,8},{24,32},{32,24},{40,48},{48,40},{56,64},{64,56},{72,... | collective-permute-start | bytes 663560 | tf_op jit(solution)/shard_map/ppermute | solution.py:558
  16.3 9.1 %copy-start.2 = (bf16[512,256]{1,0:T(8,128)(2,1)S(1)}, bf16[512,256]{1,0:T(8,128)(2,1)}, u32[]{:S(2)}) copy-start(bf16[512,256]{1,0:T(8,128)(2,1)} %constant.10.clone.edge_center) | copy-start | bytes 786436
  16.3 9.1 %copy-start.3 = (bf16[384,256]{1,0:T(8,128)(2,1)S(1)}, bf16[384,256]{1,0:T(8,128)(2,1)}, u32[]{:S(2)}) copy-start(bf16[384,256]{1,0:T(8,128)(2,1)} %constant.9.clone.edge) | copy-start | bytes 589828
  16.3 9.1 %copy-start.4 = (bf16[128,384]{1,0:T(8,128)(2,1)S(1)}, bf16[128,384]{1,0:T(8,128)(2,1)}, u32[]{:S(2)}) copy-start(bf16[128,384]{1,0:T(8,128)(2,1)} %constant.11.clone.scatter) | copy-start | bytes 294916
  16.4 9.1 %collective-permute-start.2 = (bf16[368,128]{1,0:T(8,128)(2,1)S(1)}, bf16[368,128]{1,0:T(8,128)(2,1)S(1)}, u32[]{:S(2)}, u32[]{:S(2)}) collective-permute-start(bf16[368,128]{1,0:T(8,128)(2,1)S(1)} %get-tuple-element.29), channel_id=1, source_target_pairs={{0,1},{1,0},{2,3},{3,2},{4,5},{5,4},{6,7},{7,6},{8,9},{9,8},{10,11... | collective-permute-start | bytes 282632 | tf_op jit(solution)/shard_map/ppermute | solution.py:558
  16.5 9.0 %collective-permute-start.3 = (bf16[368,128]{1,0:T(8,128)(2,1)S(1)}, bf16[368,128]{1,0:T(8,128)(2,1)S(1)}, u32[]{:S(2)}, u32[]{:S(2)}) collective-permute-start(bf16[368,128]{1,0:T(8,128)(2,1)S(1)} %get-tuple-element.30), channel_id=1, source_target_pairs={{1,2},{2,1},{3,4},{4,3},{5,6},{6,5},{9,10},{10,9},{11,12},{12,11},... | collective-permute-start | bytes 282632 | tf_op jit(solution)/shard_map/ppermute | solution.py:558

commit v5 on v4

--- a/solution.py
+++ b/solution.py
@@ -21,7 +21,7 @@
 PIECES = 3
 PACKED = ANG * ROWS + 2 * PIECES * EDGE
 PAIRS = ((-4, -3), (-2, -1), (1, 2), (3, 4), (0, 0))
-SENT = len(PAIRS) * ROWS + PIECES * EDGE
+SHARED = len(PAIRS) * ROWS
 LANES = 128
 SMOOTH = 2.0
 DAMPING = 0.1
@@ -93,7 +93,7 @@
         scatter[lane, col % (3 * LANES)] = 1
     for col in (-3, -2, -1, COLS, COLS + 1, COLS + 2):
         center[center_source(col), LANES + col % LANES] = 1
-    return tuple(x.astype(ml_dtypes.bfloat16) for x in (inner, edge, center, scatter))
+    return tuple(x.astype(ml_dtypes.bfloat16) for x in (*inner, edge, center, scatter))
 
 
 def dot(a, b):
@@ -104,50 +104,36 @@
     return lax.rem(lax.axis_index(axis), 2) == 0
 
 
-def pack_rows(views, send_pair, send_next, tops, bottoms, ups, downs, sems):
-    count = (HALF + 1) * ANG
-    get_tops = pltpu.make_async_copy(
-        views.at[pl.ds(HALF * ANG, count), pl.ds(0, EDGE)], tops, sems.at[0]
-    )
-    get_bottoms = pltpu.make_async_copy(
-        views.at[pl.ds(0, count), pl.ds(ROWS - EDGE, EDGE)], bottoms, sems.at[1]
-    )
-    get_tops.start()
-    get_bottoms.start()
+def pack_rows(views, send_pair, send_next, ups_out, downs_out):
+    even = is_even("row")
     index = lax.broadcasted_iota(jnp.int32, (EDGE, COLS), 0)
 
-    def put(out, q, ti, rows):
-        out[q * ANG + ti] = rows.astype(jnp.bfloat16)
-
-    get_tops.wait()
+    def put(ups, q, ti, rows):
+        (ups_out if ups else downs_out)[q * ANG + ti] = rows.astype(jnp.bfloat16)
+
     for ti in range(ANG):
 
-        def first(s, ti=ti):
-            return tops[s * ANG + ti].astype(F32)
-
-        put(ups, 0, ti, first(4))
-        put(ups, 1, ti, jnp.where(index < 12, first(3), pltpu.roll(first(0), 12, 0)))
-        put(ups, 2, ti, jnp.where(index < 9, first(2), pltpu.roll(first(1), 9, 0)))
-    get_bottoms.wait()
-    for ti in range(ANG):
-
-        def last(s, ti=ti):
-            return bottoms[(s + HALF) * ANG + ti].astype(F32)
-
-        put(downs, 0, ti, last(-4))
-        put(downs, 1, ti, jnp.where(index < 4, pltpu.roll(last(0), 4, 0), last(-3)))
-        put(downs, 2, ti, jnp.where(index < 7, pltpu.roll(last(-1), 7, 0), last(-2)))
-    even = is_even("row")
+        def rows_of(s, start, ti=ti):
+            return views[(s + HALF) * ANG + ti, pl.ds(start, EDGE), :].astype(F32)
+
+        first = functools.partial(rows_of, start=0)
+        last = functools.partial(rows_of, start=ROWS - EDGE)
+        put(True, 0, ti, first(4))
+        put(True, 1, ti, jnp.where(index < 12, first(3), pltpu.roll(first(0), 12, 0)))
+        put(True, 2, ti, jnp.where(index < 9, first(2), pltpu.roll(first(1), 9, 0)))
+        put(False, 0, ti, last(-4))
+        put(False, 1, ti, jnp.where(index < 4, pltpu.roll(last(0), 4, 0), last(-3)))
+        put(False, 2, ti, jnp.where(index < 7, pltpu.roll(last(-1), 7, 0), last(-2)))
 
     @pl.when(even)
     def _():
-        send_pair[...] = downs[...]
-        send_next[...] = ups[...]
+        send_pair[...] = downs_out[...]
+        send_next[...] = ups_out[...]
 
     @pl.when(jnp.logical_not(even))
     def _():
-        send_pair[...] = ups[...]
-        send_next[...] = downs[...]
+        send_pair[...] = ups_out[...]
+        send_next[...] = downs_out[...]
 
 
 PLACES = {
@@ -176,7 +162,21 @@
     )
 
 
-def pack_own(views, own, to_left, to_right, pack):
+def by_pair(to_left, to_right, send_pair, send_next):
+    even = is_even("col")
+
+    @pl.when(even)
+    def _():
+        send_pair[...] = to_right[...]
+        send_next[...] = to_left[...]
+
+    @pl.when(jnp.logical_not(even))
+    def _():
+        send_pair[...] = to_left[...]
+        send_next[...] = to_right[...]
+
+
+def pack_own(views, own, send_pair, send_next, pack, to_left, to_right):
     column = lax.broadcasted_iota(jnp.int32, (COLS, LANES), 0)
     lane = lax.broadcasted_iota(jnp.int32, (COLS, LANES), 1)
     for t in range(-HALF, HALF + 1):
@@ -202,11 +202,13 @@
             own[(s + HALF) * ROWS : (s + HALF + 1) * ROWS, :] = total.astype(jnp.bfloat16)
             both.append(total)
         share(both[0], both[1], to_left, to_right, p * ROWS)
-
-
-def pack_edges(
-    got_pair, got_next, pack, own_in, left_in, right_in,
-    above, below, own, send_pair, send_next, to_left, to_right,
+    by_pair(to_left, to_right, send_pair, send_next)
+
+
+def pack_edges_and_left_sums(
+    views, inner, got_pair, got_next, pack, own_in,
+    data_out, source_out, above, below, own, send_pair, send_next,
+    to_left, to_right, *scratch,
 ):
     even = is_even("row")
 
@@ -230,26 +232,13 @@
             own[pl.ds(packed_piece(side, q), EDGE), :] = total.astype(jnp.bfloat16)
             both.append(total)
         share(both[0], both[1], to_left, to_right, q * EDGE)
-    rows = len(PAIRS) * ROWS
-    even = is_even("col")
-
-    def send(out, block, piece):
-        out[:rows, :] = block[...]
-        out[rows:, :] = piece[...]
-
-    @pl.when(even)
-    def _():
-        send(send_pair, right_in, to_right)
-        send(send_next, left_in, to_left)
-
-    @pl.when(jnp.logical_not(even))
-    def _():
-        send(send_pair, left_in, to_left)
-        send(send_next, right_in, to_right)
-
-
-def unshare(source, high, out):
-    def move(at, to, count, half):
+    by_pair(to_left, to_right, send_pair, send_next)
+    edges = {"above": above, "below": below}
+    inner_sums(0, views, edges, inner, data_out, source_out, *scratch)
+
+
+def unshare(blocks, pieces, high, out):
+    def move(source, at, to, count, half):
         rows = source[pl.ds(at, count), :]
         if half != high:
             rows = pltpu.roll(rows.astype(F32), 64, 1).astype(jnp.bfloat16)
@@ -258,10 +247,10 @@
     for p, pair in enumerate(PAIRS):
         for half, s in enumerate(pair):
             if s or not half:
-                move(p * ROWS, (s + HALF) * ROWS, ROWS, half)
+                move(blocks, p * ROWS, (s + HALF) * ROWS, ROWS, half)
     for q in range(PIECES):
         for half, side in enumerate(("above", "below")):
-            move(len(PAIRS) * ROWS + q * EDGE, packed_piece(side, q), EDGE, half)
+            move(pieces, q * EDGE, packed_piece(side, q), EDGE, half)
 
 
 def first_row(s):
@@ -306,55 +295,64 @@
     return both[:, :LANES], both[:, LANES:]
 
 
-def shifted_views(matrix, own, piece, center, warped, side, data, source):
-    fill_pieces(lambda name, q: halves(dot(piece(name, q), matrix)), (warped, side))
-    for s in range(-HALF, HALF + 1):
+def shifted_views(matrix, own, piece, center, warped, side):
+    span = range(-HALF, HALF + 1)
+    rows = [own(s) for s in span] + [piece(name, q) for name, q in PLACES]
+    both = dot(jnp.concatenate(rows, axis=0), matrix)
+    first = {key: ANG * ROWS + i * EDGE for i, key in enumerate(PLACES)}
+
+    def part(at, count):
+        return both[at : at + count, :LANES], both[at : at + count, LANES:]
+
+    fill_pieces(lambda name, q: part(first[name, q], EDGE), (warped, side))
+    data = source = jnp.zeros((OUT, LANES), F32)
+    for s in span:
         w, d = warped.at[s + HALF], side.at[s + HALF]
-        both = dot(own(s), matrix)
-        fill(w, own_row(s), both[:, :LANES])
-        fill(d, own_row(s), both[:, LANES:])
+        shifted, slope = part((s + HALF) * ROWS, ROWS)
+        fill(w, own_row(s), shifted)
+        fill(d, own_row(s), slope)
         data, source = accumulate(s, w, d, center, data, source)
     return data, source
 
 
-def inner_sums(views, above, below, inner, data_out, source_out, warped, side, center_ref):
+def inner_sums(tile, views, edges, inner, data_out, source_out, warped, side, center_ref):
     zero_tails(warped)
     zero_tails(side)
-    zero = jnp.zeros((OUT, LANES), F32)
+    lanes = slice(tile * LANES, (tile + 1) * LANES)
+    fill_pieces(
+        lambda name, q: (edges[name][q * ANG + HALF][:, lanes].astype(F32),), (warped,)
+    )
+    data = source = jnp.zeros((OUT, LANES), F32)
+    for s in (0, -4, -3, -2, -1, 1, 2, 3, 4):
+        w = warped.at[s + HALF]
+        fill(w, own_row(s), views[(s + HALF) * ANG + HALF][:, lanes].astype(F32))
+        if s == 0:
+            center_ref[...] = w[pl.ds(first_row(0), OUT), :]
+        data, source = accumulate(s, w, None, center_ref[...], data, source)
+    data_out[...] = data
+    source_out[...] = source
+
+    def body(a, carry, sign):
+        ti = HALF + 1 + a if sign else HALF - 1 - a
+        data, source = shifted_views(
+            inner[sign, a],
+            lambda s: views[(s + HALF) * ANG + ti],
+            lambda name, q: edges[name][q * ANG + ti],
+            center_ref[...],
+            warped,
+            side,
+        )
+        data_out[...] += data
+        source_out[...] += source
+        return carry
+
+    for sign in (0, 1):
+        lax.fori_loop(0, HALF, functools.partial(body, sign=sign), 0)
+
+
+def right_sums(views, above, below, inner, data_out, source_out, *scratch):
     edges = {"above": above, "below": below}
-    for tile in (0, 1):
-        lanes = slice(tile * LANES, (tile + 1) * LANES)
-        fill_pieces(
-            lambda name, q: (edges[name][q * ANG + HALF][:, lanes].astype(F32),), (warped,)
-        )
-        data = source = zero
-        for s in (0, -4, -3, -2, -1, 1, 2, 3, 4):
-            w = warped.at[s + HALF]
-            fill(w, own_row(s), views[(s + HALF) * ANG + HALF][:, lanes].astype(F32))
-            if s == 0:
-                center_ref[...] = w[pl.ds(first_row(0), OUT), :]
-            data, source = accumulate(s, w, None, center_ref[...], data, source)
-        data_out[tile] = data
-        source_out[tile] = source
-
-        def body(a, carry, sign, tile=tile):
-            ti = HALF + 1 + a if sign else HALF - 1 - a
-            data, source = shifted_views(
-                inner[tile, sign, a],
-                lambda s: views[(s + HALF) * ANG + ti],
-                lambda name, q: edges[name][q * ANG + ti],
-                center_ref[...],
-                warped,
-                side,
-                zero,
-                zero,
-            )
-            data_out[tile] += data
-            source_out[tile] += source
-            return carry
-
-        for sign in (0, 1):
-            lax.fori_loop(0, HALF, functools.partial(body, sign=sign), 0)
+    inner_sums(1, views, edges, inner, data_out, source_out, *scratch)
 
 
 def outer_sums(
@@ -366,8 +364,12 @@
     own,
     got_pair,
     got_next,
-    data_in,
-    source_in,
+    got_piece_pair,
+    got_piece_next,
+    data_left,
+    source_left,
+    data_right,
+    source_right,
     edge,
     edge_center,
     scatter,
@@ -387,13 +389,13 @@
 
     @pl.when(even)
     def _():
-        unshare(got_next, 1, left)
-        unshare(got_pair, 0, right)
+        unshare(got_next, got_piece_next, 1, left)
+        unshare(got_pair, got_piece_pair, 0, right)
 
     @pl.when(jnp.logical_not(even))
     def _():
-        unshare(got_pair, 1, left)
-        unshare(got_next, 0, right)
+        unshare(got_pair, got_piece_pair, 1, left)
+        unshare(got_next, got_piece_next, 0, right)
 
     edges = {"above": above, "below": below}
     zero_tails(warped)
@@ -423,8 +425,6 @@
         center_ref[...],
         warped,
         side,
-        zero,
-        zero,
     )
 
     def total(inside, x):
@@ -433,10 +433,10 @@
         middle = rest.astype(jnp.bfloat16)
         low = (rest - middle.astype(F32)).astype(jnp.bfloat16)
         spread = dot(low, scatter[...]) + dot(middle, scatter[...]) + dot(high, scatter[...])
-        return jnp.concatenate([inside[0], inside[1], zero], axis=1) + spread
-
-    data_sum = total(data_in, sums[0])
-    source_sum = total(source_in, sums[1])
+        return jnp.concatenate([inside[0][...], inside[1][...], zero], axis=1) + spread
+
+    data_sum = total((data_left, data_right), sums[0])
+    source_sum = total((source_left, source_right), sums[1])
 
     wide = 3 * LANES
 
@@ -540,14 +540,13 @@
     )
 
 
-def call(kernel, outs, scratch=(), name=None, vmem=24, **more):
+def call(kernel, outs, scratch=(), name=None):
     return pl.pallas_call(
         kernel,
         out_shape=outs,
         scratch_shapes=list(scratch),
-        compiler_params=pltpu.CompilerParams(vmem_limit_bytes=vmem * 1024 * 1024),
+        compiler_params=pltpu.CompilerParams(vmem_limit_bytes=24 * 1024 * 1024),
         name=name,
-        **more,
     )
 
 
@@ -560,45 +559,41 @@
 
 def shards(views):
     rows, cols = lax.axis_size("row"), lax.axis_size("col")
-    inner, edge_matrix, center, scatter = (jnp.asarray(x) for x in tables())
+    left_inner, right_inner, edge_matrix, center, scatter = (jnp.asarray(x) for x in tables())
     bf16 = jnp.bfloat16
     struct = jax.ShapeDtypeStruct
 
     edge = struct((PIECES * ANG, EDGE, COLS), bf16)
     room = pltpu.VMEM(edge.shape, bf16)
-    taken = pltpu.VMEM(((HALF + 1) * ANG, EDGE, COLS), bf16)
-    pair, after = call(
-        pack_rows,
-        (edge, edge),
-        (taken, taken, room, room, pltpu.SemaphoreType.DMA((2,))),
-        name="pack_rows",
-        vmem=60,
-        in_specs=[pl.BlockSpec(memory_space=pltpu.HBM)],
-    )(views)
+    pair, after = call(pack_rows, (edge, edge), (room, room), name="pack_rows")(views)
     pair = swap(pair, "row", 0)
     after = swap(after, "row", 1)
-    shared = struct((len(PAIRS) * ROWS, LANES), bf16)
-    own, to_left, to_right, pack = call(
+    shared = struct((SHARED, LANES), bf16)
+    room = pltpu.VMEM((SHARED, LANES), bf16)
+    own, block_pair, block_next, pack = call(
         pack_own,
         (struct((ANG * ROWS, LANES), bf16), shared, shared, struct((ANG, COLS, LANES), bf16)),
+        (room, room),
         name="pack_own",
     )(views)
-    sent = struct((SENT, LANES), bf16)
-    small = pltpu.VMEM((PIECES * EDGE, LANES), bf16)
-    above, below, own, pair, after = call(
-        pack_edges,
-        (edge, edge, struct((PACKED, LANES), bf16), sent, sent),
-        (small, small),
-        name="pack_edges",
-    )(pair, after, pack, own, to_left, to_right)
-    pair = swap(pair, "col", 0)
-    after = swap(after, "col", 1)
+    block_next = swap(block_next, "col", 1)
+    block_pair = swap(block_pair, "col", 0)
     slab = pltpu.VMEM((ANG, SLAB, LANES), F32)
     tile = pltpu.VMEM((OUT, LANES), F32)
-    sums = struct((2, OUT, LANES), F32)
-    data, source = call(inner_sums, (sums, sums), (slab, slab, tile), name="inner_sums")(
-        views, above, below, inner
-    )
+    sums = struct((OUT, LANES), F32)
+    sent = struct((PIECES * EDGE, LANES), bf16)
+    small = pltpu.VMEM((PIECES * EDGE, LANES), bf16)
+    data_left, source_left, above, below, own, piece_pair, piece_next = call(
+        pack_edges_and_left_sums,
+        (sums, sums, edge, edge, struct((PACKED, LANES), bf16), sent, sent),
+        (small, small, slab, slab, tile),
+        name="left_sums",
+    )(views, left_inner, pair, after, pack, own)
+    piece_next = swap(piece_next, "col", 1)
+    piece_pair = swap(piece_pair, "col", 0)
+    data_right, source_right = call(
+        right_sums, (sums, sums), (slab, slab, tile), name="right_sums"
+    )(views, above, below, right_inner)
     field = struct((OUT, COLS), F32)
     zed, near, nxt, precond, message = call(
         functools.partial(outer_sums, rows * ROWS, cols * COLS),
@@ -612,7 +607,10 @@
             pltpu.VMEM((PACKED, LANES), bf16),
         ),
         name="outer_sums",
-    )(views, above, below, own, pair, after, data, source, edge_matrix, center, scatter)
+    )(
+        views, above, below, own, block_pair, block_next, piece_pair, piece_next,
+        data_left, source_left, data_right, source_right, edge_matrix, center, scatter,
+    )
     n = rows * cols
     messages = lax.all_to_all(
         jnp.broadcast_to(message[None], (n, 1, LANES)), ALL, 0, 0, tiled=True

time: 58.6 us -> 59.2 us (1.010)
  Pallas kernels: 14.9 us -> 10.1 us
  blocking collectives: 30.2 us -> 34.1 us
  waiting for transfers between devices: 6.28 us -> 4.13 us
  starting transfers between devices: 6.12 us -> 8 us
  local copies, waits for them, and re-layouts: 0.09 us -> 1.84 us
    pallas_call x3, Pallas kernels: 11 us -> 6.12 us  [the longest x1 3.37 us: shards(): call(pack_edges_and_left_sums, (sums, sums, edge, edge, struct((PACKED, L...]
    all_to_all x1, blocking collectives: 30.2 us -> 34.1 us  [shards(): lax.all_to_all(jnp.broadcast_to(message[None], (n, 1, LANES)), ALL, 0, 0,...]
    ppermute x4 -> x6, waiting for transfers between devices: 6.28 us -> 4.13 us  [swap(): return lax.ppermute(array, axis, pairs)]
    ppermute x4 -> x6, starting transfers between devices: 6.12 us -> 8 us  [swap(): return lax.ppermute(array, axis, pairs)]
    unnamed x10 -> x12, local copies, waits for them, and re-layouts: 0.02 us -> 1.77 us
  transfers between devices with their start and end apart: 4 -> 6, of which waited for: 1 -> 1; matrix products, arithmetic and copies ran while one was open for 0% -> 0% of each run, Pallas kernels for 16% -> 13%
where the time goes in v5:
time: 59.2 us; the launch traced here: 59 us
  blocking collectives  34.1 us (58%)
  Pallas kernels  10.1 us (17%)
  starting transfers between devices  8 us (14%)
  waiting for transfers between devices  4.13 us (7%)
  local copies, waits for them, and re-layouts  1.84 us (3%)
  between operations  0.82 us (1%)
    all_to_all x1, blocking collectives, shards(): lax.all_to_all(jnp.broadcast_to(message[None], (n, 1, LANES)), ALL, 0, 0,...  34.1 us
    ppermute x6, starting transfers between devices, swap(): return lax.ppermute(array, axis, pairs)  8 us
    ppermute x6, waiting for transfers between devices, swap(): return lax.ppermute(array, axis, pairs)  4.13 us
    pallas_call x1, Pallas kernels, shards(): call(pack_edges_and_left_sums, (sums, sums, edge, edge, struct((PACKED, L...  3.37 us
    pallas_call x1, Pallas kernels, shards(): call(right_sums, (sums, sums), (slab, slab, tile), name='right_sums')  2.65 us
    unnamed x12, local copies, waits for them, and re-layouts  1.77 us
    pallas_call x1, Pallas kernels, shards(): call(functools.partial(outer_sums, rows * ROWS, cols * COLS), (field, fie...  1.54 us
    pallas_call x1, Pallas kernels, shards(): call(pack_own, (struct((ANG * ROWS, LANES), bf16), shared, shared, struct...  1.38 us
  transfers between devices with their start and end apart: 6, of which 1 were waited for; matrix products, arithmetic and copies ran while one was open for 0% of the time, Pallas kernels for 13%

profile of v5, /device:TPU:1, one launch (start us, length us, event | category | flops | bytes accessed | tf_op | source)
XLA Modules:
  0.0 59.0 jit_solution(11466420811844879654)
XLA Ops:
  0.6 0.0 copy-start
  0.6 1.7 %copy-done = bf16[81,64,256]{2,1,0:T(8,128)(2,1)S(1)} copy-done((bf16[81,64,256]{2,1,0:T(8,128)(2,1)S(1)}, bf16[81,64,256]{2,1,0:T(8,128)(2,1)}, u32[]{:S(2)}) %copy-start) | copy-done | bytes 2654232
  2.4 0.0 copy-start.1
  2.4 0.1 pack_rows.1
  2.5 3.3 %collective-permute-start = (bf16[27,16,256]{2,1,0:T(8,128)(2,1)S(1)}, bf16[27,16,256]{2,1,0:T(8,128)(2,1)S(1)}, u32[]{:S(2)}, u32[]{:S(2)}) collective-permute-start(bf16[27,16,256]{2,1,0:T(8,128)(2,1)S(1)} %get-tuple-element.22), channel_id=1, source_target_pairs={{0,8},{8,0},{16,24},{24,16},{32,40},{40,32},{48,56},{56,48},{64,72... | collective-permute-start | bytes 663560 | tf_op jit(solution)/shard_map/ppermute | solution.py:557
  5.8 1.9 %collective-permute-start.1 = (bf16[27,16,256]{2,1,0:T(8,128)(2,1)S(1)}, bf16[27,16,256]{2,1,0:T(8,128)(2,1)S(1)}, u32[]{:S(2)}, u32[]{:S(2)}) collective-permute-start(bf16[27,16,256]{2,1,0:T(8,128)(2,1)S(1)} %get-tuple-element.23), channel_id=1, source_target_pairs={{8,16},{16,8},{24,32},{32,24},{40,48},{48,40},{56,64},{64,56},{72,... | collective-permute-start | bytes 663560 | tf_op jit(solution)/shard_map/ppermute | solution.py:557
  7.7 1.4 %pack_own.1 = (bf16[576,128]{1,0:T(8,128)(2,1)S(1)}, bf16[320,128]{1,0:T(8,128)(2,1)S(1)}, bf16[320,128]{1,0:T(8,128)(2,1)S(1)}, bf16[9,256,128]{2,1,0:T(8,128)(2,1)S(1)}) custom-call(bf16[81,64,256]{2,1,0:T(8,128)(2,1)S(1)} %copy-done), custom_call_target="tpu_custom_call" | custom-call | tf_op jit(solution)/shard_map/pack_own/pallas_call | solution.py:573
  9.1 0.0 copy-start.2
  9.1 1.2 %collective-permute-start.2 = (bf16[320,128]{1,0:T(8,128)(2,1)S(1)}, bf16[320,128]{1,0:T(8,128)(2,1)S(1)}, u32[]{:S(2)}, u32[]{:S(2)}) collective-permute-start(bf16[320,128]{1,0:T(8,128)(2,1)S(1)} %get-tuple-element.29), channel_id=1, source_target_pairs={{0,1},{1,0},{2,3},{3,2},{4,5},{5,4},{6,7},{7,6},{8,9},{9,8},{10,11... | collective-permute-start | bytes 245768 | tf_op jit(solution)/shard_map/ppermute | solution.py:557
  10.4 0.7 %collective-permute-start.3 = (bf16[320,128]{1,0:T(8,128)(2,1)S(1)}, bf16[320,128]{1,0:T(8,128)(2,1)S(1)}, u32[]{:S(2)}, u32[]{:S(2)}) collective-permute-start(bf16[320,128]{1,0:T(8,128)(2,1)S(1)} %get-tuple-element.30), channel_id=1, source_target_pairs={{1,2},{2,1},{3,4},{4,3},{5,6},{6,5},{9,10},{10,9},{11,12},{12,11},... | collective-permute-start | bytes 245768 | tf_op jit(solution)/shard_map/ppermute | solution.py:557
  11.0 0.0 collective-permute-done.got_pair
  11.0 4.1 %collective-permute-done.1.got_next = bf16[27,16,256]{2,1,0:T(8,128)(2,1)S(1)} collective-permute-done((bf16[27,16,256]{2,1,0:T(8,128)(2,1)S(1)}, bf16[27,16,256]{2,1,0:T(8,128)(2,1)S(1)}, u32[]{:S(2)}, u32[]{:S(2)}) %collective-permute-start.1) | collective-permute-done | bytes 221216 | tf_op jit(solution)/shard_map/ppermute | solution.py:557
  15.1 0.0 copy-done.1
  15.2 3.4 %left_sums.1 = (f32[72,128]{1,0:T(8,128)S(1)}, f32[72,128]{1,0:T(8,128)S(1)}, bf16[27,16,256]{2,1,0:T(8,128)(2,1)S(1)}, bf16[27,16,256]{2,1,0:T(8,128)(2,1)S(1)}...) custom-call(bf16[81,64,256]{2,1,0:T(8,128)(2,1)S(1)} %copy-done, ...), custom_call_target="tpu_custom_call" | custom-call | tf_op jit(solution)/shard_map/left_sums/pallas_call | solution.py:586
  18.5 0.0 copy-start.3
  18.5 0.0 copy-start.4
  18.6 0.0 copy-start.5
  18.6 0.1 collective-permute-start.4
  18.7 0.8 %collective-permute-start.5 = (bf16[48,128]{1,0:T(8,128)(2,1)S(1)}, bf16[48,128]{1,0:T(8,128)(2,1)S(1)}, u32[]{:S(2)}, u32[]{:S(2)}) collective-permute-start(bf16[48,128]{1,0:T(8,128)(2,1)S(1)} %get-tuple-element.32), channel_id=1, source_target_pairs={{1,2},{2,1},{3,4},{4,3},{5,6},{6,5},{9,10},{10,9},{11,12},{12,11},... | collective-permute-start | bytes 36872 | tf_op jit(solution)/shard_map/ppermute | solution.py:557
  19.5 0.0 copy-done.2
  19.5 2.6 %right_sums.1 = (f32[72,128]{1,0:T(8,128)S(1)}, f32[72,128]{1,0:T(8,128)S(1)}) custom-call(bf16[81,64,256]{2,1,0:T(8,128)(2,1)S(1)} %copy-done, bf16[27,16,256]{2,1,0:T(8,128)(2,1)S(1)} %get-tuple-element.26.above, bf16[27,16,256]{2,1,0:T(8,128)(2,1)S(1)} %get-tuple-element.27.below, bf16[2,4,256,256]{3,2,1,0:T(8,128)(2,1)S(1)} %copy-done.2), custom_call_target="tpu_custom_call" | custom-call | tf_op jit(solution)/shard_map/right_sums/pallas_call | solution.py:594
  22.1 0.0 collective-permute-done.2.got_pair
  22.1 0.0 collective-permute-done.3.got_next
  22.2 0.0 collective-permute-done.4.got_piece_pair
  22.2 0.0 collective-permute-done.5.got_piece_next
  22.2 0.0 copy-done.3
  22.2 0.0 copy-done.4
  22.2 0.0 copy-done.5
  22.2 1.5 %outer_sums.1 = (f32[72,256]{1,0:T(8,128)S(1)}, f32[72,256]{1,0:T(8,128)S(1)}, f32[72,256]{1,0:T(8,128)S(1)}, f32[72,256]{1,0:T(8,128)S(1)}, f32[1,128]{1,0:T(1,128)S(1)}) custom-call(bf16[81,64,256]{2,1,0:T(8,128)(2,1)S(1)} %copy-done, bf16[27,16,256]{2,1,0:T(8,128)(2,1)S(1)} %get-tuple-element.26.above, bf16[27,16,256]{2,1,0:T(8,128)(2,1)S(1)} %get-tuple-element.27.below, ...), custom_call_target="tpu_custom_call" | custom-call | tf_op jit(solution)/shard_map/outer_sums/pallas_call | solution.py:598
  23.8 0.1 broadcast_in_dim.9
  23.8 34.1 %all_to_all.5 = f32[256,1,128]{2,1,0:T(1,128)S(1)} all-to-all(f32[256,1,128]{2,1,0:T(1,128)S(1)} %broadcast_in_dim.9), channel_id=1, replica_groups=mesh['row'=32,'col'=8] {'row','col'}, dimensions={0} | all-to-all | bytes 262144 | tf_op jit(solution)/shard_map/all_to_all | solution.py:615
  57.9 1.1 %finish.1 = (f32[64,256]{1,0:T(8,128)}, f32[64,256]{1,0:T(8,128)}) custom-call(f32[256,128]{1,0:T(8,128)S(1)} %bitcast.2, f32[72,256]{1,0:T(8,128)S(1)} %get-tuple-element.38.zed_ref, f32[72,256]{1,0:T(8,128)S(1)} %get-tuple-element.39.near_ref, f32[72,256]{1,0:T(8,128)S(1)} %get-tuple-element.40.next_ref, f32[72,256]{1,0:T(8,128)S(1)} %get-tuple-element.41.precond_ref), custom_call_target="tpu_custom_call" | custom-call | tf_op jit(solution)/shard_map/finish/pallas_call | solution.py:619
Async XLA Ops:
  0.6 1.8 %copy-start = (bf16[81,64,256]{2,1,0:T(8,128)(2,1)S(1)}, bf16[81,64,256]{2,1,0:T(8,128)(2,1)}, u32[]{:S(2)}) copy-start(bf16[81,64,256]{2,1,0:T(8,128)(2,1)} %views.9) | copy-start | bytes 7962628
  2.4 12.8 %copy-start.1 = (bf16[2,4,256,256]{3,2,1,0:T(8,128)(2,1)S(1)}, bf16[2,4,256,256]{3,2,1,0:T(8,128)(2,1)}, u32[]{:S(2)}) copy-start(bf16[2,4,256,256]{3,2,1,0:T(8,128)(2,1)} %constant.10.clone.inner) | copy-start | bytes 3145732
  2.5 8.5 %collective-permute-start = (bf16[27,16,256]{2,1,0:T(8,128)(2,1)S(1)}, bf16[27,16,256]{2,1,0:T(8,128)(2,1)S(1)}, u32[]{:S(2)}, u32[]{:S(2)}) collective-permute-start(bf16[27,16,256]{2,1,0:T(8,128)(2,1)S(1)} %get-tuple-element.22), channel_id=1, source_target_pairs={{0,8},{8,0},{16,24},{24,16},{32,40},{40,32},{48,56},{56,48},{64,72... | collective-permute-start | bytes 663560 | tf_op jit(solution)/shard_map/ppermute | solution.py:557
  5.8 9.3 %collective-permute-start.1 = (bf16[27,16,256]{2,1,0:T(8,128)(2,1)S(1)}, bf16[27,16,256]{2,1,0:T(8,128)(2,1)S(1)}, u32[]{:S(2)}, u32[]{:S(2)}) collective-permute-start(bf16[27,16,256]{2,1,0:T(8,128)(2,1)S(1)} %get-tuple-element.23), channel_id=1, source_target_pairs={{8,16},{16,8},{24,32},{32,24},{40,48},{48,40},{56,64},{64,56},{72,... | collective-permute-start | bytes 663560 | tf_op jit(solution)/shard_map/ppermute | solution.py:557
  9.1 10.4 %copy-start.2 = (bf16[2,4,256,256]{3,2,1,0:T(8,128)(2,1)S(1)}, bf16[2,4,256,256]{3,2,1,0:T(8,128)(2,1)}, u32[]{:S(2)}) copy-start(bf16[2,4,256,256]{3,2,1,0:T(8,128)(2,1)} %constant.11.clone.inner) | copy-start | bytes 3145732
  9.1 13.0 %collective-permute-start.2 = (bf16[320,128]{1,0:T(8,128)(2,1)S(1)}, bf16[320,128]{1,0:T(8,128)(2,1)S(1)}, u32[]{:S(2)}, u32[]{:S(2)}) collective-permute-start(bf16[320,128]{1,0:T(8,128)(2,1)S(1)} %get-tuple-element.29), channel_id=1, source_target_pairs={{0,1},{1,0},{2,3},{3,2},{4,5},{5,4},{6,7},{7,6},{8,9},{9,8},{10,11... | collective-permute-start | bytes 245768 | tf_op jit(solution)/shard_map/ppermute | solution.py:557
  10.4 11.8 %collective-permute-start.3 = (bf16[320,128]{1,0:T(8,128)(2,1)S(1)}, bf16[320,128]{1,0:T(8,128)(2,1)S(1)}, u32[]{:S(2)}, u32[]{:S(2)}) collective-permute-start(bf16[320,128]{1,0:T(8,128)(2,1)S(1)} %get-tuple-element.30), channel_id=1, source_target_pairs={{1,2},{2,1},{3,4},{4,3},{5,6},{6,5},{9,10},{10,9},{11,12},{12,11},... | collective-permute-start | bytes 245768 | tf_op jit(solution)/shard_map/ppermute | solution.py:557
  18.5 3.6 %copy-start.3 = (bf16[512,256]{1,0:T(8,128)(2,1)S(1)}, bf16[512,256]{1,0:T(8,128)(2,1)}, u32[]{:S(2)}) copy-start(bf16[512,256]{1,0:T(8,128)(2,1)} %constant.13.clone.edge_center) | copy-start | bytes 786436
  18.5 3.6 %copy-start.4 = (bf16[384,256]{1,0:T(8,128)(2,1)S(1)}, bf16[384,256]{1,0:T(8,128)(2,1)}, u32[]{:S(2)}) copy-start(bf16[384,256]{1,0:T(8,128)(2,1)} %constant.12.clone.edge) | copy-start | bytes 589828
  18.6 3.6 %copy-start.5 = (bf16[128,384]{1,0:T(8,128)(2,1)S(1)}, bf16[128,384]{1,0:T(8,128)(2,1)}, u32[]{:S(2)}) copy-start(bf16[128,384]{1,0:T(8,128)(2,1)} %constant.14.clone.scatter) | copy-start | bytes 294916
  18.6 3.6 %collective-permute-start.4 = (bf16[48,128]{1,0:T(8,128)(2,1)S(1)}, bf16[48,128]{1,0:T(8,128)(2,1)S(1)}, u32[]{:S(2)}, u32[]{:S(2)}) collective-permute-start(bf16[48,128]{1,0:T(8,128)(2,1)S(1)} %get-tuple-element.31), channel_id=1, source_target_pairs={{0,1},{1,0},{2,3},{3,2},{4,5},{5,4},{6,7},{7,6},{8,9},{9,8},{10,11... | collective-permute-start | bytes 36872 | tf_op jit(solution)/shard_map/ppermute | solution.py:557
  18.7 3.5 %collective-permute-start.5 = (bf16[48,128]{1,0:T(8,128)(2,1)S(1)}, bf16[48,128]{1,0:T(8,128)(2,1)S(1)}, u32[]{:S(2)}, u32[]{:S(2)}) collective-permute-start(bf16[48,128]{1,0:T(8,128)(2,1)S(1)} %get-tuple-element.32), channel_id=1, source_target_pairs={{1,2},{2,1},{3,4},{4,3},{5,6},{6,5},{9,10},{10,9},{11,12},{12,11},... | collective-permute-start | bytes 36872 | tf_op jit(solution)/shard_map/ppermute | solution.py:557

commit v6 on v5

--- a/solution.py
+++ b/solution.py
@@ -20,8 +20,10 @@
 SLAB = 96
 PIECES = 3
 PACKED = ANG * ROWS + 2 * PIECES * EDGE
-PAIRS = ((-4, -3), (-2, -1), (1, 2), (3, 4), (0, 0))
+PAIRS = ((-4, -3), (-2, -1), (1, 2), (3, 4))
 SHARED = len(PAIRS) * ROWS
+SENT = SHARED + PIECES * EDGE
+SPARE = ((0, 0, 18, 45), (0, 18, 12, 109), (1, 30, 15, 45))
 LANES = 128
 SMOOTH = 2.0
 DAMPING = 0.1
@@ -150,33 +152,20 @@
     return ANG * ROWS + ((0 if side == "above" else PIECES) + q) * EDGE
 
 
-def share(first_of, second_of, to_left, to_right, at):
-    low = lax.broadcasted_iota(jnp.int32, first_of.shape, 1) < 64
-    turned = pltpu.roll(second_of, 64, 1)
-    to_left[pl.ds(at, first_of.shape[0]), :] = jnp.where(low, first_of, turned).astype(
-        jnp.bfloat16
-    )
-    turned = pltpu.roll(first_of, 64, 1)
-    to_right[pl.ds(at, first_of.shape[0]), :] = jnp.where(low, turned, second_of).astype(
-        jnp.bfloat16
-    )
-
-
-def by_pair(to_left, to_right, send_pair, send_next):
-    even = is_even("col")
-
-    @pl.when(even)
-    def _():
-        send_pair[...] = to_right[...]
-        send_next[...] = to_left[...]
-
-    @pl.when(jnp.logical_not(even))
-    def _():
-        send_pair[...] = to_left[...]
-        send_next[...] = to_right[...]
-
-
-def pack_own(views, own, send_pair, send_next, pack, to_left, to_right):
+def share(first_of, second_of, to_left, to_right, at, spare=()):
+    lane = lax.broadcasted_iota(jnp.int32, first_of.shape, 1)
+    rows = pl.ds(at, first_of.shape[0])
+    for out, turn in ((to_left, 0), (to_right, 64)):
+        low = pltpu.roll(first_of, 64, 1) if turn else first_of
+        high = second_of if turn else pltpu.roll(second_of, 64, 1)
+        both = jnp.where(lane < 64, low, high)
+        for pack, start, count, there in spare:
+            moved = pltpu.roll(pack, (there - start - turn) % LANES, 1)
+            both = jnp.where((lane >= there) & (lane < there + count), moved, both)
+        out[rows, :] = both.astype(jnp.bfloat16)
+
+
+def pack_own(views, own, to_left, to_right, pack):
     column = lax.broadcasted_iota(jnp.int32, (COLS, LANES), 0)
     lane = lax.broadcasted_iota(jnp.int32, (COLS, LANES), 1)
     for t in range(-HALF, HALF + 1):
@@ -193,22 +182,23 @@
             apart = lane_here(t, 0)
             hit = jnp.where(near & (lane - column == apart), 1.0, hit)
         pack[t + HALF] = hit.astype(jnp.bfloat16)
-    for p, pair in enumerate(PAIRS):
-        both = []
-        for s in pair:
-            total = dot(views[(s + HALF) * ANG], pack[0])
-            for ti in range(1, ANG):
-                total = total + dot(views[(s + HALF) * ANG + ti], pack[ti])
-            own[(s + HALF) * ROWS : (s + HALF + 1) * ROWS, :] = total.astype(jnp.bfloat16)
-            both.append(total)
-        share(both[0], both[1], to_left, to_right, p * ROWS)
-    by_pair(to_left, to_right, send_pair, send_next)
-
-
-def pack_edges_and_left_sums(
-    views, inner, got_pair, got_next, pack, own_in,
-    data_out, source_out, above, below, own, send_pair, send_next,
-    to_left, to_right, *scratch,
+
+    def packed(s):
+        total = dot(views[(s + HALF) * ANG], pack[0])
+        for ti in range(1, ANG):
+            total = total + dot(views[(s + HALF) * ANG + ti], pack[ti])
+        own[(s + HALF) * ROWS : (s + HALF + 1) * ROWS, :] = total.astype(jnp.bfloat16)
+        return total
+
+    middle = packed(0)
+    for p, (low, high) in enumerate(PAIRS):
+        spare = [(middle, *lanes) for q, *lanes in SPARE if q == p]
+        share(packed(low), packed(high), to_left, to_right, p * ROWS, spare)
+
+
+def pack_edges(
+    got_pair, got_next, pack, own_in, left_in, right_in,
+    above, below, own, send_pair, send_next, to_left, to_right,
 ):
     even = is_even("row")
 
@@ -232,25 +222,46 @@
             own[pl.ds(packed_piece(side, q), EDGE), :] = total.astype(jnp.bfloat16)
             both.append(total)
         share(both[0], both[1], to_left, to_right, q * EDGE)
-    by_pair(to_left, to_right, send_pair, send_next)
-    edges = {"above": above, "below": below}
-    inner_sums(0, views, edges, inner, data_out, source_out, *scratch)
-
-
-def unshare(blocks, pieces, high, out):
-    def move(source, at, to, count, half):
-        rows = source[pl.ds(at, count), :]
+    even = is_even("col")
+
+    def send(out, block, piece):
+        out[:SHARED, :] = block[...]
+        out[SHARED:, :] = piece[...]
+
+    @pl.when(even)
+    def _():
+        send(send_pair, right_in, to_right)
+        send(send_next, left_in, to_left)
+
+    @pl.when(jnp.logical_not(even))
+    def _():
+        send(send_pair, left_in, to_left)
+        send(send_next, right_in, to_right)
+
+
+def unshare(source, high, out):
+    def rows_at(at, count):
+        return source[pl.ds(at, count), :].astype(F32)
+
+    def move(at, to, count, half):
+        rows = rows_at(at, count)
         if half != high:
-            rows = pltpu.roll(rows.astype(F32), 64, 1).astype(jnp.bfloat16)
-        out[pl.ds(to, count), :] = rows
+            rows = pltpu.roll(rows, 64, 1)
+        out[pl.ds(to, count), :] = rows.astype(jnp.bfloat16)
 
     for p, pair in enumerate(PAIRS):
         for half, s in enumerate(pair):
-            if s or not half:
-                move(blocks, p * ROWS, (s + HALF) * ROWS, ROWS, half)
+            move(p * ROWS, (s + HALF) * ROWS, ROWS, half)
     for q in range(PIECES):
         for half, side in enumerate(("above", "below")):
-            move(pieces, q * EDGE, packed_piece(side, q), EDGE, half)
+            move(SHARED + q * EDGE, packed_piece(side, q), EDGE, half)
+    lane = lax.broadcasted_iota(jnp.int32, (ROWS, LANES), 1)
+    middle = jnp.zeros((ROWS, LANES), F32)
+    for p, start, count, there in SPARE:
+        at = start + 64 * high
+        rows = pltpu.roll(rows_at(p * ROWS, ROWS), (at - there) % LANES, 1)
+        middle = jnp.where((lane >= at) & (lane < at + count), rows, middle)
+    out[pl.ds(HALF * ROWS, ROWS), :] = middle.astype(jnp.bfloat16)
 
 
 def first_row(s):
@@ -350,9 +361,10 @@
         lax.fori_loop(0, HALF, functools.partial(body, sign=sign), 0)
 
 
-def right_sums(views, above, below, inner, data_out, source_out, *scratch):
+def both_sums(views, above, below, left, right, data_out, source_out, *scratch):
     edges = {"above": above, "below": below}
-    inner_sums(1, views, edges, inner, data_out, source_out, *scratch)
+    for tile, inner in enumerate((left, right)):
+        inner_sums(tile, views, edges, inner, data_out.at[tile], source_out.at[tile], *scratch)
 
 
 def outer_sums(
@@ -362,14 +374,10 @@
     above,
     below,
     own,
+    got_next,
     got_pair,
-    got_next,
-    got_piece_pair,
-    got_piece_next,
-    data_left,
-    source_left,
-    data_right,
-    source_right,
+    data_in,
+    source_in,
     edge,
     edge_center,
     scatter,
@@ -389,13 +397,13 @@
 
     @pl.when(even)
     def _():
-        unshare(got_next, got_piece_next, 1, left)
-        unshare(got_pair, got_piece_pair, 0, right)
+        unshare(got_next, 1, left)
+        unshare(got_pair, 0, right)
 
     @pl.when(jnp.logical_not(even))
     def _():
-        unshare(got_pair, got_piece_pair, 1, left)
-        unshare(got_next, got_piece_next, 0, right)
+        unshare(got_pair, 1, left)
+        unshare(got_next, 0, right)
 
     edges = {"above": above, "below": below}
     zero_tails(warped)
@@ -433,10 +441,10 @@
         middle = rest.astype(jnp.bfloat16)
         low = (rest - middle.astype(F32)).astype(jnp.bfloat16)
         spread = dot(low, scatter[...]) + dot(middle, scatter[...]) + dot(high, scatter[...])
-        return jnp.concatenate([inside[0][...], inside[1][...], zero], axis=1) + spread
-
-    data_sum = total((data_left, data_right), sums[0])
-    source_sum = total((source_left, source_right), sums[1])
+        return jnp.concatenate([inside[0], inside[1], zero], axis=1) + spread
+
+    data_sum = total(data_in, sums[0])
+    source_sum = total(source_in, sums[1])
 
     wide = 3 * LANES
 
@@ -569,31 +577,27 @@
     pair = swap(pair, "row", 0)
     after = swap(after, "row", 1)
     shared = struct((SHARED, LANES), bf16)
-    room = pltpu.VMEM((SHARED, LANES), bf16)
-    own, block_pair, block_next, pack = call(
+    own, to_left, to_right, pack = call(
         pack_own,
         (struct((ANG * ROWS, LANES), bf16), shared, shared, struct((ANG, COLS, LANES), bf16)),
-        (room, room),
         name="pack_own",
     )(views)
-    block_next = swap(block_next, "col", 1)
-    block_pair = swap(block_pair, "col", 0)
+    sent = struct((SENT, LANES), bf16)
+    small = pltpu.VMEM((PIECES * EDGE, LANES), bf16)
+    above, below, own, pair, after = call(
+        pack_edges,
+        (edge, edge, struct((PACKED, LANES), bf16), sent, sent),
+        (small, small),
+        name="pack_edges",
+    )(pair, after, pack, own, to_left, to_right)
+    after = swap(after, "col", 1)
+    pair = swap(pair, "col", 0)
     slab = pltpu.VMEM((ANG, SLAB, LANES), F32)
     tile = pltpu.VMEM((OUT, LANES), F32)
-    sums = struct((OUT, LANES), F32)
-    sent = struct((PIECES * EDGE, LANES), bf16)
-    small = pltpu.VMEM((PIECES * EDGE, LANES), bf16)
-    data_left, source_left, above, below, own, piece_pair, piece_next = call(
-        pack_edges_and_left_sums,
-        (sums, sums, edge, edge, struct((PACKED, LANES), bf16), sent, sent),
-        (small, small, slab, slab, tile),
-        name="left_sums",
-    )(views, left_inner, pair, after, pack, own)
-    piece_next = swap(piece_next, "col", 1)
-    piece_pair = swap(piece_pair, "col", 0)
-    data_right, source_right = call(
-        right_sums, (sums, sums), (slab, slab, tile), name="right_sums"
-    )(views, above, below, right_inner)
+    sums = struct((2, OUT, LANES), F32)
+    data, source = call(both_sums, (sums, sums), (slab, slab, tile), name="inner_sums")(
+        views, above, below, left_inner, right_inner
+    )
     field = struct((OUT, COLS), F32)
     zed, near, nxt, precond, message = call(
         functools.partial(outer_sums, rows * ROWS, cols * COLS),
@@ -607,10 +611,7 @@
             pltpu.VMEM((PACKED, LANES), bf16),
         ),
         name="outer_sums",
-    )(
-        views, above, below, own, block_pair, block_next, piece_pair, piece_next,
-        data_left, source_left, data_right, source_right, edge_matrix, center, scatter,
-    )
+    )(views, above, below, own, after, pair, data, source, edge_matrix, center, scatter)
     n = rows * cols
     messages = lax.all_to_all(
         jnp.broadcast_to(message[None], (n, 1, LANES)), ALL, 0, 0, tiled=True

time: 59.2 us -> 55.9 us (0.944)
  blocking collectives: 34.1 us -> 30.9 us
  waiting for transfers between devices: 4.13 us -> 5.99 us
  starting transfers between devices: 8 us -> 6.29 us
    all_to_all x1, blocking collectives: 34.1 us -> 30.9 us  [shards(): lax.all_to_all(jnp.broadcast_to(message[None], (n, 1, LANES)), ALL, 0, 0,...]
    ppermute x6 -> x4, waiting for transfers between devices: 4.13 us -> 5.99 us  [swap(): return lax.ppermute(array, axis, pairs)]
    ppermute x6 -> x4, starting transfers between devices: 8 us -> 6.29 us  [swap(): return lax.ppermute(array, axis, pairs)]
    unnamed x12 -> x14, local copies, waits for them, and re-layouts: 1.77 us -> 1.77 us
  transfers between devices with their start and end apart: 6 -> 4, of which waited for: 1 -> 1; matrix products, arithmetic and copies ran while one was open for 0% -> 0% of each run, Pallas kernels for 13% -> 12%
where the time goes in v6:
time: 55.9 us; the launch traced here: 55.8 us
  blocking collectives  30.9 us (55%)
  Pallas kernels  9.98 us (18%)
  starting transfers between devices  6.29 us (11%)
  waiting for transfers between devices  5.99 us (11%)
  local copies, waits for them, and re-layouts  1.84 us (3%)
  between operations  0.77 us (1%)
    all_to_all x1, blocking collectives, shards(): lax.all_to_all(jnp.broadcast_to(message[None], (n, 1, LANES)), ALL, 0, 0,...  30.9 us
    ppermute x4, starting transfers between devices, swap(): return lax.ppermute(array, axis, pairs)  6.29 us
    ppermute x4, waiting for transfers between devices, swap(): return lax.ppermute(array, axis, pairs)  5.99 us
    pallas_call x1, Pallas kernels, shards(): call(both_sums, (sums, sums), (slab, slab, tile), name='inner_sums')  5.29 us
    unnamed x14, local copies, waits for them, and re-layouts  1.77 us
    pallas_call x1, Pallas kernels, shards(): call(functools.partial(outer_sums, rows * ROWS, cols * COLS), (field, fie...  1.56 us
    pallas_call x1, Pallas kernels, shards(): call(pack_own, (struct((ANG * ROWS, LANES), bf16), shared, shared, struct...  1.22 us
  transfers between devices with their start and end apart: 4, of which 1 were waited for; matrix products, arithmetic and copies ran while one was open for 0% of the time, Pallas kernels for 12%

profile of v6, /device:TPU:1, one launch (start us, length us, event | category | flops | bytes accessed | tf_op | source)
XLA Modules:
  0.0 55.8 jit_solution(8528107170541912572)
XLA Ops:
  0.6 0.0 copy-start
  0.6 1.7 %copy-done = bf16[81,64,256]{2,1,0:T(8,128)(2,1)S(1)} copy-done((bf16[81,64,256]{2,1,0:T(8,128)(2,1)S(1)}, bf16[81,64,256]{2,1,0:T(8,128)(2,1)}, u32[]{:S(2)}) %copy-start) | copy-done | bytes 2654232
  2.4 0.0 copy-start.3
  2.4 0.1 pack_rows.1
  2.5 0.0 copy-start.1
  2.5 0.0 copy-start.2
  2.5 3.3 %collective-permute-start = (bf16[27,16,256]{2,1,0:T(8,128)(2,1)S(1)}, bf16[27,16,256]{2,1,0:T(8,128)(2,1)S(1)}, u32[]{:S(2)}, u32[]{:S(2)}) collective-permute-start(bf16[27,16,256]{2,1,0:T(8,128)(2,1)S(1)} %get-tuple-element.20), channel_id=1, source_target_pairs={{0,8},{8,0},{16,24},{24,16},{32,40},{40,32},{48,56},{56,48},{64,72... | collective-permute-start | bytes 663560 | tf_op jit(solution)/shard_map/ppermute | solution.py:565
  5.8 2.0 %collective-permute-start.1 = (bf16[27,16,256]{2,1,0:T(8,128)(2,1)S(1)}, bf16[27,16,256]{2,1,0:T(8,128)(2,1)S(1)}, u32[]{:S(2)}, u32[]{:S(2)}) collective-permute-start(bf16[27,16,256]{2,1,0:T(8,128)(2,1)S(1)} %get-tuple-element.21), channel_id=1, source_target_pairs={{8,16},{16,8},{24,32},{32,24},{40,48},{48,40},{56,64},{64,56},{72,... | collective-permute-start | bytes 663560 | tf_op jit(solution)/shard_map/ppermute | solution.py:565
  7.8 1.2 %pack_own.1 = (bf16[576,128]{1,0:T(8,128)(2,1)S(1)}, bf16[256,128]{1,0:T(8,128)(2,1)S(1)}, bf16[256,128]{1,0:T(8,128)(2,1)S(1)}, bf16[9,256,128]{2,1,0:T(8,128)(2,1)S(1)}) custom-call(bf16[81,64,256]{2,1,0:T(8,128)(2,1)S(1)} %copy-done), custom_call_target="tpu_custom_call" | custom-call | tf_op jit(solution)/shard_map/pack_own/pallas_call | solution.py:580
  9.1 0.0 collective-permute-done.got_pair
  9.1 6.0 %collective-permute-done.1.got_next = bf16[27,16,256]{2,1,0:T(8,128)(2,1)S(1)} collective-permute-done((bf16[27,16,256]{2,1,0:T(8,128)(2,1)S(1)}, bf16[27,16,256]{2,1,0:T(8,128)(2,1)S(1)}, u32[]{:S(2)}, u32[]{:S(2)}) %collective-permute-start.1) | collective-permute-done | bytes 221216 | tf_op jit(solution)/shard_map/ppermute | solution.py:565
  15.0 0.7 %pack_edges.1 = (bf16[27,16,256]{2,1,0:T(8,128)(2,1)S(1)}, bf16[27,16,256]{2,1,0:T(8,128)(2,1)S(1)}, bf16[672,128]{1,0:T(8,128)(2,1)S(1)}, bf16[304,128]{1,0:T(8,128)(2,1)S(1)}, bf16[304,128]{1,0:T(8,128)(2,1)S(1)}) custom-call(bf16[27,16,256]{2,1,0:T(8,128)(2,1)S(1)} %collective-permute-done.got_pair, ...), custom_call_target="tpu_custom_call" | custom-call | tf_op jit(solution)/shard_map/pack_edges/pallas_call | solution.py:587
  15.7 0.0 copy-start.4
  15.7 0.0 copy-start.5
  15.7 0.0 copy-start.6
  15.8 0.8 %collective-permute-start.2 = (bf16[304,128]{1,0:T(8,128)(2,1)S(1)}, bf16[304,128]{1,0:T(8,128)(2,1)S(1)}, u32[]{:S(2)}, u32[]{:S(2)}) collective-permute-start(bf16[304,128]{1,0:T(8,128)(2,1)S(1)} %get-tuple-element.29), channel_id=1, source_target_pairs={{1,2},{2,1},{3,4},{4,3},{5,6},{6,5},{9,10},{10,9},{11,12},{12,11},... | collective-permute-start | bytes 233480 | tf_op jit(solution)/shard_map/ppermute | solution.py:565
  16.6 0.2 collective-permute-start.3
  16.8 0.0 copy-done.3
  16.8 0.0 copy-done.1
  16.8 0.0 copy-done.2
  16.8 5.3 %inner_sums.1 = (f32[2,72,128]{2,1,0:T(8,128)S(1)}, f32[2,72,128]{2,1,0:T(8,128)S(1)}) custom-call(bf16[81,64,256]{2,1,0:T(8,128)(2,1)S(1)} %copy-done.1, bf16[27,16,256]{2,1,0:T(8,128)(2,1)S(1)} %get-tuple-element.26.above, bf16[27,16,256]{2,1,0:T(8,128)(2,1)S(1)} %get-tuple-element.27.below, bf16[2,4,256,256]{3,2,1,0:T(8,128)(2,1)S(1)} %copy-done.3, ...), custom_call_target="tpu_custom_call" | custom-call | tf_op jit(solution)/shard_map/inner_sums/pallas_call | solution.py:598
  22.1 0.0 collective-permute-done.2.got_next
  22.1 0.0 collective-permute-done.3.got_pair
  22.1 0.0 copy-done.4
  22.1 0.0 copy-done.5
  22.1 0.0 copy-done.6
  22.1 1.6 %outer_sums.1 = (f32[72,256]{1,0:T(8,128)S(1)}, f32[72,256]{1,0:T(8,128)S(1)}, f32[72,256]{1,0:T(8,128)S(1)}, f32[72,256]{1,0:T(8,128)S(1)}, f32[1,128]{1,0:T(1,128)S(1)}) custom-call(bf16[81,64,256]{2,1,0:T(8,128)(2,1)S(1)} %copy-done.1, bf16[27,16,256]{2,1,0:T(8,128)(2,1)S(1)} %get-tuple-element.26.above, ...), custom_call_target="tpu_custom_call" | custom-call | tf_op jit(solution)/shard_map/outer_sums/pallas_call | solution.py:602
  23.7 0.1 broadcast_in_dim.9
  23.8 30.9 %all_to_all.5 = f32[256,1,128]{2,1,0:T(1,128)S(1)} all-to-all(f32[256,1,128]{2,1,0:T(1,128)S(1)} %broadcast_in_dim.9), channel_id=1, replica_groups=mesh['row'=32,'col'=8] {'row','col'}, dimensions={0} | all-to-all | bytes 262144 | tf_op jit(solution)/shard_map/all_to_all | solution.py:616
  54.7 1.1 %finish.1 = (f32[64,256]{1,0:T(8,128)}, f32[64,256]{1,0:T(8,128)}) custom-call(f32[256,128]{1,0:T(8,128)S(1)} %bitcast.2, f32[72,256]{1,0:T(8,128)S(1)} %get-tuple-element.34.zed_ref, f32[72,256]{1,0:T(8,128)S(1)} %get-tuple-element.35.near_ref, f32[72,256]{1,0:T(8,128)S(1)} %get-tuple-element.36.next_ref, f32[72,256]{1,0:T(8,128)S(1)} %get-tuple-element.37.precond_ref), custom_call_target="tpu_custom_call" | custom-call | tf_op jit(solution)/shard_map/finish/pallas_call | solution.py:620
Async XLA Ops:
  0.6 1.8 %copy-start = (bf16[81,64,256]{2,1,0:T(8,128)(2,1)S(1)}, bf16[81,64,256]{2,1,0:T(8,128)(2,1)}, u32[]{:S(2)}) copy-start(bf16[81,64,256]{2,1,0:T(8,128)(2,1)} %views.7) | copy-start | bytes 7962628
  2.4 14.4 %copy-start.3 = (bf16[2,4,256,256]{3,2,1,0:T(8,128)(2,1)S(1)}, bf16[2,4,256,256]{3,2,1,0:T(8,128)(2,1)}, u32[]{:S(2)}) copy-start(bf16[2,4,256,256]{3,2,1,0:T(8,128)(2,1)} %constant.10.clone.left) | copy-start | bytes 3145732
  2.5 14.3 %copy-start.1 = (bf16[81,64,256]{2,1,0:T(8,128)(2,1)S(1)}, bf16[81,64,256]{2,1,0:T(8,128)(2,1)}, u32[]{:S(2)}) copy-start(bf16[81,64,256]{2,1,0:T(8,128)(2,1)} %views.7) | copy-start | bytes 7962628
  2.5 14.3 %copy-start.2 = (bf16[2,4,256,256]{3,2,1,0:T(8,128)(2,1)S(1)}, bf16[2,4,256,256]{3,2,1,0:T(8,128)(2,1)}, u32[]{:S(2)}) copy-start(bf16[2,4,256,256]{3,2,1,0:T(8,128)(2,1)} %constant.11.clone.right) | copy-start | bytes 3145732
  2.5 6.5 %collective-permute-start = (bf16[27,16,256]{2,1,0:T(8,128)(2,1)S(1)}, bf16[27,16,256]{2,1,0:T(8,128)(2,1)S(1)}, u32[]{:S(2)}, u32[]{:S(2)}) collective-permute-start(bf16[27,16,256]{2,1,0:T(8,128)(2,1)S(1)} %get-tuple-element.20), channel_id=1, source_target_pairs={{0,8},{8,0},{16,24},{24,16},{32,40},{40,32},{48,56},{56,48},{64,72... | collective-permute-start | bytes 663560 | tf_op jit(solution)/shard_map/ppermute | solution.py:565
  5.8 9.2 %collective-permute-start.1 = (bf16[27,16,256]{2,1,0:T(8,128)(2,1)S(1)}, bf16[27,16,256]{2,1,0:T(8,128)(2,1)S(1)}, u32[]{:S(2)}, u32[]{:S(2)}) collective-permute-start(bf16[27,16,256]{2,1,0:T(8,128)(2,1)S(1)} %get-tuple-element.21), channel_id=1, source_target_pairs={{8,16},{16,8},{24,32},{32,24},{40,48},{48,40},{56,64},{64,56},{72,... | collective-permute-start | bytes 663560 | tf_op jit(solution)/shard_map/ppermute | solution.py:565
  15.7 6.3 %copy-start.4 = (bf16[512,256]{1,0:T(8,128)(2,1)S(1)}, bf16[512,256]{1,0:T(8,128)(2,1)}, u32[]{:S(2)}) copy-start(bf16[512,256]{1,0:T(8,128)(2,1)} %constant.13.clone.edge_center) | copy-start | bytes 786436
  15.7 6.4 %copy-start.5 = (bf16[384,256]{1,0:T(8,128)(2,1)S(1)}, bf16[384,256]{1,0:T(8,128)(2,1)}, u32[]{:S(2)}) copy-start(bf16[384,256]{1,0:T(8,128)(2,1)} %constant.12.clone.edge) | copy-start | bytes 589828
  15.7 6.4 %copy-start.6 = (bf16[128,384]{1,0:T(8,128)(2,1)S(1)}, bf16[128,384]{1,0:T(8,128)(2,1)}, u32[]{:S(2)}) copy-start(bf16[128,384]{1,0:T(8,128)(2,1)} %constant.14.clone.scatter) | copy-start | bytes 294916
  15.8 6.3 %collective-permute-start.2 = (bf16[304,128]{1,0:T(8,128)(2,1)S(1)}, bf16[304,128]{1,0:T(8,128)(2,1)S(1)}, u32[]{:S(2)}, u32[]{:S(2)}) collective-permute-start(bf16[304,128]{1,0:T(8,128)(2,1)S(1)} %get-tuple-element.29), channel_id=1, source_target_pairs={{1,2},{2,1},{3,4},{4,3},{5,6},{6,5},{9,10},{10,9},{11,12},{12,11},... | collective-permute-start | bytes 233480 | tf_op jit(solution)/shard_map/ppermute | solution.py:565
  16.6 5.5 %collective-permute-start.3 = (bf16[304,128]{1,0:T(8,128)(2,1)S(1)}, bf16[304,128]{1,0:T(8,128)(2,1)S(1)}, u32[]{:S(2)}, u32[]{:S(2)}) collective-permute-start(bf16[304,128]{1,0:T(8,128)(2,1)S(1)} %get-tuple-element.30), channel_id=1, source_target_pairs={{0,1},{1,0},{2,3},{3,2},{4,5},{5,4},{6,7},{7,6},{8,9},{9,8},{10,11... | collective-permute-start | bytes 233480 | tf_op jit(solution)/shard_map/ppermute | solution.py:565

commit v7 on v6

--- a/solution.py
+++ b/solution.py
@@ -22,8 +22,8 @@
 PACKED = ANG * ROWS + 2 * PIECES * EDGE
 PAIRS = ((-4, -3), (-2, -1), (1, 2), (3, 4))
 SHARED = len(PAIRS) * ROWS
-SENT = SHARED + PIECES * EDGE
-SPARE = ((0, 0, 18, 45), (0, 18, 12, 109), (1, 30, 15, 45))
+CUTS = ((0, 18), (18, 12), (30, 15))
+SPARE = tuple((p, *cut, there) for cut, (p, there) in zip(CUTS, ((0, 45), (0, 109), (1, 45))))
 LANES = 128
 SMOOTH = 2.0
 DAMPING = 0.1
@@ -150,6 +150,16 @@
 
 def packed_piece(side, q):
     return ANG * ROWS + ((0 if side == "above" else PIECES) + q) * EDGE
+
+
+def piece_places():
+    slots = ((1, 109), (2, 45), (2, 109), (3, 45), (3, 109))
+    places = {}
+    for n, (name, cut) in enumerate((name, cut) for name in PLACES for cut in CUTS):
+        p, there = slots[n % len(slots)]
+        row = p * ROWS + n // len(slots) * EDGE
+        places.setdefault(name, []).append((row, *cut, there))
+    return places
 
 
 def share(first_of, second_of, to_left, to_right, at, spare=()):
@@ -213,55 +223,63 @@
         above[...] = got_pair[...]
 
     own[: ANG * ROWS, :] = own_in[...]
-    for q in range(PIECES):
-        both = []
-        for side, ref in (("above", above), ("below", below)):
-            total = dot(ref[q * ANG], pack[0])
-            for ti in range(1, ANG):
-                total = total + dot(ref[q * ANG + ti], pack[ti])
-            own[pl.ds(packed_piece(side, q), EDGE), :] = total.astype(jnp.bfloat16)
-            both.append(total)
-        share(both[0], both[1], to_left, to_right, q * EDGE)
+    edges = {"above": above, "below": below}
+    total = jnp.zeros((len(PLACES) * EDGE, LANES), F32)
+    for ti in range(ANG):
+        rows = [edges[side][q * ANG + ti] for side, q in PLACES]
+        total = total + dot(jnp.concatenate(rows, axis=0), pack[ti])
+    parts = {}
+    places = piece_places()
+    for i, (side, q) in enumerate(PLACES):
+        piece = total[i * EDGE : (i + 1) * EDGE]
+        own[pl.ds(packed_piece(side, q), EDGE), :] = piece.astype(jnp.bfloat16)
+        for row, *lanes in places[side, q]:
+            parts.setdefault(row, []).append((piece, *lanes))
+    lane = lax.broadcasted_iota(jnp.int32, (EDGE, LANES), 1)
+    for out, block, turn in ((to_left, left_in, 0), (to_right, right_in, 64)):
+        out[...] = block[...]
+        for row, group in parts.items():
+            both = block[row : row + EDGE, :].astype(F32)
+            for piece, start, count, there in group:
+                moved = pltpu.roll(piece, (there - start - turn) % LANES, 1)
+                both = jnp.where((lane >= there) & (lane < there + count), moved, both)
+            out[row : row + EDGE, :] = both.astype(jnp.bfloat16)
     even = is_even("col")
 
-    def send(out, block, piece):
-        out[:SHARED, :] = block[...]
-        out[SHARED:, :] = piece[...]
-
     @pl.when(even)
     def _():
-        send(send_pair, right_in, to_right)
-        send(send_next, left_in, to_left)
+        send_pair[...] = to_right[...]
+        send_next[...] = to_left[...]
 
     @pl.when(jnp.logical_not(even))
     def _():
-        send(send_pair, left_in, to_left)
-        send(send_next, right_in, to_right)
+        send_pair[...] = to_left[...]
+        send_next[...] = to_right[...]
 
 
 def unshare(source, high, out):
     def rows_at(at, count):
         return source[pl.ds(at, count), :].astype(F32)
 
-    def move(at, to, count, half):
-        rows = rows_at(at, count)
-        if half != high:
-            rows = pltpu.roll(rows, 64, 1)
-        out[pl.ds(to, count), :] = rows.astype(jnp.bfloat16)
-
     for p, pair in enumerate(PAIRS):
         for half, s in enumerate(pair):
-            move(p * ROWS, (s + HALF) * ROWS, ROWS, half)
-    for q in range(PIECES):
-        for half, side in enumerate(("above", "below")):
-            move(SHARED + q * EDGE, packed_piece(side, q), EDGE, half)
-    lane = lax.broadcasted_iota(jnp.int32, (ROWS, LANES), 1)
-    middle = jnp.zeros((ROWS, LANES), F32)
-    for p, start, count, there in SPARE:
-        at = start + 64 * high
-        rows = pltpu.roll(rows_at(p * ROWS, ROWS), (at - there) % LANES, 1)
-        middle = jnp.where((lane >= at) & (lane < at + count), rows, middle)
-    out[pl.ds(HALF * ROWS, ROWS), :] = middle.astype(jnp.bfloat16)
+            rows = rows_at(p * ROWS, ROWS)
+            if half != high:
+                rows = pltpu.roll(rows, 64, 1)
+            out[pl.ds((s + HALF) * ROWS, ROWS), :] = rows.astype(jnp.bfloat16)
+
+    def join(parts, to, count):
+        lane = lax.broadcasted_iota(jnp.int32, (count, LANES), 1)
+        whole = jnp.zeros((count, LANES), F32)
+        for row, start, lanes, there in parts:
+            at = start + 64 * high
+            rows = pltpu.roll(rows_at(row, count), (at - there) % LANES, 1)
+            whole = jnp.where((lane >= at) & (lane < at + lanes), rows, whole)
+        out[pl.ds(to, count), :] = whole.astype(jnp.bfloat16)
+
+    join([(p * ROWS, *lanes) for p, *lanes in SPARE], HALF * ROWS, ROWS)
+    for (side, q), parts in piece_places().items():
+        join(parts, packed_piece(side, q), EDGE)
 
 
 def first_row(s):
@@ -582,12 +600,11 @@
         (struct((ANG * ROWS, LANES), bf16), shared, shared, struct((ANG, COLS, LANES), bf16)),
         name="pack_own",
     )(views)
-    sent = struct((SENT, LANES), bf16)
-    small = pltpu.VMEM((PIECES * EDGE, LANES), bf16)
+    room = pltpu.VMEM(shared.shape, bf16)
     above, below, own, pair, after = call(
         pack_edges,
-        (edge, edge, struct((PACKED, LANES), bf16), sent, sent),
-        (small, small),
+        (edge, edge, struct((PACKED, LANES), bf16), shared, shared),
+        (room, room),
         name="pack_edges",
     )(pair, after, pack, own, to_left, to_right)
     after = swap(after, "col", 1)

time: 55.9 us -> 55.6 us (level)
  no operation moved by 1% of the time
where the time goes in v7:
time: 55.6 us; the launch traced here: 55.4 us
  blocking collectives  30.8 us (55%)
  Pallas kernels  9.75 us (18%)
  starting transfers between devices  6.29 us (11%)
  waiting for transfers between devices  5.99 us (11%)
  local copies, waits for them, and re-layouts  1.85 us (3%)
  between operations  0.79 us (1%)
    all_to_all x1, blocking collectives, shards(): lax.all_to_all(jnp.broadcast_to(message[None], (n, 1, LANES)), ALL, 0, 0,...  30.8 us
    ppermute x4, starting transfers between devices, swap(): return lax.ppermute(array, axis, pairs)  6.29 us
    ppermute x4, waiting for transfers between devices, swap(): return lax.ppermute(array, axis, pairs)  5.99 us
    pallas_call x1, Pallas kernels, shards(): call(both_sums, (sums, sums), (slab, slab, tile), name='inner_sums')  5.29 us
    unnamed x14, local copies, waits for them, and re-layouts  1.78 us
    pallas_call x1, Pallas kernels, shards(): call(functools.partial(outer_sums, rows * ROWS, cols * COLS), (field, fie...  1.59 us
    pallas_call x1, Pallas kernels, shards(): call(pack_own, (struct((ANG * ROWS, LANES), bf16), shared, shared, struct...  1.22 us
  transfers between devices with their start and end apart: 4, of which 1 were waited for; matrix products, arithmetic and copies ran while one was open for 0% of the time, Pallas kernels for 12%

profile of v7, /device:TPU:1, one launch (start us, length us, event | category | flops | bytes accessed | tf_op | source)
XLA Modules:
  0.0 55.4 jit_solution(3764706635284569643)
XLA Ops:
  0.6 0.0 copy-start
  0.6 1.7 %copy-done = bf16[81,64,256]{2,1,0:T(8,128)(2,1)S(1)} copy-done((bf16[81,64,256]{2,1,0:T(8,128)(2,1)S(1)}, bf16[81,64,256]{2,1,0:T(8,128)(2,1)}, u32[]{:S(2)}) %copy-start) | copy-done | bytes 2654232
  2.4 0.0 copy-start.3
  2.4 0.1 pack_rows.1
  2.5 0.0 copy-start.1
  2.5 0.0 copy-start.2
  2.5 3.3 %collective-permute-start = (bf16[27,16,256]{2,1,0:T(8,128)(2,1)S(1)}, bf16[27,16,256]{2,1,0:T(8,128)(2,1)S(1)}, u32[]{:S(2)}, u32[]{:S(2)}) collective-permute-start(bf16[27,16,256]{2,1,0:T(8,128)(2,1)S(1)} %get-tuple-element.20), channel_id=1, source_target_pairs={{0,8},{8,0},{16,24},{24,16},{32,40},{40,32},{48,56},{56,48},{64,72... | collective-permute-start | bytes 663560 | tf_op jit(solution)/shard_map/ppermute | solution.py:583
  5.8 2.0 %collective-permute-start.1 = (bf16[27,16,256]{2,1,0:T(8,128)(2,1)S(1)}, bf16[27,16,256]{2,1,0:T(8,128)(2,1)S(1)}, u32[]{:S(2)}, u32[]{:S(2)}) collective-permute-start(bf16[27,16,256]{2,1,0:T(8,128)(2,1)S(1)} %get-tuple-element.21), channel_id=1, source_target_pairs={{8,16},{16,8},{24,32},{32,24},{40,48},{48,40},{56,64},{64,56},{72,... | collective-permute-start | bytes 663560 | tf_op jit(solution)/shard_map/ppermute | solution.py:583
  7.8 1.2 %pack_own.1 = (bf16[576,128]{1,0:T(8,128)(2,1)S(1)}, bf16[256,128]{1,0:T(8,128)(2,1)S(1)}, bf16[256,128]{1,0:T(8,128)(2,1)S(1)}, bf16[9,256,128]{2,1,0:T(8,128)(2,1)S(1)}) custom-call(bf16[81,64,256]{2,1,0:T(8,128)(2,1)S(1)} %copy-done), custom_call_target="tpu_custom_call" | custom-call | tf_op jit(solution)/shard_map/pack_own/pallas_call | solution.py:598
  9.1 0.0 collective-permute-done.got_pair
  9.1 6.0 %collective-permute-done.1.got_next = bf16[27,16,256]{2,1,0:T(8,128)(2,1)S(1)} collective-permute-done((bf16[27,16,256]{2,1,0:T(8,128)(2,1)S(1)}, bf16[27,16,256]{2,1,0:T(8,128)(2,1)S(1)}, u32[]{:S(2)}, u32[]{:S(2)}) %collective-permute-start.1) | collective-permute-done | bytes 221216 | tf_op jit(solution)/shard_map/ppermute | solution.py:583
  15.0 0.4 pack_edges.1
  15.5 0.0 copy-start.4
  15.5 0.0 copy-start.5
  15.5 0.0 copy-start.6
  15.5 0.8 %collective-permute-start.2 = (bf16[256,128]{1,0:T(8,128)(2,1)S(1)}, bf16[256,128]{1,0:T(8,128)(2,1)S(1)}, u32[]{:S(2)}, u32[]{:S(2)}) collective-permute-start(bf16[256,128]{1,0:T(8,128)(2,1)S(1)} %get-tuple-element.29), channel_id=1, source_target_pairs={{1,2},{2,1},{3,4},{4,3},{5,6},{6,5},{9,10},{10,9},{11,12},{12,11},... | collective-permute-start | bytes 196616 | tf_op jit(solution)/shard_map/ppermute | solution.py:583
  16.3 0.2 collective-permute-start.3
  16.5 0.0 copy-done.3
  16.5 0.0 copy-done.1
  16.5 0.0 copy-done.2
  16.5 5.3 %inner_sums.1 = (f32[2,72,128]{2,1,0:T(8,128)S(1)}, f32[2,72,128]{2,1,0:T(8,128)S(1)}) custom-call(bf16[81,64,256]{2,1,0:T(8,128)(2,1)S(1)} %copy-done.1, bf16[27,16,256]{2,1,0:T(8,128)(2,1)S(1)} %get-tuple-element.26.above, bf16[27,16,256]{2,1,0:T(8,128)(2,1)S(1)} %get-tuple-element.27.below, bf16[2,4,256,256]{3,2,1,0:T(8,128)(2,1)S(1)} %copy-done.3, ...), custom_call_target="tpu_custom_call" | custom-call | tf_op jit(solution)/shard_map/inner_sums/pallas_call | solution.py:615
  21.8 0.0 collective-permute-done.2.got_next
  21.8 0.0 collective-permute-done.3.got_pair
  21.8 0.0 copy-done.4
  21.9 0.0 copy-done.5
  21.9 0.0 copy-done.6
  21.9 1.6 %outer_sums.1 = (f32[72,256]{1,0:T(8,128)S(1)}, f32[72,256]{1,0:T(8,128)S(1)}, f32[72,256]{1,0:T(8,128)S(1)}, f32[72,256]{1,0:T(8,128)S(1)}, f32[1,128]{1,0:T(1,128)S(1)}) custom-call(bf16[81,64,256]{2,1,0:T(8,128)(2,1)S(1)} %copy-done.1, bf16[27,16,256]{2,1,0:T(8,128)(2,1)S(1)} %get-tuple-element.26.above, ...), custom_call_target="tpu_custom_call" | custom-call | tf_op jit(solution)/shard_map/outer_sums/pallas_call | solution.py:619
  23.5 0.1 broadcast_in_dim.9
  23.6 30.8 %all_to_all.5 = f32[256,1,128]{2,1,0:T(1,128)S(1)} all-to-all(f32[256,1,128]{2,1,0:T(1,128)S(1)} %broadcast_in_dim.9), channel_id=1, replica_groups=mesh['row'=32,'col'=8] {'row','col'}, dimensions={0} | all-to-all | bytes 262144 | tf_op jit(solution)/shard_map/all_to_all | solution.py:633
  54.3 1.1 %finish.1 = (f32[64,256]{1,0:T(8,128)}, f32[64,256]{1,0:T(8,128)}) custom-call(f32[256,128]{1,0:T(8,128)S(1)} %bitcast.2, f32[72,256]{1,0:T(8,128)S(1)} %get-tuple-element.34.zed_ref, f32[72,256]{1,0:T(8,128)S(1)} %get-tuple-element.35.near_ref, f32[72,256]{1,0:T(8,128)S(1)} %get-tuple-element.36.next_ref, f32[72,256]{1,0:T(8,128)S(1)} %get-tuple-element.37.precond_ref), custom_call_target="tpu_custom_call" | custom-call | tf_op jit(solution)/shard_map/finish/pallas_call | solution.py:637
Async XLA Ops:
  0.6 1.8 %copy-start = (bf16[81,64,256]{2,1,0:T(8,128)(2,1)S(1)}, bf16[81,64,256]{2,1,0:T(8,128)(2,1)}, u32[]{:S(2)}) copy-start(bf16[81,64,256]{2,1,0:T(8,128)(2,1)} %views.7) | copy-start | bytes 7962628
  2.4 14.1 %copy-start.3 = (bf16[2,4,256,256]{3,2,1,0:T(8,128)(2,1)S(1)}, bf16[2,4,256,256]{3,2,1,0:T(8,128)(2,1)}, u32[]{:S(2)}) copy-start(bf16[2,4,256,256]{3,2,1,0:T(8,128)(2,1)} %constant.10.clone.left) | copy-start | bytes 3145732
  2.5 14.0 %copy-start.1 = (bf16[81,64,256]{2,1,0:T(8,128)(2,1)S(1)}, bf16[81,64,256]{2,1,0:T(8,128)(2,1)}, u32[]{:S(2)}) copy-start(bf16[81,64,256]{2,1,0:T(8,128)(2,1)} %views.7) | copy-start | bytes 7962628
  2.5 14.0 %copy-start.2 = (bf16[2,4,256,256]{3,2,1,0:T(8,128)(2,1)S(1)}, bf16[2,4,256,256]{3,2,1,0:T(8,128)(2,1)}, u32[]{:S(2)}) copy-start(bf16[2,4,256,256]{3,2,1,0:T(8,128)(2,1)} %constant.11.clone.right) | copy-start | bytes 3145732
  2.5 6.5 %collective-permute-start = (bf16[27,16,256]{2,1,0:T(8,128)(2,1)S(1)}, bf16[27,16,256]{2,1,0:T(8,128)(2,1)S(1)}, u32[]{:S(2)}, u32[]{:S(2)}) collective-permute-start(bf16[27,16,256]{2,1,0:T(8,128)(2,1)S(1)} %get-tuple-element.20), channel_id=1, source_target_pairs={{0,8},{8,0},{16,24},{24,16},{32,40},{40,32},{48,56},{56,48},{64,72... | collective-permute-start | bytes 663560 | tf_op jit(solution)/shard_map/ppermute | solution.py:583
  5.8 9.2 %collective-permute-start.1 = (bf16[27,16,256]{2,1,0:T(8,128)(2,1)S(1)}, bf16[27,16,256]{2,1,0:T(8,128)(2,1)S(1)}, u32[]{:S(2)}, u32[]{:S(2)}) collective-permute-start(bf16[27,16,256]{2,1,0:T(8,128)(2,1)S(1)} %get-tuple-element.21), channel_id=1, source_target_pairs={{8,16},{16,8},{24,32},{32,24},{40,48},{48,40},{56,64},{64,56},{72,... | collective-permute-start | bytes 663560 | tf_op jit(solution)/shard_map/ppermute | solution.py:583
  15.5 6.4 %copy-start.4 = (bf16[512,256]{1,0:T(8,128)(2,1)S(1)}, bf16[512,256]{1,0:T(8,128)(2,1)}, u32[]{:S(2)}) copy-start(bf16[512,256]{1,0:T(8,128)(2,1)} %constant.13.clone.edge_center) | copy-start | bytes 786436
  15.5 6.4 %copy-start.5 = (bf16[384,256]{1,0:T(8,128)(2,1)S(1)}, bf16[384,256]{1,0:T(8,128)(2,1)}, u32[]{:S(2)}) copy-start(bf16[384,256]{1,0:T(8,128)(2,1)} %constant.12.clone.edge) | copy-start | bytes 589828
  15.5 6.4 %copy-start.6 = (bf16[128,384]{1,0:T(8,128)(2,1)S(1)}, bf16[128,384]{1,0:T(8,128)(2,1)}, u32[]{:S(2)}) copy-start(bf16[128,384]{1,0:T(8,128)(2,1)} %constant.14.clone.scatter) | copy-start | bytes 294916
  15.5 6.3 %collective-permute-start.2 = (bf16[256,128]{1,0:T(8,128)(2,1)S(1)}, bf16[256,128]{1,0:T(8,128)(2,1)S(1)}, u32[]{:S(2)}, u32[]{:S(2)}) collective-permute-start(bf16[256,128]{1,0:T(8,128)(2,1)S(1)} %get-tuple-element.29), channel_id=1, source_target_pairs={{1,2},{2,1},{3,4},{4,3},{5,6},{6,5},{9,10},{10,9},{11,12},{12,11},... | collective-permute-start | bytes 196616 | tf_op jit(solution)/shard_map/ppermute | solution.py:583
  16.3 5.5 %collective-permute-start.3 = (bf16[256,128]{1,0:T(8,128)(2,1)S(1)}, bf16[256,128]{1,0:T(8,128)(2,1)S(1)}, u32[]{:S(2)}, u32[]{:S(2)}) collective-permute-start(bf16[256,128]{1,0:T(8,128)(2,1)S(1)} %get-tuple-element.30), channel_id=1, source_target_pairs={{0,1},{1,0},{2,3},{3,2},{4,5},{5,4},{6,7},{7,6},{8,9},{9,8},{10,11... | collective-permute-start | bytes 196616 | tf_op jit(solution)/shard_map/ppermute | solution.py:583

commit v8 on v7

--- a/solution.py
+++ b/solution.py
@@ -106,36 +106,50 @@
     return lax.rem(lax.axis_index(axis), 2) == 0
 
 
-def pack_rows(views, send_pair, send_next, ups_out, downs_out):
+def pack_rows(views, send_pair, send_next, tops, bottoms, ups, downs, sems):
+    count = (HALF + 1) * ANG
+    get_tops = pltpu.make_async_copy(
+        views.at[pl.ds(HALF * ANG, count), pl.ds(0, EDGE)], tops, sems.at[0]
+    )
+    get_bottoms = pltpu.make_async_copy(
+        views.at[pl.ds(0, count), pl.ds(ROWS - EDGE, EDGE)], bottoms, sems.at[1]
+    )
+    get_tops.start()
+    get_bottoms.start()
+    index = lax.broadcasted_iota(jnp.int32, (EDGE, COLS), 0)
+
+    def put(out, q, ti, rows):
+        out[q * ANG + ti] = rows.astype(jnp.bfloat16)
+
+    get_tops.wait()
+    for ti in range(ANG):
+
+        def first(s, ti=ti):
+            return tops[s * ANG + ti].astype(F32)
+
+        put(ups, 0, ti, first(4))
+        put(ups, 1, ti, jnp.where(index < 12, first(3), pltpu.roll(first(0), 12, 0)))
+        put(ups, 2, ti, jnp.where(index < 9, first(2), pltpu.roll(first(1), 9, 0)))
+    get_bottoms.wait()
+    for ti in range(ANG):
+
+        def last(s, ti=ti):
+            return bottoms[(s + HALF) * ANG + ti].astype(F32)
+
+        put(downs, 0, ti, last(-4))
+        put(downs, 1, ti, jnp.where(index < 4, pltpu.roll(last(0), 4, 0), last(-3)))
+        put(downs, 2, ti, jnp.where(index < 7, pltpu.roll(last(-1), 7, 0), last(-2)))
     even = is_even("row")
-    index = lax.broadcasted_iota(jnp.int32, (EDGE, COLS), 0)
-
-    def put(ups, q, ti, rows):
-        (ups_out if ups else downs_out)[q * ANG + ti] = rows.astype(jnp.bfloat16)
-
-    for ti in range(ANG):
-
-        def rows_of(s, start, ti=ti):
-            return views[(s + HALF) * ANG + ti, pl.ds(start, EDGE), :].astype(F32)
-
-        first = functools.partial(rows_of, start=0)
-        last = functools.partial(rows_of, start=ROWS - EDGE)
-        put(True, 0, ti, first(4))
-        put(True, 1, ti, jnp.where(index < 12, first(3), pltpu.roll(first(0), 12, 0)))
-        put(True, 2, ti, jnp.where(index < 9, first(2), pltpu.roll(first(1), 9, 0)))
-        put(False, 0, ti, last(-4))
-        put(False, 1, ti, jnp.where(index < 4, pltpu.roll(last(0), 4, 0), last(-3)))
-        put(False, 2, ti, jnp.where(index < 7, pltpu.roll(last(-1), 7, 0), last(-2)))
 
     @pl.when(even)
     def _():
-        send_pair[...] = downs_out[...]
-        send_next[...] = ups_out[...]
+        send_pair[...] = downs[...]
+        send_next[...] = ups[...]
 
     @pl.when(jnp.logical_not(even))
     def _():
-        send_pair[...] = ups_out[...]
-        send_next[...] = downs_out[...]
+        send_pair[...] = ups[...]
+        send_next[...] = downs[...]
 
 
 PLACES = {
@@ -453,16 +467,20 @@
         side,
     )
 
-    def total(inside, x):
-        high = x.astype(jnp.bfloat16)
-        rest = x - high.astype(F32)
-        middle = rest.astype(jnp.bfloat16)
-        low = (rest - middle.astype(F32)).astype(jnp.bfloat16)
-        spread = dot(low, scatter[...]) + dot(middle, scatter[...]) + dot(high, scatter[...])
-        return jnp.concatenate([inside[0], inside[1], zero], axis=1) + spread
-
-    data_sum = total(data_in, sums[0])
-    source_sum = total(source_in, sums[1])
+    parts = []
+    for x in sums:
+        for _ in range(3):
+            part = x.astype(jnp.bfloat16)
+            parts.append(part)
+            x = x - part.astype(F32)
+    spread = dot(jnp.concatenate(parts, axis=0), scatter[...])
+
+    def total(inside, at):
+        high, middle, low = (spread[(at + i) * OUT : (at + i + 1) * OUT] for i in range(3))
+        return jnp.concatenate([inside[0], inside[1], zero], axis=1) + ((low + middle) + high)
+
+    data_sum = total(data_in, 0)
+    source_sum = total(source_in, 3)
 
     wide = 3 * LANES
 
@@ -566,13 +584,14 @@
     )
 
 
-def call(kernel, outs, scratch=(), name=None):
+def call(kernel, outs, scratch=(), name=None, vmem=24, **more):
     return pl.pallas_call(
         kernel,
         out_shape=outs,
         scratch_shapes=list(scratch),
-        compiler_params=pltpu.CompilerParams(vmem_limit_bytes=24 * 1024 * 1024),
+        compiler_params=pltpu.CompilerParams(vmem_limit_bytes=vmem * 1024 * 1024),
         name=name,
+        **more,
     )
 
 
@@ -591,7 +610,15 @@
 
     edge = struct((PIECES * ANG, EDGE, COLS), bf16)
     room = pltpu.VMEM(edge.shape, bf16)
-    pair, after = call(pack_rows, (edge, edge), (room, room), name="pack_rows")(views)
+    taken = pltpu.VMEM(((HALF + 1) * ANG, EDGE, COLS), bf16)
+    pair, after = call(
+        pack_rows,
+        (edge, edge),
+        (taken, taken, room, room, pltpu.SemaphoreType.DMA((2,))),
+        name="pack_rows",
+        vmem=62,
+        in_specs=[pl.BlockSpec(memory_space=pltpu.HBM)],
+    )(views)
     pair = swap(pair, "row", 0)
     after = swap(after, "row", 1)
     shared = struct((SHARED, LANES), bf16)

time: 55.6 us -> 55.8 us (level)
  Pallas kernels: 9.75 us -> 11.6 us
  waiting for transfers between devices: 5.99 us -> 4.63 us
    pallas_call x1, Pallas kernels: 0.11 us -> 2.04 us  [shards(): call(pack_rows, (edge, edge), (taken, taken, room, room, pltpu.SemaphoreT...]
    ppermute x4, waiting for transfers between devices: 5.99 us -> 4.63 us  [swap(): return lax.ppermute(array, axis, pairs)]
where the time goes in v8:
time: 55.8 us; the launch traced here: 55.6 us
  blocking collectives  30.6 us (55%)
  Pallas kernels  11.6 us (21%)
  starting transfers between devices  6.12 us (11%)
  waiting for transfers between devices  4.63 us (8%)
  local copies, waits for them, and re-layouts  1.85 us (3%)
  between operations  0.81 us (1%)
    all_to_all x1, blocking collectives, shards(): lax.all_to_all(jnp.broadcast_to(message[None], (n, 1, LANES)), ALL, 0, 0,...  30.6 us
    ppermute x4, starting transfers between devices, swap(): return lax.ppermute(array, axis, pairs)  6.12 us
    pallas_call x1, Pallas kernels, shards(): call(both_sums, (sums, sums), (slab, slab, tile), name='inner_sums')  5.3 us
    ppermute x4, waiting for transfers between devices, swap(): return lax.ppermute(array, axis, pairs)  4.63 us
    pallas_call x1, Pallas kernels, shards(): call(pack_rows, (edge, edge), (taken, taken, room, room, pltpu.SemaphoreT...  2.04 us
    unnamed x14, local copies, waits for them, and re-layouts  1.78 us
    pallas_call x1, Pallas kernels, shards(): call(functools.partial(outer_sums, rows * ROWS, cols * COLS), (field, fie...  1.54 us
    pallas_call x1, Pallas kernels, shards(): call(pack_own, (struct((ANG * ROWS, LANES), bf16), shared, shared, struct...  1.22 us
  transfers between devices with their start and end apart: 4, of which 1 were waited for; matrix products, arithmetic and copies ran while one was open for 0% of the time, Pallas kernels for 12%

profile of v8, /device:TPU:1, one launch (start us, length us, event | category | flops | bytes accessed | tf_op | source)
XLA Modules:
  0.0 55.6 jit_solution(8945603391236436986)
XLA Ops:
  0.6 0.0 copy-start.2
  0.6 2.0 %pack_rows.1 = (bf16[27,16,256]{2,1,0:T(8,128)(2,1)}, bf16[27,16,256]{2,1,0:T(8,128)(2,1)}) custom-call(bf16[81,64,256]{2,1,0:T(8,128)(2,1)} %views.7), custom_call_target="tpu_custom_call" | custom-call | tf_op jit(solution)/shard_map/pack_rows/pallas_call | solution.py:614
  2.7 3.3 %collective-permute-start = (bf16[27,16,256]{2,1,0:T(8,128)(2,1)}, bf16[27,16,256]{2,1,0:T(8,128)(2,1)S(1)}, u32[]{:S(2)}, u32[]{:S(2)}) collective-permute-start(bf16[27,16,256]{2,1,0:T(8,128)(2,1)} %get-tuple-element.20), channel_id=1, source_target_pairs={{0,8},{8,0},{16,24},{24,16},{32,40},{40,32},{48,56},{56,48},{64,72... | collective-permute-start | bytes 663560 | tf_op jit(solution)/shard_map/ppermute | solution.py:602
  6.0 1.9 %collective-permute-start.1 = (bf16[27,16,256]{2,1,0:T(8,128)(2,1)}, bf16[27,16,256]{2,1,0:T(8,128)(2,1)S(1)}, u32[]{:S(2)}, u32[]{:S(2)}) collective-permute-start(bf16[27,16,256]{2,1,0:T(8,128)(2,1)} %get-tuple-element.21), channel_id=1, source_target_pairs={{8,16},{16,8},{24,32},{32,24},{40,48},{48,40},{56,64},{64,56},{72,... | collective-permute-start | bytes 663560 | tf_op jit(solution)/shard_map/ppermute | solution.py:602
  7.9 0.0 copy-start
  7.9 1.7 %copy-done = bf16[81,64,256]{2,1,0:T(8,128)(2,1)S(1)} copy-done((bf16[81,64,256]{2,1,0:T(8,128)(2,1)S(1)}, bf16[81,64,256]{2,1,0:T(8,128)(2,1)}, u32[]{:S(2)}) %copy-start) | copy-done | bytes 2654232
  9.7 0.0 copy-start.1
  9.7 0.0 copy-start.3
  9.7 1.2 %pack_own.1 = (bf16[576,128]{1,0:T(8,128)(2,1)S(1)}, bf16[256,128]{1,0:T(8,128)(2,1)S(1)}, bf16[256,128]{1,0:T(8,128)(2,1)S(1)}, bf16[9,256,128]{2,1,0:T(8,128)(2,1)S(1)}) custom-call(bf16[81,64,256]{2,1,0:T(8,128)(2,1)S(1)} %copy-done), custom_call_target="tpu_custom_call" | custom-call | tf_op jit(solution)/shard_map/pack_own/pallas_call | solution.py:625
  10.9 0.0 collective-permute-done.got_pair
  10.9 4.6 %collective-permute-done.1.got_next = bf16[27,16,256]{2,1,0:T(8,128)(2,1)S(1)} collective-permute-done((bf16[27,16,256]{2,1,0:T(8,128)(2,1)}, bf16[27,16,256]{2,1,0:T(8,128)(2,1)S(1)}, u32[]{:S(2)}, u32[]{:S(2)}) %collective-permute-start.1) | collective-permute-done | bytes 221216 | tf_op jit(solution)/shard_map/ppermute | solution.py:602
  15.6 0.4 pack_edges.1
  16.0 0.0 copy-start.4
  16.0 0.0 copy-start.5
  16.0 0.0 copy-start.6
  16.0 0.8 %collective-permute-start.2 = (bf16[256,128]{1,0:T(8,128)(2,1)S(1)}, bf16[256,128]{1,0:T(8,128)(2,1)S(1)}, u32[]{:S(2)}, u32[]{:S(2)}) collective-permute-start(bf16[256,128]{1,0:T(8,128)(2,1)S(1)} %get-tuple-element.29), channel_id=1, source_target_pairs={{1,2},{2,1},{3,4},{4,3},{5,6},{6,5},{9,10},{10,9},{11,12},{12,11},... | collective-permute-start | bytes 196616 | tf_op jit(solution)/shard_map/ppermute | solution.py:602
  16.8 0.1 collective-permute-start.3
  16.9 0.0 copy-done.2
  16.9 0.0 copy-done.1
  17.0 0.0 copy-done.3
  17.0 5.3 %inner_sums.1 = (f32[2,72,128]{2,1,0:T(8,128)S(1)}, f32[2,72,128]{2,1,0:T(8,128)S(1)}) custom-call(bf16[81,64,256]{2,1,0:T(8,128)(2,1)S(1)} %copy-done.1, bf16[27,16,256]{2,1,0:T(8,128)(2,1)S(1)} %get-tuple-element.26.above, bf16[27,16,256]{2,1,0:T(8,128)(2,1)S(1)} %get-tuple-element.27.below, bf16[2,4,256,256]{3,2,1,0:T(8,128)(2,1)S(1)} %copy-done.3, ...), custom_call_target="tpu_custom_call" | custom-call | tf_op jit(solution)/shard_map/inner_sums/pallas_call | solution.py:642
  22.3 0.0 collective-permute-done.2.got_next
  22.3 0.0 collective-permute-done.3.got_pair
  22.3 0.0 copy-done.4
  22.3 0.0 copy-done.5
  22.3 0.0 copy-done.6
  22.3 1.5 %outer_sums.1 = (f32[72,256]{1,0:T(8,128)S(1)}, f32[72,256]{1,0:T(8,128)S(1)}, f32[72,256]{1,0:T(8,128)S(1)}, f32[72,256]{1,0:T(8,128)S(1)}, f32[1,128]{1,0:T(1,128)S(1)}) custom-call(bf16[81,64,256]{2,1,0:T(8,128)(2,1)S(1)} %copy-done.1, bf16[27,16,256]{2,1,0:T(8,128)(2,1)S(1)} %get-tuple-element.26.above, ...), custom_call_target="tpu_custom_call" | custom-call | tf_op jit(solution)/shard_map/outer_sums/pallas_call | solution.py:646
  23.9 0.1 broadcast_in_dim.9
  23.9 30.6 %all_to_all.5 = f32[256,1,128]{2,1,0:T(1,128)S(1)} all-to-all(f32[256,1,128]{2,1,0:T(1,128)S(1)} %broadcast_in_dim.9), channel_id=1, replica_groups=mesh['row'=32,'col'=8] {'row','col'}, dimensions={0} | all-to-all | bytes 262144 | tf_op jit(solution)/shard_map/all_to_all | solution.py:660
  54.5 1.1 %finish.1 = (f32[64,256]{1,0:T(8,128)}, f32[64,256]{1,0:T(8,128)}) custom-call(f32[256,128]{1,0:T(8,128)S(1)} %bitcast.2, f32[72,256]{1,0:T(8,128)S(1)} %get-tuple-element.34.zed_ref, f32[72,256]{1,0:T(8,128)S(1)} %get-tuple-element.35.near_ref, f32[72,256]{1,0:T(8,128)S(1)} %get-tuple-element.36.next_ref, f32[72,256]{1,0:T(8,128)S(1)} %get-tuple-element.37.precond_ref), custom_call_target="tpu_custom_call" | custom-call | tf_op jit(solution)/shard_map/finish/pallas_call | solution.py:664
Async XLA Ops:
  0.6 16.3 %copy-start.2 = (bf16[2,4,256,256]{3,2,1,0:T(8,128)(2,1)S(1)}, bf16[2,4,256,256]{3,2,1,0:T(8,128)(2,1)}, u32[]{:S(2)}) copy-start(bf16[2,4,256,256]{3,2,1,0:T(8,128)(2,1)} %constant.11.clone.right) | copy-start | bytes 3145732
  2.7 8.2 %collective-permute-start = (bf16[27,16,256]{2,1,0:T(8,128)(2,1)}, bf16[27,16,256]{2,1,0:T(8,128)(2,1)S(1)}, u32[]{:S(2)}, u32[]{:S(2)}) collective-permute-start(bf16[27,16,256]{2,1,0:T(8,128)(2,1)} %get-tuple-element.20), channel_id=1, source_target_pairs={{0,8},{8,0},{16,24},{24,16},{32,40},{40,32},{48,56},{56,48},{64,72... | collective-permute-start | bytes 663560 | tf_op jit(solution)/shard_map/ppermute | solution.py:602
  6.0 9.5 %collective-permute-start.1 = (bf16[27,16,256]{2,1,0:T(8,128)(2,1)}, bf16[27,16,256]{2,1,0:T(8,128)(2,1)S(1)}, u32[]{:S(2)}, u32[]{:S(2)}) collective-permute-start(bf16[27,16,256]{2,1,0:T(8,128)(2,1)} %get-tuple-element.21), channel_id=1, source_target_pairs={{8,16},{16,8},{24,32},{32,24},{40,48},{48,40},{56,64},{64,56},{72,... | collective-permute-start | bytes 663560 | tf_op jit(solution)/shard_map/ppermute | solution.py:602
  7.9 1.8 %copy-start = (bf16[81,64,256]{2,1,0:T(8,128)(2,1)S(1)}, bf16[81,64,256]{2,1,0:T(8,128)(2,1)}, u32[]{:S(2)}) copy-start(bf16[81,64,256]{2,1,0:T(8,128)(2,1)} %views.7) | copy-start | bytes 7962628
  9.7 7.3 %copy-start.1 = (bf16[81,64,256]{2,1,0:T(8,128)(2,1)S(1)}, bf16[81,64,256]{2,1,0:T(8,128)(2,1)}, u32[]{:S(2)}) copy-start(bf16[81,64,256]{2,1,0:T(8,128)(2,1)} %views.7) | copy-start | bytes 7962628
  9.7 7.3 %copy-start.3 = (bf16[2,4,256,256]{3,2,1,0:T(8,128)(2,1)S(1)}, bf16[2,4,256,256]{3,2,1,0:T(8,128)(2,1)}, u32[]{:S(2)}) copy-start(bf16[2,4,256,256]{3,2,1,0:T(8,128)(2,1)} %constant.10.clone.left) | copy-start | bytes 3145732
  16.0 6.3 %copy-start.4 = (bf16[512,256]{1,0:T(8,128)(2,1)S(1)}, bf16[512,256]{1,0:T(8,128)(2,1)}, u32[]{:S(2)}) copy-start(bf16[512,256]{1,0:T(8,128)(2,1)} %constant.13.clone.edge_center) | copy-start | bytes 786436
  16.0 6.3 %copy-start.5 = (bf16[384,256]{1,0:T(8,128)(2,1)S(1)}, bf16[384,256]{1,0:T(8,128)(2,1)}, u32[]{:S(2)}) copy-start(bf16[384,256]{1,0:T(8,128)(2,1)} %constant.12.clone.edge) | copy-start | bytes 589828
  16.0 6.3 %copy-start.6 = (bf16[128,384]{1,0:T(8,128)(2,1)S(1)}, bf16[128,384]{1,0:T(8,128)(2,1)}, u32[]{:S(2)}) copy-start(bf16[128,384]{1,0:T(8,128)(2,1)} %constant.14.clone.scatter) | copy-start | bytes 294916
  16.0 6.2 %collective-permute-start.2 = (bf16[256,128]{1,0:T(8,128)(2,1)S(1)}, bf16[256,128]{1,0:T(8,128)(2,1)S(1)}, u32[]{:S(2)}, u32[]{:S(2)}) collective-permute-start(bf16[256,128]{1,0:T(8,128)(2,1)S(1)} %get-tuple-element.29), channel_id=1, source_target_pairs={{1,2},{2,1},{3,4},{4,3},{5,6},{6,5},{9,10},{10,9},{11,12},{12,11},... | collective-permute-start | bytes 196616 | tf_op jit(solution)/shard_map/ppermute | solution.py:602
  16.8 5.4 %collective-permute-start.3 = (bf16[256,128]{1,0:T(8,128)(2,1)S(1)}, bf16[256,128]{1,0:T(8,128)(2,1)S(1)}, u32[]{:S(2)}, u32[]{:S(2)}) collective-permute-start(bf16[256,128]{1,0:T(8,128)(2,1)S(1)} %get-tuple-element.30), channel_id=1, source_target_pairs={{0,1},{1,0},{2,3},{3,2},{4,5},{5,4},{6,7},{7,6},{8,9},{9,8},{10,11... | collective-permute-start | bytes 196616 | tf_op jit(solution)/shard_map/ppermute | solution.py:602

commit v9 on v7

--- a/solution.py
+++ b/solution.py
@@ -7,6 +7,7 @@
 from jax import lax
 from jax.experimental import pallas as pl
 from jax.experimental.pallas import tpu as pltpu
+from jax.sharding import Mesh
 from jax.sharding import PartitionSpec as P
 
 ANG = 9
@@ -27,7 +28,8 @@
 LANES = 128
 SMOOTH = 2.0
 DAMPING = 0.1
-ALL = ("row", "col")
+ROW = ("chip", "core")
+COL = "col"
 F32 = jnp.float32
 
 
@@ -107,7 +109,7 @@
 
 
 def pack_rows(views, send_pair, send_next, ups_out, downs_out):
-    even = is_even("row")
+    even = is_even(ROW)
     index = lax.broadcasted_iota(jnp.int32, (EDGE, COLS), 0)
 
     def put(ups, q, ti, rows):
@@ -210,7 +212,7 @@
     got_pair, got_next, pack, own_in, left_in, right_in,
     above, below, own, send_pair, send_next, to_left, to_right,
 ):
-    even = is_even("row")
+    even = is_even(ROW)
 
     @pl.when(even)
     def _():
@@ -244,7 +246,7 @@
                 moved = pltpu.roll(piece, (there - start - turn) % LANES, 1)
                 both = jnp.where((lane >= there) & (lane < there + count), moved, both)
             out[row : row + EDGE, :] = both.astype(jnp.bfloat16)
-    even = is_even("col")
+    even = is_even(COL)
 
     @pl.when(even)
     def _():
@@ -411,7 +413,7 @@
     left,
     right,
 ):
-    even = is_even("col")
+    even = is_even(COL)
 
     @pl.when(even)
     def _():
@@ -453,16 +455,20 @@
         side,
     )
 
-    def total(inside, x):
-        high = x.astype(jnp.bfloat16)
-        rest = x - high.astype(F32)
-        middle = rest.astype(jnp.bfloat16)
-        low = (rest - middle.astype(F32)).astype(jnp.bfloat16)
-        spread = dot(low, scatter[...]) + dot(middle, scatter[...]) + dot(high, scatter[...])
-        return jnp.concatenate([inside[0], inside[1], zero], axis=1) + spread
-
-    data_sum = total(data_in, sums[0])
-    source_sum = total(source_in, sums[1])
+    parts = []
+    for x in sums:
+        for _ in range(3):
+            part = x.astype(jnp.bfloat16)
+            parts.append(part)
+            x = x - part.astype(F32)
+    spread = dot(jnp.concatenate(parts, axis=0), scatter[...])
+
+    def total(inside, at):
+        high, middle, low = (spread[(at + i) * OUT : (at + i + 1) * OUT] for i in range(3))
+        return jnp.concatenate([inside[0], inside[1], zero], axis=1) + ((low + middle) + high)
+
+    data_sum = total(data_in, 0)
+    source_sum = total(source_in, 3)
 
     wide = 3 * LANES
 
@@ -483,8 +489,8 @@
     higher = jnp.concatenate([center_slab[i, pl.ds(at - 1, OUT), :] for i in range(3)], axis=1)
     lane = lax.broadcasted_iota(jnp.int32, (OUT, wide), 1)
     local_row = lax.broadcasted_iota(jnp.int32, (OUT, wide), 0) - 2
-    column = jnp.where(lane < wide - 64, lane, lane - wide) + lax.axis_index("col") * COLS
-    row = local_row + lax.axis_index("row") * ROWS
+    column = jnp.where(lane < wide - 64, lane, lane - wide) + lax.axis_index(COL) * COLS
+    row = local_row + lax.axis_index(ROW) * ROWS
     across = here - before(here)
     vertical = here - higher
     h_left = jnp.where((column >= 1) & (column <= total_cols - 1), jnp.exp(-across * across), 0.0)
@@ -542,15 +548,15 @@
 def finish(messages, zed_ref, near_ref, next_ref, precond_ref, increment, residual):
     all_of = messages[...]
     total = jnp.sum(all_of, axis=0, keepdims=True)
-    zz = total[:, 64:65]
-    zn = total[:, 65:66]
+    zz = total[:, 64:65] + total[:, 66:67]
+    zn = total[:, 65:66] + total[:, 67:68]
     kappa = zn / zz
     delta = pltpu.roll(all_of, 32, 1) - kappa
     linear = pltpu.roll(all_of, 96, 1)
     quad = pltpu.roll(all_of, 64, 1)
     moved = jnp.sum(all_of + delta * (linear + delta * quad), axis=0, keepdims=True)
-    yy = moved[:, 0:1]
-    yny = moved[:, 1:2]
+    yy = moved[:, 0:1] + moved[:, 2:3]
+    yny = moved[:, 1:2] + moved[:, 3:4]
     step0 = zz / (zz - zn)
     beta = step0 * step0 * yy / zz
     step1 = yy / (yy - yny - step0 * yy * yy / zz)
@@ -584,7 +590,7 @@
 
 
 def shards(views):
-    rows, cols = lax.axis_size("row"), lax.axis_size("col")
+    rows, cols = lax.axis_size(ROW), lax.axis_size(COL)
     left_inner, right_inner, edge_matrix, center, scatter = (jnp.asarray(x) for x in tables())
     bf16 = jnp.bfloat16
     struct = jax.ShapeDtypeStruct
@@ -592,8 +598,8 @@
     edge = struct((PIECES * ANG, EDGE, COLS), bf16)
     room = pltpu.VMEM(edge.shape, bf16)
     pair, after = call(pack_rows, (edge, edge), (room, room), name="pack_rows")(views)
-    pair = swap(pair, "row", 0)
-    after = swap(after, "row", 1)
+    pair = swap(pair, ROW, 0)
+    after = swap(after, ROW, 1)
     shared = struct((SHARED, LANES), bf16)
     own, to_left, to_right, pack = call(
         pack_own,
@@ -607,8 +613,8 @@
         (room, room),
         name="pack_edges",
     )(pair, after, pack, own, to_left, to_right)
-    after = swap(after, "col", 1)
-    pair = swap(pair, "col", 0)
+    after = swap(after, COL, 1)
+    pair = swap(pair, COL, 0)
     slab = pltpu.VMEM((ANG, SLAB, LANES), F32)
     tile = pltpu.VMEM((OUT, LANES), F32)
     sums = struct((2, OUT, LANES), F32)
@@ -629,19 +635,22 @@
         ),
         name="outer_sums",
     )(views, above, below, own, after, pair, data, source, edge_matrix, center, scatter)
-    n = rows * cols
+    message = message + jnp.roll(swap(message, ROW, 0), 2, axis=1)
+    n = rows * cols // 2
     messages = lax.all_to_all(
-        jnp.broadcast_to(message[None], (n, 1, LANES)), ALL, 0, 0, tiled=True
+        jnp.broadcast_to(message[None], (n, 1, LANES)), ("chip", COL), 0, 0, tiled=True
     ).reshape(n, LANES)
     block = struct((ROWS, COLS), F32)
     return call(finish, (block, block), name="finish")(messages, zed, near, nxt, precond)
 
 
 def solution(mesh):
+    rows, cols = mesh.devices.shape
+    finer = Mesh(mesh.devices.reshape(rows // 2, 2, cols), (*ROW, COL))
     return jax.shard_map(
         shards,
-        mesh=mesh,
-        in_specs=(P(None, "row", "col"),),
-        out_specs=(P("row", "col"), P("row", "col")),
+        mesh=finer,
+        in_specs=(P(None, ROW, COL),),
+        out_specs=(P(ROW, COL), P(ROW, COL)),
         check_vma=False,
     )

time: 55.6 us -> 55.6 us (level)
  blocking collectives: 30.8 us -> 29.4 us
  waiting for transfers between devices: 5.99 us -> 7.09 us
    all_to_all x1, blocking collectives: 30.8 us -> 29.4 us  [shards(): lax.all_to_all(jnp.broadcast_to(message[None], (n, 1, LANES)), ('chip', C...]
    ppermute x4 -> x5, waiting for transfers between devices: 5.99 us -> 7.09 us  [swap(): return lax.ppermute(array, axis, pairs)]
    ppermute x4 -> x5, starting transfers between devices: 6.29 us -> 6.39 us  [swap(): return lax.ppermute(array, axis, pairs)]
  transfers between devices with their start and end apart: 4 -> 5, of which waited for: 1 -> 2; matrix products, arithmetic and copies ran while one was open for 0% -> 0% of each run, Pallas kernels for 12% -> 12%
where the time goes in v9:
time: 55.6 us; the launch traced here: 55.4 us
  blocking collectives  29.4 us (53%)
  Pallas kernels  9.79 us (18%)
  waiting for transfers between devices  7.09 us (13%)
  starting transfers between devices  6.39 us (11%)
  local copies, waits for them, and re-layouts  1.89 us (3%)
  between operations  0.79 us (1%)
    all_to_all x1, blocking collectives, shards(): lax.all_to_all(jnp.broadcast_to(message[None], (n, 1, LANES)), ('chip', C...  29.4 us
    ppermute x5, waiting for transfers between devices, swap(): return lax.ppermute(array, axis, pairs)  7.09 us
    ppermute x5, starting transfers between devices, swap(): return lax.ppermute(array, axis, pairs)  6.39 us
    pallas_call x1, Pallas kernels, shards(): call(both_sums, (sums, sums), (slab, slab, tile), name='inner_sums')  5.29 us
    unnamed x14, local copies, waits for them, and re-layouts  1.78 us
    pallas_call x1, Pallas kernels, shards(): call(functools.partial(outer_sums, rows * ROWS, cols * COLS), (field, fie...  1.54 us
    pallas_call x1, Pallas kernels, shards(): call(pack_own, (struct((ANG * ROWS, LANES), bf16), shared, shared, struct...  1.22 us
    pallas_call x1, Pallas kernels, shards(): call(finish, (block, block), name='finish')  1.21 us
  transfers between devices with their start and end apart: 5, of which 2 were waited for; matrix products, arithmetic and copies ran while one was open for 0% of the time, Pallas kernels for 12%

profile of v9, /device:TPU:1, one launch (start us, length us, event | category | flops | bytes accessed | tf_op | source)
XLA Modules:
  0.0 55.4 jit_solution(18420378939662401721)
XLA Ops:
  0.6 0.0 copy-start
  0.6 1.7 %copy-done = bf16[81,64,256]{2,1,0:T(8,128)(2,1)S(1)} copy-done((bf16[81,64,256]{2,1,0:T(8,128)(2,1)S(1)}, bf16[81,64,256]{2,1,0:T(8,128)(2,1)}, u32[]{:S(2)}) %copy-start) | copy-done | bytes 2654232
  2.4 0.0 copy-start.3
  2.4 0.1 pack_rows.1
  2.5 0.0 copy-start.1
  2.5 0.0 copy-start.2
  2.5 3.3 %collective-permute-start = (bf16[27,16,256]{2,1,0:T(8,128)(2,1)S(1)}, bf16[27,16,256]{2,1,0:T(8,128)(2,1)S(1)}, u32[]{:S(2)}, u32[]{:S(2)}) collective-permute-start(bf16[27,16,256]{2,1,0:T(8,128)(2,1)S(1)} %get-tuple-element.20), channel_id=1, source_target_pairs={{0,8},{8,0},{16,24},{24,16},{32,40},{40,32},{48,56},{56,48},{64,72... | collective-permute-start | bytes 663560 | tf_op jit(solution)/shard_map/ppermute | solution.py:589
  5.8 2.0 %collective-permute-start.1 = (bf16[27,16,256]{2,1,0:T(8,128)(2,1)S(1)}, bf16[27,16,256]{2,1,0:T(8,128)(2,1)S(1)}, u32[]{:S(2)}, u32[]{:S(2)}) collective-permute-start(bf16[27,16,256]{2,1,0:T(8,128)(2,1)S(1)} %get-tuple-element.21), channel_id=1, source_target_pairs={{8,16},{16,8},{24,32},{32,24},{40,48},{48,40},{56,64},{64,56},{72,... | collective-permute-start | bytes 663560 | tf_op jit(solution)/shard_map/ppermute | solution.py:589
  7.8 1.2 %pack_own.1 = (bf16[576,128]{1,0:T(8,128)(2,1)S(1)}, bf16[256,128]{1,0:T(8,128)(2,1)S(1)}, bf16[256,128]{1,0:T(8,128)(2,1)S(1)}, bf16[9,256,128]{2,1,0:T(8,128)(2,1)S(1)}) custom-call(bf16[81,64,256]{2,1,0:T(8,128)(2,1)S(1)} %copy-done), custom_call_target="tpu_custom_call" | custom-call | tf_op jit(solution)/shard_map/pack_own/pallas_call | solution.py:604
  9.1 0.0 collective-permute-done.got_pair
  9.1 6.0 %collective-permute-done.1.got_next = bf16[27,16,256]{2,1,0:T(8,128)(2,1)S(1)} collective-permute-done((bf16[27,16,256]{2,1,0:T(8,128)(2,1)S(1)}, bf16[27,16,256]{2,1,0:T(8,128)(2,1)S(1)}, u32[]{:S(2)}, u32[]{:S(2)}) %collective-permute-start.1) | collective-permute-done | bytes 221216 | tf_op jit(solution)/shard_map/ppermute | solution.py:589
  15.0 0.4 pack_edges.1
  15.5 0.0 copy-start.4
  15.5 0.0 copy-start.5
  15.5 0.0 copy-start.6
  15.5 0.8 %collective-permute-start.2 = (bf16[256,128]{1,0:T(8,128)(2,1)S(1)}, bf16[256,128]{1,0:T(8,128)(2,1)S(1)}, u32[]{:S(2)}, u32[]{:S(2)}) collective-permute-start(bf16[256,128]{1,0:T(8,128)(2,1)S(1)} %get-tuple-element.29), channel_id=1, source_target_pairs={{1,2},{2,1},{3,4},{4,3},{5,6},{6,5},{9,10},{10,9},{11,12},{12,11},... | collective-permute-start | bytes 196616 | tf_op jit(solution)/shard_map/ppermute | solution.py:589
  16.3 0.2 collective-permute-start.3
  16.5 0.0 copy-done.3
  16.5 0.0 copy-done.1
  16.5 0.0 copy-done.2
  16.5 5.3 %inner_sums.1 = (f32[2,72,128]{2,1,0:T(8,128)S(1)}, f32[2,72,128]{2,1,0:T(8,128)S(1)}) custom-call(bf16[81,64,256]{2,1,0:T(8,128)(2,1)S(1)} %copy-done.1, bf16[27,16,256]{2,1,0:T(8,128)(2,1)S(1)} %get-tuple-element.26.above, bf16[27,16,256]{2,1,0:T(8,128)(2,1)S(1)} %get-tuple-element.27.below, bf16[2,4,256,256]{3,2,1,0:T(8,128)(2,1)S(1)} %copy-done.3, ...), custom_call_target="tpu_custom_call" | custom-call | tf_op jit(solution)/shard_map/inner_sums/pallas_call | solution.py:621
  21.8 0.0 collective-permute-done.2.got_next
  21.8 0.0 collective-permute-done.3.got_pair
  21.8 0.0 copy-done.4
  21.9 0.0 copy-done.5
  21.9 0.0 copy-done.6
  21.9 1.5 %outer_sums.1 = (f32[72,256]{1,0:T(8,128)S(1)}, f32[72,256]{1,0:T(8,128)S(1)}, f32[72,256]{1,0:T(8,128)S(1)}, f32[72,256]{1,0:T(8,128)S(1)}, f32[1,128]{1,0:T(1,128)S(1)}) custom-call(bf16[81,64,256]{2,1,0:T(8,128)(2,1)S(1)} %copy-done.1, bf16[27,16,256]{2,1,0:T(8,128)(2,1)S(1)} %get-tuple-element.26.above, ...), custom_call_target="tpu_custom_call" | custom-call | tf_op jit(solution)/shard_map/outer_sums/pallas_call | solution.py:625
  23.4 0.1 collective-permute-start.4
  23.5 1.1 %collective-permute-done.4 = f32[1,128]{1,0:T(1,128)S(1)} collective-permute-done((f32[1,128]{1,0:T(1,128)S(1)}, f32[1,128]{1,0:T(1,128)S(1)}, u32[]{:S(2)}, u32[]{:S(2)}) %collective-permute-start.4) | collective-permute-done | bytes 544 | tf_op jit(solution)/shard_map/ppermute | solution.py:589
  24.6 0.1 slice.8
  24.7 0.1 fusion
  24.8 29.4 %all_to_all.5 = f32[128,1,128]{2,1,0:T(1,128)S(1)} all-to-all(f32[128,1,128]{2,1,0:T(1,128)S(1)} %broadcast_in_dim.9), channel_id=1, replica_groups=mesh['chip'=16,'core'=2,'col'=8] {'chip','col'}, dimensions={0} | all-to-all | bytes 131072 | tf_op jit(solution)/shard_map/all_to_all | solution.py:640
  54.2 1.2 %finish.1 = (f32[64,256]{1,0:T(8,128)}, f32[64,256]{1,0:T(8,128)}) custom-call(f32[128,128]{1,0:T(8,128)S(1)} %bitcast.4, f32[72,256]{1,0:T(8,128)S(1)} %get-tuple-element.34.zed_ref, f32[72,256]{1,0:T(8,128)S(1)} %get-tuple-element.35.near_ref, f32[72,256]{1,0:T(8,128)S(1)} %get-tuple-element.36.next_ref, f32[72,256]{1,0:T(8,128)S(1)} %get-tuple-element.37.precond_ref), custom_call_target="tpu_custom_call" | custom-call | tf_op jit(solution)/shard_map/finish/pallas_call | solution.py:644
  (1 shorter events, 0.0 us)
Async XLA Ops:
  0.6 1.8 %copy-start = (bf16[81,64,256]{2,1,0:T(8,128)(2,1)S(1)}, bf16[81,64,256]{2,1,0:T(8,128)(2,1)}, u32[]{:S(2)}) copy-start(bf16[81,64,256]{2,1,0:T(8,128)(2,1)} %views.7) | copy-start | bytes 7962628
  2.4 14.1 %copy-start.3 = (bf16[2,4,256,256]{3,2,1,0:T(8,128)(2,1)S(1)}, bf16[2,4,256,256]{3,2,1,0:T(8,128)(2,1)}, u32[]{:S(2)}) copy-start(bf16[2,4,256,256]{3,2,1,0:T(8,128)(2,1)} %constant.10.clone.left) | copy-start | bytes 3145732
  2.5 14.0 %copy-start.1 = (bf16[81,64,256]{2,1,0:T(8,128)(2,1)S(1)}, bf16[81,64,256]{2,1,0:T(8,128)(2,1)}, u32[]{:S(2)}) copy-start(bf16[81,64,256]{2,1,0:T(8,128)(2,1)} %views.7) | copy-start | bytes 7962628
  2.5 14.0 %copy-start.2 = (bf16[2,4,256,256]{3,2,1,0:T(8,128)(2,1)S(1)}, bf16[2,4,256,256]{3,2,1,0:T(8,128)(2,1)}, u32[]{:S(2)}) copy-start(bf16[2,4,256,256]{3,2,1,0:T(8,128)(2,1)} %constant.11.clone.right) | copy-start | bytes 3145732
  2.5 6.5 %collective-permute-start = (bf16[27,16,256]{2,1,0:T(8,128)(2,1)S(1)}, bf16[27,16,256]{2,1,0:T(8,128)(2,1)S(1)}, u32[]{:S(2)}, u32[]{:S(2)}) collective-permute-start(bf16[27,16,256]{2,1,0:T(8,128)(2,1)S(1)} %get-tuple-element.20), channel_id=1, source_target_pairs={{0,8},{8,0},{16,24},{24,16},{32,40},{40,32},{48,56},{56,48},{64,72... | collective-permute-start | bytes 663560 | tf_op jit(solution)/shard_map/ppermute | solution.py:589
  5.8 9.2 %collective-permute-start.1 = (bf16[27,16,256]{2,1,0:T(8,128)(2,1)S(1)}, bf16[27,16,256]{2,1,0:T(8,128)(2,1)S(1)}, u32[]{:S(2)}, u32[]{:S(2)}) collective-permute-start(bf16[27,16,256]{2,1,0:T(8,128)(2,1)S(1)} %get-tuple-element.21), channel_id=1, source_target_pairs={{8,16},{16,8},{24,32},{32,24},{40,48},{48,40},{56,64},{64,56},{72,... | collective-permute-start | bytes 663560 | tf_op jit(solution)/shard_map/ppermute | solution.py:589
  15.5 6.4 %copy-start.4 = (bf16[512,256]{1,0:T(8,128)(2,1)S(1)}, bf16[512,256]{1,0:T(8,128)(2,1)}, u32[]{:S(2)}) copy-start(bf16[512,256]{1,0:T(8,128)(2,1)} %constant.13.clone.edge_center) | copy-start | bytes 786436
  15.5 6.4 %copy-start.5 = (bf16[384,256]{1,0:T(8,128)(2,1)S(1)}, bf16[384,256]{1,0:T(8,128)(2,1)}, u32[]{:S(2)}) copy-start(bf16[384,256]{1,0:T(8,128)(2,1)} %constant.12.clone.edge) | copy-start | bytes 589828
  15.5 6.4 %copy-start.6 = (bf16[128,384]{1,0:T(8,128)(2,1)S(1)}, bf16[128,384]{1,0:T(8,128)(2,1)}, u32[]{:S(2)}) copy-start(bf16[128,384]{1,0:T(8,128)(2,1)} %constant.14.clone.scatter) | copy-start | bytes 294916
  15.5 6.3 %collective-permute-start.2 = (bf16[256,128]{1,0:T(8,128)(2,1)S(1)}, bf16[256,128]{1,0:T(8,128)(2,1)S(1)}, u32[]{:S(2)}, u32[]{:S(2)}) collective-permute-start(bf16[256,128]{1,0:T(8,128)(2,1)S(1)} %get-tuple-element.29), channel_id=1, source_target_pairs={{1,2},{2,1},{3,4},{4,3},{5,6},{6,5},{9,10},{10,9},{11,12},{12,11},... | collective-permute-start | bytes 196616 | tf_op jit(solution)/shard_map/ppermute | solution.py:589
  16.3 5.5 %collective-permute-start.3 = (bf16[256,128]{1,0:T(8,128)(2,1)S(1)}, bf16[256,128]{1,0:T(8,128)(2,1)S(1)}, u32[]{:S(2)}, u32[]{:S(2)}) collective-permute-start(bf16[256,128]{1,0:T(8,128)(2,1)S(1)} %get-tuple-element.30), channel_id=1, source_target_pairs={{0,1},{1,0},{2,3},{3,2},{4,5},{5,4},{6,7},{7,6},{8,9},{9,8},{10,11... | collective-permute-start | bytes 196616 | tf_op jit(solution)/shard_map/ppermute | solution.py:589
  23.4 1.2 %collective-permute-start.4 = (f32[1,128]{1,0:T(1,128)S(1)}, f32[1,128]{1,0:T(1,128)S(1)}, u32[]{:S(2)}, u32[]{:S(2)}) collective-permute-start(f32[1,128]{1,0:T(1,128)S(1)} %get-tuple-element.33), channel_id=1, source_target_pairs={{0,8},{8,0},{16,24},{24,16},{32,40},{40,32},{48,56},{56,48},{64,72... | collective-permute-start | bytes 1544 | tf_op jit(solution)/shard_map/ppermute | solution.py:589

commit v10 on v9

--- a/solution.py
+++ b/solution.py
@@ -108,7 +108,7 @@
     return lax.rem(lax.axis_index(axis), 2) == 0
 
 
-def pack_rows(views, send_pair, send_next, ups_out, downs_out):
+def pack_rows(tops, bottoms, send_pair, send_next, ups_out, downs_out):
     even = is_even(ROW)
     index = lax.broadcasted_iota(jnp.int32, (EDGE, COLS), 0)
 
@@ -117,11 +117,12 @@
 
     for ti in range(ANG):
 
-        def rows_of(s, start, ti=ti):
-            return views[(s + HALF) * ANG + ti, pl.ds(start, EDGE), :].astype(F32)
-
-        first = functools.partial(rows_of, start=0)
-        last = functools.partial(rows_of, start=ROWS - EDGE)
+        def first(s, ti=ti):
+            return tops[s * ANG + ti].astype(F32)
+
+        def last(s, ti=ti):
+            return bottoms[(s + HALF) * ANG + ti].astype(F32)
+
         put(True, 0, ti, first(4))
         put(True, 1, ti, jnp.where(index < 12, first(3), pltpu.roll(first(0), 12, 0)))
         put(True, 2, ti, jnp.where(index < 9, first(2), pltpu.roll(first(1), 9, 0)))
@@ -406,6 +407,7 @@
     next_out,
     precond_out,
     message,
+    turned,
     warped,
     side,
     center_ref,
@@ -543,6 +545,7 @@
     for where, number in numbers:
         out = jnp.where(place == where, number, out)
     message[...] = out
+    turned[...] = pltpu.roll(out, 2, 1)
 
 
 def finish(messages, zed_ref, near_ref, next_ref, precond_ref, increment, residual):
@@ -597,7 +600,9 @@
 
     edge = struct((PIECES * ANG, EDGE, COLS), bf16)
     room = pltpu.VMEM(edge.shape, bf16)
-    pair, after = call(pack_rows, (edge, edge), (room, room), name="pack_rows")(views)
+    pair, after = call(pack_rows, (edge, edge), (room, room), name="pack_rows")(
+        views[HALF * ANG :, :EDGE, :], views[: (HALF + 1) * ANG, ROWS - EDGE :, :]
+    )
     pair = swap(pair, ROW, 0)
     after = swap(after, ROW, 1)
     shared = struct((SHARED, LANES), bf16)
@@ -622,9 +627,9 @@
         views, above, below, left_inner, right_inner
     )
     field = struct((OUT, COLS), F32)
-    zed, near, nxt, precond, message = call(
+    zed, near, nxt, precond, message, turned = call(
         functools.partial(outer_sums, rows * ROWS, cols * COLS),
-        (field, field, field, field, struct((1, LANES), F32)),
+        (field, field, field, field, struct((1, LANES), F32), struct((1, LANES), F32)),
         (
             slab,
             slab,
@@ -635,7 +640,7 @@
         ),
         name="outer_sums",
     )(views, above, below, own, after, pair, data, source, edge_matrix, center, scatter)
-    message = message + jnp.roll(swap(message, ROW, 0), 2, axis=1)
+    message = message + swap(turned, ROW, 0)
     n = rows * cols // 2
     messages = lax.all_to_all(
         jnp.broadcast_to(message[None], (n, 1, LANES)), ("chip", COL), 0, 0, tiled=True

time: 55.6 us -> 54.9 us (0.987)
  waiting for transfers between devices: 7.09 us -> 5.63 us
  local copies, waits for them, and re-layouts: 1.89 us -> 3.13 us
    ppermute x5, waiting for transfers between devices: 7.09 us -> 5.63 us  [swap(): return lax.ppermute(array, axis, pairs)]
    slice x1, local copies, waits for them, and re-layouts: 0.07 us -> 1.31 us  [shards(): views[:(HALF + 1) * ANG, ROWS - EDGE:, :]]
where the time goes in v10:
time: 54.9 us; the launch traced here: 54.7 us
  blocking collectives  29.1 us (53%)
  Pallas kernels  9.86 us (18%)
  starting transfers between devices  6.16 us (11%)
  waiting for transfers between devices  5.63 us (10%)
  local copies, waits for them, and re-layouts  3.13 us (6%)
  between operations  0.82 us (1%)
    all_to_all x1, blocking collectives, shards(): lax.all_to_all(jnp.broadcast_to(message[None], (n, 1, LANES)), ('chip', C...  29.1 us
    ppermute x5, starting transfers between devices, swap(): return lax.ppermute(array, axis, pairs)  6.16 us
    ppermute x5, waiting for transfers between devices, swap(): return lax.ppermute(array, axis, pairs)  5.63 us
    pallas_call x1, Pallas kernels, shards(): call(both_sums, (sums, sums), (slab, slab, tile), name='inner_sums')  5.3 us
    unnamed x14, local copies, waits for them, and re-layouts  1.78 us
    pallas_call x1, Pallas kernels, shards(): call(functools.partial(outer_sums, rows * ROWS, cols * COLS), (field, fie...  1.6 us
    slice x1, local copies, waits for them, and re-layouts, shards(): views[:(HALF + 1) * ANG, ROWS - EDGE:, :]  1.31 us
    pallas_call x1, Pallas kernels, shards(): call(pack_own, (struct((ANG * ROWS, LANES), bf16), shared, shared, struct...  1.22 us
  transfers between devices with their start and end apart: 5, of which 2 were waited for; matrix products, arithmetic and copies ran while one was open for 0% of the time, Pallas kernels for 12%

profile of v10, /device:TPU:1, one launch (start us, length us, event | category | flops | bytes accessed | tf_op | source)
XLA Modules:
  0.0 54.7 jit_solution(11784793648979054812)
XLA Ops:
  0.6 0.0 copy-start.2
  0.6 0.0 copy-start.3
  0.7 1.3 %fusion = (bf16[45,16,256]{2,1,0:T(8,128)(2,1)S(1)}, bf16[45,16,256]{2,1,0:T(8,128)(2,1)S(1)}) fusion(bf16[81,64,256]{2,1,0:T(8,128)(2,1)} %views.5), kind=kLoop, calls=%fused_computation.1 | loop fusion | bytes 1474560 | tf_op jit(solution)/shard_map/slice | solution.py:604
  2.0 0.1 pack_rows.1
  2.1 3.3 %collective-permute-start = (bf16[27,16,256]{2,1,0:T(8,128)(2,1)S(1)}, bf16[27,16,256]{2,1,0:T(8,128)(2,1)S(1)}, u32[]{:S(2)}, u32[]{:S(2)}) collective-permute-start(bf16[27,16,256]{2,1,0:T(8,128)(2,1)S(1)} %get-tuple-element.21), channel_id=1, source_target_pairs={{0,8},{8,0},{16,24},{24,16},{32,40},{40,32},{48,56},{56,48},{64,72... | collective-permute-start | bytes 663560 | tf_op jit(solution)/shard_map/ppermute | solution.py:592
  5.4 1.9 %collective-permute-start.1 = (bf16[27,16,256]{2,1,0:T(8,128)(2,1)S(1)}, bf16[27,16,256]{2,1,0:T(8,128)(2,1)S(1)}, u32[]{:S(2)}, u32[]{:S(2)}) collective-permute-start(bf16[27,16,256]{2,1,0:T(8,128)(2,1)S(1)} %get-tuple-element.22), channel_id=1, source_target_pairs={{8,16},{16,8},{24,32},{32,24},{40,48},{48,40},{56,64},{64,56},{72,... | collective-permute-start | bytes 663560 | tf_op jit(solution)/shard_map/ppermute | solution.py:592
  7.3 0.0 copy-start
  7.3 1.7 %copy-done = bf16[81,64,256]{2,1,0:T(8,128)(2,1)S(1)} copy-done((bf16[81,64,256]{2,1,0:T(8,128)(2,1)S(1)}, bf16[81,64,256]{2,1,0:T(8,128)(2,1)}, u32[]{:S(2)}) %copy-start) | copy-done | bytes 2654232
  9.1 0.0 copy-start.1
  9.1 1.2 %pack_own.1 = (bf16[576,128]{1,0:T(8,128)(2,1)S(1)}, bf16[256,128]{1,0:T(8,128)(2,1)S(1)}, bf16[256,128]{1,0:T(8,128)(2,1)S(1)}, bf16[9,256,128]{2,1,0:T(8,128)(2,1)S(1)}) custom-call(bf16[81,64,256]{2,1,0:T(8,128)(2,1)S(1)} %copy-done), custom_call_target="tpu_custom_call" | custom-call | tf_op jit(solution)/shard_map/pack_own/pallas_call | solution.py:609
  10.3 0.0 collective-permute-done.got_pair
  10.3 4.5 %collective-permute-done.1.got_next = bf16[27,16,256]{2,1,0:T(8,128)(2,1)S(1)} collective-permute-done((bf16[27,16,256]{2,1,0:T(8,128)(2,1)S(1)}, bf16[27,16,256]{2,1,0:T(8,128)(2,1)S(1)}, u32[]{:S(2)}, u32[]{:S(2)}) %collective-permute-start.1) | collective-permute-done | bytes 221216 | tf_op jit(solution)/shard_map/ppermute | solution.py:592
  14.8 0.4 pack_edges.1
  15.3 0.0 copy-start.4
  15.3 0.0 copy-start.5
  15.3 0.0 copy-start.6
  15.3 0.8 %collective-permute-start.2 = (bf16[256,128]{1,0:T(8,128)(2,1)S(1)}, bf16[256,128]{1,0:T(8,128)(2,1)S(1)}, u32[]{:S(2)}, u32[]{:S(2)}) collective-permute-start(bf16[256,128]{1,0:T(8,128)(2,1)S(1)} %get-tuple-element.30), channel_id=1, source_target_pairs={{1,2},{2,1},{3,4},{4,3},{5,6},{6,5},{9,10},{10,9},{11,12},{12,11},... | collective-permute-start | bytes 196616 | tf_op jit(solution)/shard_map/ppermute | solution.py:592
  16.1 0.1 collective-permute-start.3
  16.2 0.0 copy-done.2
  16.2 0.0 copy-done.3
  16.2 0.0 copy-done.1
  16.2 5.3 %inner_sums.1 = (f32[2,72,128]{2,1,0:T(8,128)S(1)}, f32[2,72,128]{2,1,0:T(8,128)S(1)}) custom-call(bf16[81,64,256]{2,1,0:T(8,128)(2,1)S(1)} %copy-done.1, bf16[27,16,256]{2,1,0:T(8,128)(2,1)S(1)} %get-tuple-element.27.above, bf16[27,16,256]{2,1,0:T(8,128)(2,1)S(1)} %get-tuple-element.28.below, bf16[2,4,256,256]{3,2,1,0:T(8,128)(2,1)S(1)} %copy-done.3, ...), custom_call_target="tpu_custom_call" | custom-call | tf_op jit(solution)/shard_map/inner_sums/pallas_call | solution.py:626
  21.5 0.0 collective-permute-done.2.got_next
  21.6 0.0 collective-permute-done.3.got_pair
  21.6 0.0 copy-done.4
  21.6 0.0 copy-done.5
  21.6 0.0 copy-done.6
  21.6 1.6 %outer_sums.1 = (f32[72,256]{1,0:T(8,128)S(1)}, f32[72,256]{1,0:T(8,128)S(1)}, f32[72,256]{1,0:T(8,128)S(1)}, f32[72,256]{1,0:T(8,128)S(1)}, f32[1,128]{1,0:T(1,128)S(1)}, /*index=5*/f32[1,128]{1,0:T(1,128)S(1)}) custom-call(bf16[81,64,256]{2,1,0:T(8,128)(2,1)S(1)} %copy-done.1, bf16[27,16,256]{2,1,0:T(8,128)(2,1)S(1)} %get-tuple-element.27.above, ...), custom_call_target="tpu_custom_call" | custom-call | tf_op jit(solution)/shard_map/outer_sums/pallas_call | solution.py:630
  23.2 0.0 collective-permute-start.4
  23.2 1.1 %collective-permute-done.4 = f32[1,128]{1,0:T(1,128)S(1)} collective-permute-done((f32[1,128]{1,0:T(1,128)S(1)}, f32[1,128]{1,0:T(1,128)S(1)}, u32[]{:S(2)}, u32[]{:S(2)}) %collective-permute-start.4) | collective-permute-done | bytes 544 | tf_op jit(solution)/shard_map/ppermute | solution.py:592
  24.4 29.1 %all_to_all.5 = f32[128,1,128]{2,1,0:T(1,128)S(1)} all-to-all(f32[128,1,128]{2,1,0:T(1,128)S(1)} %broadcast_in_dim.9), channel_id=1, replica_groups=mesh['chip'=16,'core'=2,'col'=8] {'chip','col'}, dimensions={0} | all-to-all | bytes 131072 | tf_op jit(solution)/shard_map/all_to_all | solution.py:645
  53.5 1.2 %finish.1 = (f32[64,256]{1,0:T(8,128)}, f32[64,256]{1,0:T(8,128)}) custom-call(f32[128,128]{1,0:T(8,128)S(1)} %bitcast.3, f32[72,256]{1,0:T(8,128)S(1)} %get-tuple-element.36.zed_ref, f32[72,256]{1,0:T(8,128)S(1)} %get-tuple-element.37.near_ref, f32[72,256]{1,0:T(8,128)S(1)} %get-tuple-element.38.next_ref, f32[72,256]{1,0:T(8,128)S(1)} %get-tuple-element.39.precond_ref), custom_call_target="tpu_custom_call" | custom-call | tf_op jit(solution)/shard_map/finish/pallas_call | solution.py:649
  (2 shorter events, 0.0 us)
Async XLA Ops:
  0.6 15.6 %copy-start.2 = (bf16[2,4,256,256]{3,2,1,0:T(8,128)(2,1)S(1)}, bf16[2,4,256,256]{3,2,1,0:T(8,128)(2,1)}, u32[]{:S(2)}) copy-start(bf16[2,4,256,256]{3,2,1,0:T(8,128)(2,1)} %constant.11.clone.right) | copy-start | bytes 3145732
  0.6 15.6 %copy-start.3 = (bf16[2,4,256,256]{3,2,1,0:T(8,128)(2,1)S(1)}, bf16[2,4,256,256]{3,2,1,0:T(8,128)(2,1)}, u32[]{:S(2)}) copy-start(bf16[2,4,256,256]{3,2,1,0:T(8,128)(2,1)} %constant.10.clone.left) | copy-start | bytes 3145732
  2.1 8.2 %collective-permute-start = (bf16[27,16,256]{2,1,0:T(8,128)(2,1)S(1)}, bf16[27,16,256]{2,1,0:T(8,128)(2,1)S(1)}, u32[]{:S(2)}, u32[]{:S(2)}) collective-permute-start(bf16[27,16,256]{2,1,0:T(8,128)(2,1)S(1)} %get-tuple-element.21), channel_id=1, source_target_pairs={{0,8},{8,0},{16,24},{24,16},{32,40},{40,32},{48,56},{56,48},{64,72... | collective-permute-start | bytes 663560 | tf_op jit(solution)/shard_map/ppermute | solution.py:592
  5.4 9.4 %collective-permute-start.1 = (bf16[27,16,256]{2,1,0:T(8,128)(2,1)S(1)}, bf16[27,16,256]{2,1,0:T(8,128)(2,1)S(1)}, u32[]{:S(2)}, u32[]{:S(2)}) collective-permute-start(bf16[27,16,256]{2,1,0:T(8,128)(2,1)S(1)} %get-tuple-element.22), channel_id=1, source_target_pairs={{8,16},{16,8},{24,32},{32,24},{40,48},{48,40},{56,64},{64,56},{72,... | collective-permute-start | bytes 663560 | tf_op jit(solution)/shard_map/ppermute | solution.py:592
  7.3 1.8 %copy-start = (bf16[81,64,256]{2,1,0:T(8,128)(2,1)S(1)}, bf16[81,64,256]{2,1,0:T(8,128)(2,1)}, u32[]{:S(2)}) copy-start(bf16[81,64,256]{2,1,0:T(8,128)(2,1)} %views.5) | copy-start | bytes 7962628
  9.1 7.2 %copy-start.1 = (bf16[81,64,256]{2,1,0:T(8,128)(2,1)S(1)}, bf16[81,64,256]{2,1,0:T(8,128)(2,1)}, u32[]{:S(2)}) copy-start(bf16[81,64,256]{2,1,0:T(8,128)(2,1)} %views.5) | copy-start | bytes 7962628
  15.3 6.3 %copy-start.4 = (bf16[512,256]{1,0:T(8,128)(2,1)S(1)}, bf16[512,256]{1,0:T(8,128)(2,1)}, u32[]{:S(2)}) copy-start(bf16[512,256]{1,0:T(8,128)(2,1)} %constant.13.clone.edge_center) | copy-start | bytes 786436
  15.3 6.3 %copy-start.5 = (bf16[384,256]{1,0:T(8,128)(2,1)S(1)}, bf16[384,256]{1,0:T(8,128)(2,1)}, u32[]{:S(2)}) copy-start(bf16[384,256]{1,0:T(8,128)(2,1)} %constant.12.clone.edge) | copy-start | bytes 589828
  15.3 6.3 %copy-start.6 = (bf16[128,384]{1,0:T(8,128)(2,1)S(1)}, bf16[128,384]{1,0:T(8,128)(2,1)}, u32[]{:S(2)}) copy-start(bf16[128,384]{1,0:T(8,128)(2,1)} %constant.14.clone.scatter) | copy-start | bytes 294916
  15.3 6.2 %collective-permute-start.2 = (bf16[256,128]{1,0:T(8,128)(2,1)S(1)}, bf16[256,128]{1,0:T(8,128)(2,1)S(1)}, u32[]{:S(2)}, u32[]{:S(2)}) collective-permute-start(bf16[256,128]{1,0:T(8,128)(2,1)S(1)} %get-tuple-element.30), channel_id=1, source_target_pairs={{1,2},{2,1},{3,4},{4,3},{5,6},{6,5},{9,10},{10,9},{11,12},{12,11},... | collective-permute-start | bytes 196616 | tf_op jit(solution)/shard_map/ppermute | solution.py:592
  16.1 5.4 %collective-permute-start.3 = (bf16[256,128]{1,0:T(8,128)(2,1)S(1)}, bf16[256,128]{1,0:T(8,128)(2,1)S(1)}, u32[]{:S(2)}, u32[]{:S(2)}) collective-permute-start(bf16[256,128]{1,0:T(8,128)(2,1)S(1)} %get-tuple-element.31), channel_id=1, source_target_pairs={{0,1},{1,0},{2,3},{3,2},{4,5},{5,4},{6,7},{7,6},{8,9},{9,8},{10,11... | collective-permute-start | bytes 196616 | tf_op jit(solution)/shard_map/ppermute | solution.py:592
  23.2 1.1 %collective-permute-start.4 = (f32[1,128]{1,0:T(1,128)S(1)}, f32[1,128]{1,0:T(1,128)S(1)}, u32[]{:S(2)}, u32[]{:S(2)}) collective-permute-start(f32[1,128]{1,0:T(1,128)S(1)} %get-tuple-element.35), channel_id=1, source_target_pairs={{0,8},{8,0},{16,24},{24,16},{32,40},{40,32},{48,56},{56,48},{64,72... | collective-permute-start | bytes 1544 | tf_op jit(solution)/shard_map/ppermute | solution.py:592

commit v11 on v10

--- a/solution.py
+++ b/solution.py
@@ -210,7 +210,7 @@
 
 
 def pack_edges(
-    got_pair, got_next, pack, own_in, left_in, right_in,
+    got_next, got_pair, pack, own_in, left_in, right_in,
     above, below, own, send_pair, send_next, to_left, to_right,
 ):
     even = is_even(ROW)
@@ -379,7 +379,7 @@
         return carry
 
     for sign in (0, 1):
-        lax.fori_loop(0, HALF, functools.partial(body, sign=sign), 0)
+        lax.fori_loop(0, HALF, functools.partial(body, sign=sign), 0, unroll=True)
 
 
 def both_sums(views, above, below, left, right, data_out, source_out, *scratch):
@@ -617,7 +617,7 @@
         (edge, edge, struct((PACKED, LANES), bf16), shared, shared),
         (room, room),
         name="pack_edges",
-    )(pair, after, pack, own, to_left, to_right)
+    )(after, pair, pack, own, to_left, to_right)
     after = swap(after, COL, 1)
     pair = swap(pair, COL, 0)
     slab = pltpu.VMEM((ANG, SLAB, LANES), F32)

time: 54.9 us -> 54.2 us (0.987)
  waiting for transfers between devices: 5.63 us -> 1.35 us
  starting transfers between devices: 6.16 us -> 10.2 us
  Pallas kernels: 9.86 us -> 8.21 us
  blocking collectives: 29.1 us -> 30.3 us
    ppermute x5, waiting for transfers between devices: 5.63 us -> 1.35 us  [swap(): return lax.ppermute(array, axis, pairs)]
    ppermute x5, starting transfers between devices: 6.16 us -> 10.2 us  [swap(): return lax.ppermute(array, axis, pairs)]
    pallas_call x1, Pallas kernels: 5.3 us -> 3.64 us  [shards(): call(both_sums, (sums, sums), (slab, slab, tile), name='inner_sums')]
    all_to_all x1, blocking collectives: 29.1 us -> 30.3 us  [shards(): lax.all_to_all(jnp.broadcast_to(message[None], (n, 1, LANES)), ('chip', C...]
  transfers between devices with their start and end apart: 5 -> 5, of which waited for: 2 -> 2; matrix products, arithmetic and copies ran while one was open for 0% -> 0% of each run, Pallas kernels for 12% -> 9%
where the time goes in v11:
time: 54.2 us; the launch traced here: 53.9 us
  blocking collectives  30.3 us (56%)
  starting transfers between devices  10.2 us (19%)
  Pallas kernels  8.21 us (15%)
  local copies, waits for them, and re-layouts  3.13 us (6%)
  waiting for transfers between devices  1.35 us (2%)
  between operations  0.78 us (1%)
    all_to_all x1, blocking collectives, shards(): lax.all_to_all(jnp.broadcast_to(message[None], (n, 1, LANES)), ('chip', C...  30.3 us
    ppermute x5, starting transfers between devices, swap(): return lax.ppermute(array, axis, pairs)  10.2 us
    pallas_call x1, Pallas kernels, shards(): call(both_sums, (sums, sums), (slab, slab, tile), name='inner_sums')  3.64 us
    unnamed x14, local copies, waits for them, and re-layouts  1.78 us
    pallas_call x1, Pallas kernels, shards(): call(functools.partial(outer_sums, rows * ROWS, cols * COLS), (field, fie...  1.6 us
    ppermute x5, waiting for transfers between devices, swap(): return lax.ppermute(array, axis, pairs)  1.35 us
    slice x1, local copies, waits for them, and re-layouts, shards(): views[:(HALF + 1) * ANG, ROWS - EDGE:, :]  1.31 us
    pallas_call x1, Pallas kernels, shards(): call(pack_own, (struct((ANG * ROWS, LANES), bf16), shared, shared, struct...  1.22 us
  transfers between devices with their start and end apart: 5, of which 2 were waited for; matrix products, arithmetic and copies ran while one was open for 0% of the time, Pallas kernels for 9%

profile of v11, /device:TPU:1, one launch (start us, length us, event | category | flops | bytes accessed | tf_op | source)
XLA Modules:
  0.0 53.9 jit_solution(14501159476473137843)
XLA Ops:
  0.6 0.0 copy-start.2
  0.6 0.0 copy-start.3
  0.7 1.3 %fusion = (bf16[45,16,256]{2,1,0:T(8,128)(2,1)S(1)}, bf16[45,16,256]{2,1,0:T(8,128)(2,1)S(1)}) fusion(bf16[81,64,256]{2,1,0:T(8,128)(2,1)} %views.5), kind=kLoop, calls=%fused_computation.1 | loop fusion | bytes 1474560 | tf_op jit(solution)/shard_map/slice | solution.py:604
  2.0 0.1 pack_rows.1
  2.1 4.9 %collective-permute-start = (bf16[27,16,256]{2,1,0:T(8,128)(2,1)S(1)}, bf16[27,16,256]{2,1,0:T(8,128)(2,1)S(1)}, u32[]{:S(2)}, u32[]{:S(2)}) collective-permute-start(bf16[27,16,256]{2,1,0:T(8,128)(2,1)S(1)} %get-tuple-element.21), channel_id=1, source_target_pairs={{8,16},{16,8},{24,32},{32,24},{40,48},{48,40},{56,64},{64,56},{72,... | collective-permute-start | bytes 663560 | tf_op jit(solution)/shard_map/ppermute | solution.py:592
  7.0 0.1 collective-permute-start.1
  7.1 0.0 copy-start
  7.1 1.7 %copy-done = bf16[81,64,256]{2,1,0:T(8,128)(2,1)S(1)} copy-done((bf16[81,64,256]{2,1,0:T(8,128)(2,1)S(1)}, bf16[81,64,256]{2,1,0:T(8,128)(2,1)}, u32[]{:S(2)}) %copy-start) | copy-done | bytes 2654232
  8.9 0.0 copy-start.1
  8.9 1.2 %pack_own.1 = (bf16[576,128]{1,0:T(8,128)(2,1)S(1)}, bf16[256,128]{1,0:T(8,128)(2,1)S(1)}, bf16[256,128]{1,0:T(8,128)(2,1)S(1)}, bf16[9,256,128]{2,1,0:T(8,128)(2,1)S(1)}) custom-call(bf16[81,64,256]{2,1,0:T(8,128)(2,1)S(1)} %copy-done), custom_call_target="tpu_custom_call" | custom-call | tf_op jit(solution)/shard_map/pack_own/pallas_call | solution.py:609
  10.1 0.5 collective-permute-done.got_next
  10.6 0.0 collective-permute-done.1.got_pair
  10.6 0.4 pack_edges.1
  11.1 0.0 copy-start.4
  11.1 0.0 copy-start.5
  11.1 0.0 copy-start.6
  11.1 0.8 %collective-permute-start.2 = (bf16[256,128]{1,0:T(8,128)(2,1)S(1)}, bf16[256,128]{1,0:T(8,128)(2,1)S(1)}, u32[]{:S(2)}, u32[]{:S(2)}) collective-permute-start(bf16[256,128]{1,0:T(8,128)(2,1)S(1)} %get-tuple-element.30), channel_id=1, source_target_pairs={{1,2},{2,1},{3,4},{4,3},{5,6},{6,5},{9,10},{10,9},{11,12},{12,11},... | collective-permute-start | bytes 196616 | tf_op jit(solution)/shard_map/ppermute | solution.py:592
  11.9 3.7 %collective-permute-start.3 = (bf16[256,128]{1,0:T(8,128)(2,1)S(1)}, bf16[256,128]{1,0:T(8,128)(2,1)S(1)}, u32[]{:S(2)}, u32[]{:S(2)}) collective-permute-start(bf16[256,128]{1,0:T(8,128)(2,1)S(1)} %get-tuple-element.31), channel_id=1, source_target_pairs={{0,1},{1,0},{2,3},{3,2},{4,5},{5,4},{6,7},{7,6},{8,9},{9,8},{10,11... | collective-permute-start | bytes 196616 | tf_op jit(solution)/shard_map/ppermute | solution.py:592
  15.7 0.0 copy-done.2
  15.7 0.0 copy-done.3
  15.7 0.0 copy-done.1
  15.7 3.6 %inner_sums.1 = (f32[2,72,128]{2,1,0:T(8,128)S(1)}, f32[2,72,128]{2,1,0:T(8,128)S(1)}) custom-call(bf16[81,64,256]{2,1,0:T(8,128)(2,1)S(1)} %copy-done.1, bf16[27,16,256]{2,1,0:T(8,128)(2,1)S(1)} %get-tuple-element.27.above, bf16[27,16,256]{2,1,0:T(8,128)(2,1)S(1)} %get-tuple-element.28.below, bf16[2,4,256,256]{3,2,1,0:T(8,128)(2,1)S(1)} %copy-done.3, ...), custom_call_target="tpu_custom_call" | custom-call | tf_op jit(solution)/shard_map/inner_sums/pallas_call | solution.py:626
  19.3 0.0 collective-permute-done.2.got_next
  19.3 0.0 collective-permute-done.3.got_pair
  19.3 0.0 copy-done.4
  19.4 0.0 copy-done.5
  19.4 0.0 copy-done.6
  19.4 1.6 %outer_sums.1 = (f32[72,256]{1,0:T(8,128)S(1)}, f32[72,256]{1,0:T(8,128)S(1)}, f32[72,256]{1,0:T(8,128)S(1)}, f32[72,256]{1,0:T(8,128)S(1)}, f32[1,128]{1,0:T(1,128)S(1)}, /*index=5*/f32[1,128]{1,0:T(1,128)S(1)}) custom-call(bf16[81,64,256]{2,1,0:T(8,128)(2,1)S(1)} %copy-done.1, bf16[27,16,256]{2,1,0:T(8,128)(2,1)S(1)} %get-tuple-element.27.above, ...), custom_call_target="tpu_custom_call" | custom-call | tf_op jit(solution)/shard_map/outer_sums/pallas_call | solution.py:630
  21.0 0.6 %collective-permute-start.4 = (f32[1,128]{1,0:T(1,128)S(1)}, f32[1,128]{1,0:T(1,128)S(1)}, u32[]{:S(2)}, u32[]{:S(2)}) collective-permute-start(f32[1,128]{1,0:T(1,128)S(1)} %get-tuple-element.35), channel_id=1, source_target_pairs={{0,8},{8,0},{16,24},{24,16},{32,40},{40,32},{48,56},{56,48},{64,72... | collective-permute-start | bytes 1544 | tf_op jit(solution)/shard_map/ppermute | solution.py:592
  21.6 0.8 %collective-permute-done.4 = f32[1,128]{1,0:T(1,128)S(1)} collective-permute-done((f32[1,128]{1,0:T(1,128)S(1)}, f32[1,128]{1,0:T(1,128)S(1)}, u32[]{:S(2)}, u32[]{:S(2)}) %collective-permute-start.4) | collective-permute-done | bytes 544 | tf_op jit(solution)/shard_map/ppermute | solution.py:592
  22.4 30.3 %all_to_all.5 = f32[128,1,128]{2,1,0:T(1,128)S(1)} all-to-all(f32[128,1,128]{2,1,0:T(1,128)S(1)} %broadcast_in_dim.9), channel_id=1, replica_groups=mesh['chip'=16,'core'=2,'col'=8] {'chip','col'}, dimensions={0} | all-to-all | bytes 131072 | tf_op jit(solution)/shard_map/all_to_all | solution.py:645
  52.7 1.2 %finish.1 = (f32[64,256]{1,0:T(8,128)}, f32[64,256]{1,0:T(8,128)}) custom-call(f32[128,128]{1,0:T(8,128)S(1)} %bitcast.3, f32[72,256]{1,0:T(8,128)S(1)} %get-tuple-element.36.zed_ref, f32[72,256]{1,0:T(8,128)S(1)} %get-tuple-element.37.near_ref, f32[72,256]{1,0:T(8,128)S(1)} %get-tuple-element.38.next_ref, f32[72,256]{1,0:T(8,128)S(1)} %get-tuple-element.39.precond_ref), custom_call_target="tpu_custom_call" | custom-call | tf_op jit(solution)/shard_map/finish/pallas_call | solution.py:649
  (2 shorter events, 0.0 us)
Async XLA Ops:
  0.6 15.0 %copy-start.2 = (bf16[2,4,256,256]{3,2,1,0:T(8,128)(2,1)S(1)}, bf16[2,4,256,256]{3,2,1,0:T(8,128)(2,1)}, u32[]{:S(2)}) copy-start(bf16[2,4,256,256]{3,2,1,0:T(8,128)(2,1)} %constant.11.clone.right) | copy-start | bytes 3145732
  0.6 15.0 %copy-start.3 = (bf16[2,4,256,256]{3,2,1,0:T(8,128)(2,1)S(1)}, bf16[2,4,256,256]{3,2,1,0:T(8,128)(2,1)}, u32[]{:S(2)}) copy-start(bf16[2,4,256,256]{3,2,1,0:T(8,128)(2,1)} %constant.10.clone.left) | copy-start | bytes 3145732
  2.1 8.6 %collective-permute-start = (bf16[27,16,256]{2,1,0:T(8,128)(2,1)S(1)}, bf16[27,16,256]{2,1,0:T(8,128)(2,1)S(1)}, u32[]{:S(2)}, u32[]{:S(2)}) collective-permute-start(bf16[27,16,256]{2,1,0:T(8,128)(2,1)S(1)} %get-tuple-element.21), channel_id=1, source_target_pairs={{8,16},{16,8},{24,32},{32,24},{40,48},{48,40},{56,64},{64,56},{72,... | collective-permute-start | bytes 663560 | tf_op jit(solution)/shard_map/ppermute | solution.py:592
  7.0 3.6 %collective-permute-start.1 = (bf16[27,16,256]{2,1,0:T(8,128)(2,1)S(1)}, bf16[27,16,256]{2,1,0:T(8,128)(2,1)S(1)}, u32[]{:S(2)}, u32[]{:S(2)}) collective-permute-start(bf16[27,16,256]{2,1,0:T(8,128)(2,1)S(1)} %get-tuple-element.22), channel_id=1, source_target_pairs={{0,8},{8,0},{16,24},{24,16},{32,40},{40,32},{48,56},{56,48},{64,72... | collective-permute-start | bytes 663560 | tf_op jit(solution)/shard_map/ppermute | solution.py:592
  7.1 1.8 %copy-start = (bf16[81,64,256]{2,1,0:T(8,128)(2,1)S(1)}, bf16[81,64,256]{2,1,0:T(8,128)(2,1)}, u32[]{:S(2)}) copy-start(bf16[81,64,256]{2,1,0:T(8,128)(2,1)} %views.5) | copy-start | bytes 7962628
  8.9 6.8 %copy-start.1 = (bf16[81,64,256]{2,1,0:T(8,128)(2,1)S(1)}, bf16[81,64,256]{2,1,0:T(8,128)(2,1)}, u32[]{:S(2)}) copy-start(bf16[81,64,256]{2,1,0:T(8,128)(2,1)} %views.5) | copy-start | bytes 7962628
  11.1 8.3 %copy-start.4 = (bf16[512,256]{1,0:T(8,128)(2,1)S(1)}, bf16[512,256]{1,0:T(8,128)(2,1)}, u32[]{:S(2)}) copy-start(bf16[512,256]{1,0:T(8,128)(2,1)} %constant.13.clone.edge_center) | copy-start | bytes 786436
  11.1 8.3 %copy-start.5 = (bf16[384,256]{1,0:T(8,128)(2,1)S(1)}, bf16[384,256]{1,0:T(8,128)(2,1)}, u32[]{:S(2)}) copy-start(bf16[384,256]{1,0:T(8,128)(2,1)} %constant.12.clone.edge) | copy-start | bytes 589828
  11.1 8.3 %copy-start.6 = (bf16[128,384]{1,0:T(8,128)(2,1)S(1)}, bf16[128,384]{1,0:T(8,128)(2,1)}, u32[]{:S(2)}) copy-start(bf16[128,384]{1,0:T(8,128)(2,1)} %constant.14.clone.scatter) | copy-start | bytes 294916
  11.1 8.2 %collective-permute-start.2 = (bf16[256,128]{1,0:T(8,128)(2,1)S(1)}, bf16[256,128]{1,0:T(8,128)(2,1)S(1)}, u32[]{:S(2)}, u32[]{:S(2)}) collective-permute-start(bf16[256,128]{1,0:T(8,128)(2,1)S(1)} %get-tuple-element.30), channel_id=1, source_target_pairs={{1,2},{2,1},{3,4},{4,3},{5,6},{6,5},{9,10},{10,9},{11,12},{12,11},... | collective-permute-start | bytes 196616 | tf_op jit(solution)/shard_map/ppermute | solution.py:592
  11.9 7.4 %collective-permute-start.3 = (bf16[256,128]{1,0:T(8,128)(2,1)S(1)}, bf16[256,128]{1,0:T(8,128)(2,1)S(1)}, u32[]{:S(2)}, u32[]{:S(2)}) collective-permute-start(bf16[256,128]{1,0:T(8,128)(2,1)S(1)} %get-tuple-element.31), channel_id=1, source_target_pairs={{0,1},{1,0},{2,3},{3,2},{4,5},{5,4},{6,7},{7,6},{8,9},{9,8},{10,11... | collective-permute-start | bytes 196616 | tf_op jit(solution)/shard_map/ppermute | solution.py:592
  21.0 1.4 %collective-permute-start.4 = (f32[1,128]{1,0:T(1,128)S(1)}, f32[1,128]{1,0:T(1,128)S(1)}, u32[]{:S(2)}, u32[]{:S(2)}) collective-permute-start(f32[1,128]{1,0:T(1,128)S(1)} %get-tuple-element.35), channel_id=1, source_target_pairs={{0,8},{8,0},{16,24},{24,16},{32,40},{40,32},{48,56},{56,48},{64,72... | collective-permute-start | bytes 1544 | tf_op jit(solution)/shard_map/ppermute | solution.py:592
